TPU v7x, 128 devices: a whole 4x4x4 slice. The times are simulated.
128 devices in a mesh: lat: 32 (over y, x, core), chan: 4 (over z).
Axes of the slice: x: 4, y: 4, z: 4, core: 2. Of those that a mesh axis runs over, the one named last changes fastest.
Arguments:
- grid_field: bfloat16 [512, 1440, 512], P('lat', None, 'chan'), may hold values from -6 to 6
- mode_lists: int32 [32, 16], replicated, may hold values from 0 to 511, as said below
- lat_basis: bfloat16 [512, 512, 512], P('lat'), may hold values from -0.25 to 0.25
- degree_gain: bfloat16 [512, 512], P(None, 'chan'), may hold values from 0.25 to 4
- channel_mixer: bfloat16 [2, 512, 512], P(None, 'chan'), may hold values from -0.1875 to 0.1875
Outputs:
- grid_out: bfloat16 [512, 1440, 512], P('lat', None, 'chan')
Inputs may be any that keep to these rules, and one draw needn't show every extreme that they name: Every wavenumber of 0 to 511 stands exactly once in mode_lists; entries 2k and 2k + 1 of a row sum to 511.
All inputs are finite; a program needn't handle non-finite values.
Results may differ from a plain program's by a relative error of at most 0.01.
Values may be sent and summed in bfloat16 or wider, within the bound.
No kernel may reach another device: no remote copies, remote signals or barrier semaphores. Data moves between devices by JAX's collectives and lax.ppermute only.
A program may use at most 128 MiB of HBM per device.

v0:
```python
import math

import jax
import jax.numpy as jnp
from jax import lax
from jax.sharding import PartitionSpec as P


def longitude_table(wavenumbers, lon_count):
    longitudes = jnp.arange(lon_count, dtype=jnp.int32)
    phases = longitudes[:, None] * wavenumbers[None, :] % lon_count
    angles = phases.astype(jnp.float32) * (2.0 * math.pi / lon_count)
    factor = 1.0 / math.sqrt(lon_count)
    return jnp.stack([jnp.cos(angles) * factor, -jnp.sin(angles) * factor], axis=1).astype(
        jnp.bfloat16
    )


def complex_block(channel_mixer):
    real_part = channel_mixer[0]
    imag_part = channel_mixer[1]
    upper_rows = jnp.concatenate([real_part, imag_part], axis=1)
    bottom = jnp.concatenate([-imag_part, real_part], axis=1)
    return jnp.concatenate([upper_rows, bottom], axis=0)


def triangular(basis_rows, my_modes):
    degrees = jnp.arange(basis_rows.shape[1], dtype=jnp.int32)
    keep = degrees[None, :, None] >= my_modes[:, None, None]
    return jnp.where(keep, basis_rows, jnp.zeros((), jnp.bfloat16))


def apply_mix(pieces, block_mix):
    dims = pieces.shape
    flat_rows = pieces.reshape(-1, dims[2] * dims[3])
    product = jnp.dot(flat_rows, block_mix, preferred_element_type=jnp.float32).astype(jnp.bfloat16)
    return product.reshape(dims)


def local(grid_field, mode_lists, lat_basis, degree_gain, channel_mixer):
    lon_count = grid_field.shape[1]
    all_modes = mode_lists.reshape(-1)
    forward_table = longitude_table(all_modes, lon_count)
    spectrum = jnp.einsum(
        "anc,nps->apsc", grid_field, forward_table, preferred_element_type=jnp.float32
    ).astype(jnp.bfloat16)
    row_modes = lax.dynamic_index_in_dim(mode_lists, lax.axis_index("lat"), 0, keepdims=False)
    my_basis = triangular(lat_basis, row_modes)
    by_modes = lax.all_to_all(spectrum, "lat", split_axis=2, concat_axis=0, tiled=True)
    coefficients = jnp.einsum(
        "mla,apmc->mlpc", my_basis, by_modes, preferred_element_type=jnp.float32
    )
    hidden = (coefficients * degree_gain.astype(jnp.float32)[None, :, None, :]).astype(jnp.bfloat16)
    full_mixer = lax.all_gather(channel_mixer, "chan", axis=1, tiled=True)
    block_mix = complex_block(full_mixer)
    mixed_part = apply_mix(
        lax.all_to_all(hidden, "chan", split_axis=1, concat_axis=3, tiled=True), block_mix
    )
    mixed_out = lax.all_to_all(mixed_part, "chan", split_axis=3, concat_axis=1, tiled=True)
    returned = jnp.einsum(
        "mla,mlpc->apmc", my_basis, mixed_out, preferred_element_type=jnp.float32
    ).astype(jnp.bfloat16)
    spectrum_back = lax.all_to_all(returned, "lat", split_axis=0, concat_axis=2, tiled=True)
    return jnp.einsum(
        "apsc,nps->anc", spectrum_back, forward_table, preferred_element_type=jnp.float32
    ).astype(jnp.bfloat16)


def solution(mesh):
    return jax.shard_map(
        local,
        mesh=mesh,
        in_specs=(
            P("lat", None, "chan"),
            P(),
            P("lat", None, None),
            P(None, "chan"),
            P(None, "chan", None),
        ),
        out_specs=P("lat", None, "chan"),
        check_vma=False,
    )
```

profile of v0, /device:TPU:1, one launch (start us, length us, event | category | flops | bytes accessed | tf_op | source)
XLA Modules:
  0.0 368.6 jit_solution(2828818922057742470)
XLA Ops:
  6.5 0.8 copy.25
  7.4 12.8 %multiply_convert_fusion.2 = (bf16[1440,1,512]{2,0,1:T(8,128)(2,1)S(1)}, bf16[1440,1,512]{2,0,1:T(8,128)(2,1)S(1)}) fusion(s32[512]{0:T(512)S(1)} %mul.72), kind=kLoop, calls=%fused_computation.26 | loop fusion | flops 10321920 | bytes 2951168 | tf_op jit(solution)/shard_map/convert
  20.2 1.1 copy-done
  21.3 8.9 %convert_bitcast_fusion.1 = bf16[16,2,512,128]{3,2,0,1:T(8,128)(2,1)S(1)} fusion(bf16[16,1440,128]{2,1,0:T(8,128)(2,1)} %param.5, bf16[1440,1,512]{2,0,1:T(8,128)(2,1)S(1)} %get-tuple-element.8, bf16[1440,1,512]{2,0,1:T(8,128)(2,1)S(1)} %get-tuple-element.7), kind=kOutput, calls=%fused_computation.16 | convolution fusion | flops 6047793152 | bytes 13041664 | tf_op jit(solution)/shard_map/anc,nps->apsc/dot_general | solution.py:44
  30.2 4.7 %copy.26 = bf16[16,2,512,128]{3,0,1,2:T(8,128)(2,1)} copy(bf16[16,2,512,128]{3,2,0,1:T(8,128)(2,1)S(1)} %convert_bitcast_fusion.1) | data formatting | bytes 8388608 | tf_op jit(solution)/shard_map/convert_element_type | solution.py:46
  34.9 8.8 %all-to-all-start = ((bf16[16,2,512,128]{3,0,1,2:T(8,128)(2,1)}), bf16[16,2,512,128]{3,0,1,2:T(8,128)(2,1)}, u32[]{:S(2)}, u32[]{:S(2)}) async-start(bf16[16,2,512,128]{3,0,1,2:T(8,128)(2,1)} %copy.26), calls=%async_computation | async-start | bytes 8388608 | tf_op jit(solution)/shard_map/all_to_all | solution.py:49
  43.8 0.2 dynamic-slice_reduce_fusion
  44.0 49.8 %all-to-all-done = bf16[16,2,512,128]{3,0,1,2:T(8,128)(2,1)} async-done(((bf16[16,2,512,128]{3,0,1,2:T(8,128)(2,1)}), bf16[16,2,512,128]{3,0,1,2:T(8,128)(2,1)}, u32[]{:S(2)}, u32[]{:S(2)}) %all-to-all-start) | async-done | bytes 4194336 | tf_op jit(solution)/shard_map/all_to_all | solution.py:49
  93.9 3.4 copy.27
  97.2 4.9 %multiply_convert_fusion = bf16[16,512,2,128]{3,1,2,0:T(8,128)(2,1)S(1)} fusion(f32[512,128]{1,0:T(8,128)S(1)} %convert_element_type.45, bf16[512,2,16,128]{3,0,1,2:T(8,128)(2,1)S(1)} %bitcast.75, bf16[16,512,512]{2,1,0:T(8,128)(2,1)} %param.7, pred[16,512]{1,0:T(8,128)(4,1)S(1)} %iota_compare_fusion), kind=kOutput, calls=%fused_computation.5 | convolution fusion | flops 2155872256 | bytes 17047552 | tf_op jit(solution)/shard_map/mla,apmc->mlpc/dot_general | solution.py:50
  102.1 6.3 %copy.28 = bf16[16,512,2,128]{3,2,0,1:T(2,128)(2,1)} copy(bf16[16,512,2,128]{3,1,2,0:T(8,128)(2,1)S(1)} %multiply_convert_fusion) | data formatting | bytes 8388608 | tf_op jit(solution)/shard_map/convert_element_type | solution.py:53
  108.5 5.0 %all-to-all-start.1 = ((bf16[16,512,2,128]{3,2,0,1:T(2,128)(2,1)}), bf16[16,512,2,128]{3,2,0,1:T(2,128)(2,1)}, u32[]{:S(2)}, u32[]{:S(2)}) async-start(bf16[16,512,2,128]{3,2,0,1:T(2,128)(2,1)} %copy.28), calls=%async_computation.1 | async-start | bytes 8388608 | tf_op jit(solution)/shard_map/all_to_all | solution.py:57
  113.5 0.1 all-gather.2.cloned.1.call-start
  113.6 0.6 all-gather.2.cloned.1.call-update
  114.2 33.8 %all-gather.2.cloned.1.call-done = bf16[2,512,512]{2,1,0:T(8,128)(2,1)} async-done(((bf16[2,128,512]{2,1,0:T(8,128)(2,1)}), bf16[2,512,512]{2,1,0:T(8,128)(2,1)}) %all-gather.2.cloned.1.call-update) | async-done | bytes 1048592 | tf_op jit(solution)/shard_map/all_gather | solution.py:54
  148.0 1.1 fusion.42
  149.1 1.3 slice_bitcast_fusion
  150.3 17.5 %all-to-all-done.1 = bf16[16,512,2,128]{3,2,0,1:T(2,128)(2,1)} async-done(((bf16[16,512,2,128]{3,2,0,1:T(2,128)(2,1)}), bf16[16,512,2,128]{3,2,0,1:T(2,128)(2,1)}, u32[]{:S(2)}, u32[]{:S(2)}) %all-to-all-start.1) | async-done | bytes 4194336 | tf_op jit(solution)/shard_map/all_to_all | solution.py:57
  167.9 8.3 %copy.29 = bf16[16,4,128,2,128]{2,0,4,1,3:T(8,128)(2,1)} copy(bf16[16,4,128,2,128]{4,3,0,2,1:T(2,128)(2,1)} %bitcast.9) | data formatting | bytes 8388608 | tf_op jit(solution)/shard_map/all_to_all | solution.py:57
  176.2 15.1 %fusion.12 = bf16[2048,1024]{1,0:T(8,128)(2,1)} fusion(bf16[128,8,16,128]{3,2,1,0:T(8,128)(2,1)} %bitcast.73, bf16[512,512]{1,0:T(8,128)(2,1)S(1)} %get-tuple-element.6, bf16[512,512]{1,0:T(8,128)(2,1)S(1)} %fusion.42, bf16[512,512]{1,0:T(8,128)(2,1)S(1)} %get-tuple-element.5), kind=kOutput, calls=%fused_computation.19 | convolution fusion | flops 4305453056 | bytes 9961472 | tf_op jit(solution)/shard_map/dot_general | solution.py:36
  191.3 7.8 %reshape.146 = bf16[16,128,2,512]{3,2,1,0:T(2,128)(2,1)} reshape(bf16[2048,1024]{1,0:T(8,128)(2,1)} %fusion.12) | data formatting | bytes 8388608 | tf_op jit(solution)/shard_map/reshape | solution.py:37
  199.1 8.3 %copy.30 = bf16[16,128,2,512]{1,0,2,3:T(8,128)(2,1)} copy(bf16[16,128,2,512]{3,2,1,0:T(2,128)(2,1)} %reshape.146) | data formatting | bytes 8388608 | tf_op jit(solution)/shard_map/reshape | solution.py:37
  207.4 48.1 %all_to_all.69 = bf16[16,128,2,512]{1,0,2,3:T(8,128)(2,1)S(1)} all-to-all(bf16[16,128,2,512]{1,0,2,3:T(8,128)(2,1)} %copy.30), channel_id=1, replica_groups=mesh['lat'=32,'chan'=4] {'chan'}, dimensions={3} | all-to-all | bytes 8388608 | tf_op jit(solution)/shard_map/all_to_all | solution.py:59
  255.5 5.2 %copy.46 = bf16[16,128,2,4,128]{1,3,4,2,0:T(4,128)(2,1)} copy(bf16[16,128,2,4,128]{1,0,2,4,3:T(8,128)(2,1)S(1)} %bitcast.70) | data formatting | bytes 8388608 | tf_op jit(solution)/shard_map/all_to_all | solution.py:59
  260.8 7.2 %all_to_all.60 = bf16[16,512,2,128]{1,3,2,0:T(8,128)(2,1)} reshape(bf16[16,4,128,2,128]{2,1,4,3,0:T(4,128)(2,1)} %bitcast.71) | data formatting | bytes 8388608 | tf_op jit(solution)/shard_map/all_to_all | solution.py:59
  268.0 7.3 %convert_bitcast_fusion = bf16[512,2,16,128]{0,3,1,2:T(8,128)(2,1)} fusion(bf16[16,512,2,128]{1,3,2,0:T(8,128)(2,1)} %all_to_all.60, bf16[16,512,512]{2,1,0:T(8,128)(2,1)} %param.7, pred[16,512]{1,0:T(8,128)(4,1)S(1)} %iota_compare_fusion), kind=kOutput, calls=%fused_computation.15 | convolution fusion | flops 2153775104 | bytes 16785408 | tf_op jit(solution)/shard_map/mla,mlpc->apmc/dot_general | solution.py:60
  275.3 11.2 %copy.32 = bf16[512,2,16,128]{3,1,2,0:T(2,128)(2,1)} copy(bf16[512,2,16,128]{0,3,1,2:T(8,128)(2,1)} %convert_bitcast_fusion) | data formatting | bytes 8388608 | tf_op jit(solution)/shard_map/convert_element_type | solution.py:62
  286.5 65.3 %all_to_all.70 = bf16[512,2,16,128]{3,1,2,0:T(2,128)(2,1)S(1)} all-to-all(bf16[512,2,16,128]{3,1,2,0:T(2,128)(2,1)} %copy.32), channel_id=1, replica_groups=mesh['lat'=32,'chan'=4] {'lat'}, dimensions={0} | all-to-all | bytes 8388608 | tf_op jit(solution)/shard_map/all_to_all | solution.py:63
  351.8 0.5 copy.33
  352.3 1.2 copy.34
  353.5 0.2 copy-done.1
  353.7 8.0 %fusion.6 = bf16[16,1440,128]{2,1,0:T(8,128)(2,1)} fusion(bf16[16,2,512,128]{3,2,1,0:T(8,128)(2,1)S(1)} %bitcast.74, bf16[1440,1,512]{2,0,1:T(8,128)(2,1)S(1)} %copy-done.1, bf16[1440,1,512]{2,0,1:T(8,128)(2,1)S(1)} %get-tuple-element.7), kind=kOutput, calls=%fused_computation.10 | convolution fusion | flops 6048645120 | bytes 13041664 | tf_op jit(solution)/shard_map/apsc,nps->anc/dot_general | solution.py:64
  (9 shorter events, 0.2 us)
Async XLA Ops:
  20.2 1.2 copy-start
  34.9 8.8 %copy-start.2 = (bf16[512,128]{1,0:T(8,128)(2,1)S(1)}, bf16[512,128]{1,0:T(8,128)(2,1)}, u32[]{:S(2)}) copy-start(bf16[512,128]{1,0:T(8,128)(2,1)} %param.8) | copy-start | bytes 393220
  34.9 8.8 %copy-start.3 = (s32[32,16]{0,1:T(8,128)S(1)}, s32[32,16]{0,1:T(8,128)}, u32[]{:S(2)}) copy-start(s32[32,16]{0,1:T(8,128)} %param.6) | copy-start | bytes 6148
  34.9 59.0 %all-to-all-start = ((bf16[16,2,512,128]{3,0,1,2:T(8,128)(2,1)}), bf16[16,2,512,128]{3,0,1,2:T(8,128)(2,1)}, u32[]{:S(2)}, u32[]{:S(2)}) async-start(bf16[16,2,512,128]{3,0,1,2:T(8,128)(2,1)} %copy.26), calls=%async_computation | async-start | bytes 8388608 | tf_op jit(solution)/shard_map/all_to_all | solution.py:49
  108.5 59.4 %all-to-all-start.1 = ((bf16[16,512,2,128]{3,2,0,1:T(2,128)(2,1)}), bf16[16,512,2,128]{3,2,0,1:T(2,128)(2,1)}, u32[]{:S(2)}, u32[]{:S(2)}) async-start(bf16[16,512,2,128]{3,2,0,1:T(2,128)(2,1)} %copy.28), calls=%async_computation.1 | async-start | bytes 8388608 | tf_op jit(solution)/shard_map/all_to_all | solution.py:57
  113.5 34.5 %all-gather.2.cloned.1.call-start = ((), (), s32[]{:S(2)}) async-start(), calls=%async_computation.4 | async-start | bytes 1310720 | tf_op jit(solution)/shard_map/all_gather | solution.py:54
  352.3 1.4 copy-start.1
Sparse Core Ops, SparseCore 0:
  116.0 31.9 all-gather.1
where the time goes:
time: 370 us; the launch traced here: 369 us
  blocking collectives  113 us (31%)
  waiting for transfers between devices  102 us (28%)
  local copies, waits for them, and re-layouts  67.8 us (18%)
  matrix products  44.2 us (12%)
  other arithmetic  13.9 us (4%)
  starting transfers between devices  13.9 us (4%)
  between operations  13.5 us (4%)
    all_to_all x1, blocking collectives, local(): lax.all_to_all(returned, 'lat', split_axis=0, concat_axis=2, tiled=True)  65.3 us
    all_to_all x1, waiting for transfers between devices, local(): lax.all_to_all(spectrum, 'lat', split_axis=2, concat_axis=0, tiled=True)  49.8 us
    all_to_all x1, blocking collectives, local(): lax.all_to_all(mixed_part, 'chan', split_axis=3, concat_axis=1, tiled=True)  48.1 us
    all_gather x1, waiting for transfers between devices, local(): full_mixer = lax.all_gather(channel_mixer, 'chan', axis=1, tiled=True)  33.8 us
    all_to_all x1, waiting for transfers between devices, local(): lax.all_to_all(hidden, 'chan', split_axis=1, concat_axis=3, tiled=True)  17.5 us
    reshape x2, local copies, waits for them, and re-layouts, apply_mix(): return product.reshape(dims)  16.1 us
    dot_general x1, matrix products, apply_mix(): jnp.dot(flat_rows, block_mix, preferred_element_type=jnp.float32)  15.1 us
    another operation x1, other arithmetic  12.8 us
  transfers between devices with their start and end apart: 3, of which 3 were waited for; matrix products, arithmetic and copies ran while one was open for 1% of the time, Pallas kernels for 0%

commit v1 on v0

v1 whole, which is shorter than its diff:
```python
import functools
import math

import jax
import jax.numpy as jnp
import ml_dtypes
import numpy as np
from jax import lax
from jax.experimental import pallas as pl
from jax.experimental.pallas import tpu as pltpu
from jax.sharding import PartitionSpec as P

BF16 = jnp.bfloat16
F32 = jnp.float32


def folded_tables(lon_count, wave_count):
    half = lon_count // 2
    waves = np.arange(wave_count).reshape(-1, 2).T
    phases = (waves[:, :, None] * np.arange(half)[None, None, :]) % lon_count
    angles = phases * (2.0 * math.pi / lon_count)
    factor = 1.0 / math.sqrt(lon_count)
    table = np.stack([np.cos(angles) * factor, -np.sin(angles) * factor], axis=2)
    table = table.reshape(2, wave_count, half).astype(np.float32).astype(ml_dtypes.bfloat16)
    return table, np.ascontiguousarray(table.transpose(0, 2, 1))


def fourier_kernel(modes, field, table, out, wide):
    step = pl.program_id(0)
    lats = field.shape[0]
    half = field.shape[1] // 2
    waves = table.shape[1]
    width = field.shape[2]
    band = out.shape[-2]
    low = jnp.concatenate([field[a, :half, :] for a in range(lats)], axis=1)
    high = jnp.concatenate([field[a, half:, :] for a in range(lats)], axis=1)
    for parity in range(2):
        folded = low + high if parity == 0 else low - high
        result = jnp.dot(table[parity], folded, preferred_element_type=F32)
        for a in range(lats):
            rows = pl.ds(parity * waves * band + step * lats + a, waves, stride=band)
            wide[rows, :] = result[:, a * width : (a + 1) * width]

    @pl.when(step == pl.num_programs(0) - 1)
    def _():
        def place(device, carry):
            for q in range(out.shape[1]):
                mode = modes[device * out.shape[1] + q]
                first = (mode % 2) * waves + (mode // 2) * 2
                for p in range(2):
                    start = pl.multiple_of((first + p) * band, band)
                    out[device, q, p] = wide[pl.ds(start, band), :].astype(BF16)
            return carry

        lax.fori_loop(0, out.shape[0], place, 0, unroll=4)


def fourier(modes, field, table, devices, slots):
    band, lon_count, width = field.shape
    waves = table.shape[1]
    lats = 2
    return pl.pallas_call(
        fourier_kernel,
        grid_spec=pltpu.PrefetchScalarGridSpec(
            num_scalar_prefetch=1,
            grid=(band // lats,),
            in_specs=[
                pl.BlockSpec((lats, lon_count, width), lambda i, m: (i, 0, 0)),
                pl.BlockSpec((2, waves, lon_count // 2), lambda i, m: (0, 0, 0)),
            ],
            out_specs=pl.BlockSpec(memory_space=pltpu.VMEM),
            scratch_shapes=[pltpu.VMEM((2 * waves * band, width), F32)],
        ),
        out_shape=jax.ShapeDtypeStruct((devices, slots, 2, band, width), BF16),
        compiler_params=pltpu.CompilerParams(vmem_limit_bytes=30 * 2**20),
        name="fourier",
    )(modes, field, table)


def inverse_kernel(modes, pieces, table, out, wide):
    step = pl.program_id(0)
    lats = out.shape[0]
    half = out.shape[1] // 2
    waves = table.shape[2]
    width = out.shape[2]
    band = pieces.shape[-2]

    @pl.when(step == 0)
    def _():
        def place(device, carry):
            for q in range(pieces.shape[1]):
                mode = modes[device * pieces.shape[1] + q]
                first = (mode % 2) * waves + (mode // 2) * 2
                for p in range(2):
                    start = pl.multiple_of((first + p) * band, band)
                    wide[pl.ds(start, band), :] = pieces[device, q, p].astype(F32)
            return carry

        lax.fori_loop(0, pieces.shape[0], place, 0, unroll=4)

    sums = []
    for parity in range(2):
        columns = []
        for a in range(lats):
            rows = pl.ds(parity * waves * band + step * lats + a, waves, stride=band)
            columns.append(wide[rows, :].astype(BF16))
        sums.append(
            jnp.dot(table[parity], jnp.concatenate(columns, axis=1), preferred_element_type=F32)
        )
    low = (sums[0] + sums[1]).astype(BF16)
    high = (sums[0] - sums[1]).astype(BF16)
    for a in range(lats):
        out[a, :half, :] = low[:, a * width : (a + 1) * width]
        out[a, half:, :] = high[:, a * width : (a + 1) * width]


def inverse(modes, pieces, table):
    devices, slots, _, band, width = pieces.shape
    _, half, waves = table.shape
    lats = 2
    return pl.pallas_call(
        inverse_kernel,
        grid_spec=pltpu.PrefetchScalarGridSpec(
            num_scalar_prefetch=1,
            grid=(band // lats,),
            in_specs=[
                pl.BlockSpec(memory_space=pltpu.VMEM),
                pl.BlockSpec((2, half, waves), lambda i, m: (0, 0, 0)),
            ],
            out_specs=pl.BlockSpec((lats, 2 * half, width), lambda i, m: (i, 0, 0)),
            scratch_shapes=[pltpu.VMEM((2 * waves * band, width), F32)],
        ),
        out_shape=jax.ShapeDtypeStruct((band, 2 * half, width), BF16),
        compiler_params=pltpu.CompilerParams(vmem_limit_bytes=30 * 2**20),
        name="inverse_fourier",
    )(modes, pieces, table)


def spectral_kernel(chosen, pieces, basis_low, basis_high, gain, mix, out, column, hidden, mixed):
    pair = pl.program_id(0)
    lat_parts, chan_parts, _, _, band, width = pieces.shape
    lat_count = lat_parts * band
    channels = chan_parts * width
    for which, basis in enumerate((basis_low, basis_high)):
        slot = chosen[pair, which]
        wave = chosen[pair, 2 + which]
        count = basis.shape[1]
        first = gain.shape[1] - count
        for p in range(2):
            for j in range(chan_parts):
                start = p * channels + j * width
                column[:, start : start + width] = pieces[:, j, slot, p].reshape(lat_count, width)
        degrees = first + lax.broadcasted_iota(jnp.int32, (count, lat_count), 0)
        kept = jnp.where(degrees >= wave, basis[0], jnp.zeros((), BF16))
        rows = 256
        for begin in range(0, count, rows):
            part = jnp.dot(kept[begin : begin + rows], column[...], preferred_element_type=F32)
            for p in range(2):
                for j in range(chan_parts):
                    start = p * channels + j * width
                    factor = gain[j, first + begin : first + begin + rows, :].astype(F32)
                    hidden[begin : begin + rows, start : start + width] = (
                        part[:, start : start + width] * factor
                    ).astype(BF16)
        for begin in range(0, count, rows):
            mixed[begin : begin + rows, :] = jnp.dot(
                hidden[begin : begin + rows, :], mix[...], preferred_element_type=F32
            ).astype(BF16)
        for p in range(2):
            for j in range(chan_parts):
                start = p * channels + j * width
                if j % 2:
                    continue
                back = lax.dot_general(
                    kept,
                    mixed[:count, start : start + 2 * width],
                    (((0,), (0,)), ((), ())),
                    preferred_element_type=F32,
                ).astype(BF16)
                for k in range(2):
                    out[:, j + k, slot, p] = back[:, k * width : (k + 1) * width].reshape(
                        lat_parts, band, width
                    )


def spectral(chosen, pieces, basis, gain, mix):
    lat_parts, chan_parts, slots, _, band, width = pieces.shape
    degrees, lat_count = basis.shape[1:]
    channels2 = mix.shape[0]
    return pl.pallas_call(
        spectral_kernel,
        grid_spec=pltpu.PrefetchScalarGridSpec(
            num_scalar_prefetch=1,
            grid=(slots // 2,),
            in_specs=[
                pl.BlockSpec(memory_space=pltpu.VMEM),
                pl.BlockSpec((1, degrees, lat_count), lambda i, c: (c[i, 4], 0, 0)),
                pl.BlockSpec((1, degrees // 2, lat_count), lambda i, c: (c[i, 5], 1, 0)),
                pl.BlockSpec(gain.shape, lambda i, c: (0, 0, 0)),
                pl.BlockSpec(mix.shape, lambda i, c: (0, 0)),
            ],
            out_specs=pl.BlockSpec(memory_space=pltpu.VMEM),
            scratch_shapes=[
                pltpu.VMEM((lat_count, channels2), BF16),
                pltpu.VMEM((degrees, channels2), BF16),
                pltpu.VMEM((degrees, channels2), BF16),
            ],
        ),
        out_shape=jax.ShapeDtypeStruct(pieces.shape, BF16),
        compiler_params=pltpu.CompilerParams(vmem_limit_bytes=36 * 2**20),
        name="spectral",
    )(chosen, pieces, basis, basis, gain, mix)


def pair_choice(mode_lists, lat_index, chan_index, slots):
    row = lax.dynamic_index_in_dim(mode_lists, lat_index, 0, keepdims=False)
    mine = lax.dynamic_slice_in_dim(row, chan_index * slots, slots).reshape(slots // 2, 2)
    swapped = (mine[:, 0] > mine[:, 1]).astype(jnp.int32)
    low_slot = 2 * jnp.arange(slots // 2, dtype=jnp.int32) + swapped
    high_slot = 2 * jnp.arange(slots // 2, dtype=jnp.int32) + 1 - swapped
    return jnp.stack(
        [
            low_slot,
            high_slot,
            jnp.minimum(mine[:, 0], mine[:, 1]),
            jnp.maximum(mine[:, 0], mine[:, 1]),
            low_slot + chan_index * slots,
            high_slot + chan_index * slots,
        ],
        axis=1,
    )


def local(lat_parts, chan_parts, grid_field, mode_lists, lat_basis, degree_gain, channel_mixer):
    devices = lat_parts * chan_parts
    slots = lat_basis.shape[0] // chan_parts
    width = grid_field.shape[2]
    channels = width * chan_parts
    forward_table, back_table = folded_tables(grid_field.shape[1], mode_lists.size)
    modes = mode_lists.reshape(-1)

    all_gain = lax.all_gather(degree_gain, "chan", axis=0)
    all_mixer = lax.all_gather(channel_mixer, "chan", axis=1, tiled=True)
    real, imag = all_mixer[0], all_mixer[1]
    mix = jnp.concatenate(
        [jnp.concatenate([real, imag], axis=1), jnp.concatenate([-imag, real], axis=1)], axis=0
    )
    chosen = pair_choice(mode_lists, lax.axis_index("lat"), lax.axis_index("chan"), slots)

    sent = fourier(modes, grid_field, jnp.asarray(forward_table), devices, slots)
    got = lax.all_to_all(sent, ("lat", "chan"), 0, 0, tiled=True)
    got = got.reshape((lat_parts, chan_parts) + got.shape[1:])
    back = spectral(chosen, got, lat_basis, all_gain, mix)
    back = back.reshape((devices,) + back.shape[2:])
    returned = lax.all_to_all(back, ("lat", "chan"), 0, 0, tiled=True)
    return inverse(modes, returned, jnp.asarray(back_table))


def solution(mesh):
    return jax.shard_map(
        functools.partial(local, mesh.shape["lat"], mesh.shape["chan"]),
        mesh=mesh,
        in_specs=(
            P("lat", None, "chan"),
            P(),
            P("lat", None, None),
            P(None, "chan"),
            P(None, "chan", None),
        ),
        out_specs=P("lat", None, "chan"),
        check_vma=False,
    )
```

time: 370 us -> 190 us (0.51)
  waiting for transfers between devices: 102 us -> 4.36 us
  local copies, waits for them, and re-layouts: 67.8 us -> 9.29 us
  matrix products: 44.2 us -> 0 us
  Pallas kernels: 0 us -> 32.9 us
  other arithmetic: 13.9 us -> 1.4 us
  blocking collectives: 113 us -> 117 us
    all_to_all x2 -> x1, waiting for transfers between devices: 67.4 us -> 0.01 us  [local(): got = lax.all_to_all(sent, ('lat', 'chan'), 0, 0, tiled=True)]
    all_gather x0 -> x1, blocking collectives: none -> 56.5 us  [local(): all_gain = lax.all_gather(degree_gain, 'chan', axis=0)]
    all_to_all x2 -> x1, blocking collectives: 113 us -> 60.2 us  [local(): returned = lax.all_to_all(back, ('lat', 'chan'), 0, 0, tiled=True)]
    dot_general x5 -> x0, matrix products: 44.2 us -> none  [the longest x1 15.1 us: apply_mix(): jnp.dot(flat_rows, block_mix, preferred_element_type=jnp.float32)]
    pallas_call x0 -> x3, Pallas kernels: none -> 32.9 us  [the longest x1 11.3 us: inverse(): pl.pallas_call(inverse_kernel, grid_spec=pltpu.PrefetchScalarGridSpec(num...]
    all_gather x1, waiting for transfers between devices: 33.8 us -> 3.68 us  [local(): all_mixer = lax.all_gather(channel_mixer, 'chan', axis=1, tiled=True)]
    all_to_all x6 -> x0, local copies, waits for them, and re-layouts: 25.8 us -> none  [the longest x2 12.5 us: local(): lax.all_to_all(mixed_part, 'chan', split_axis=3, concat_axis=1, tiled=True)]
    convert_element_type x3 -> x0, local copies, waits for them, and re-layouts: 22.2 us -> none  [the longest x1 11.2 us: local(): returned = jnp.einsum('mla,mlpc->apmc', my_basis, mixed_out, preferred_el...]
  transfers between devices with their start and end apart: 3 -> 2, of which waited for: 3 -> 1; matrix products, arithmetic and copies ran while one was open for 1% -> 2% of each run, Pallas kernels for 0% -> 0%
where the time goes in v1:
time: 190 us
  blocking collectives  117 us (62%)
  Pallas kernels  32.9 us (17%)
  between operations  13.5 us (7%)
  starting transfers between devices  12 us (6%)
  local copies, waits for them, and re-layouts  9.29 us (5%)
  waiting for transfers between devices  4.36 us (2%)
    all_to_all x1, blocking collectives, local(): returned = lax.all_to_all(back, ('lat', 'chan'), 0, 0, tiled=True)  60.2 us
    all_gather x1, blocking collectives, local(): all_gain = lax.all_gather(degree_gain, 'chan', axis=0)  56.5 us
    all_to_all x1, starting transfers between devices, local(): got = lax.all_to_all(sent, ('lat', 'chan'), 0, 0, tiled=True)  12 us
    pallas_call x1, Pallas kernels, inverse(): pl.pallas_call(inverse_kernel, grid_spec=pltpu.PrefetchScalarGridSpec(num...  11.3 us
    pallas_call x1, Pallas kernels, fourier(): pl.pallas_call(fourier_kernel, grid_spec=pltpu.PrefetchScalarGridSpec(num...  10.9 us
    pallas_call x1, Pallas kernels, spectral(): pl.pallas_call(spectral_kernel, grid_spec=pltpu.PrefetchScalarGridSpec(nu...  10.6 us
    unnamed x11, local copies, waits for them, and re-layouts  6.87 us
  transfers between devices with their start and end apart: 2, of which 1 were waited for; matrix products, arithmetic and copies ran while one was open for 2% of the time, Pallas kernels for 0%

profile of v1, /device:TPU:1, one launch (start us, length us, event | category | flops | bytes accessed | tf_op | source)
XLA Modules:
  0.0 190.1 jit_solution(10627503925814052398)
XLA Ops:
  6.5 0.8 copy.8
  7.3 0.1 reshape.27.modes
  7.4 0.0 copy-start.1
  7.4 2.7 %copy-done.1 = bf16[16,1440,128]{2,1,0:T(8,128)(2,1)S(1)} copy-done((bf16[16,1440,128]{2,1,0:T(8,128)(2,1)S(1)}, bf16[16,1440,128]{2,1,0:T(8,128)(2,1)}, u32[]{:S(2)}) %copy-start.1) | copy-done | bytes 5898264
  10.1 0.0 copy-start.2
  10.1 1.4 copy-done.2
  11.5 10.9 %fourier.1 = bf16[128,4,2,16,128]{4,3,2,1,0:T(8,128)(2,1)S(1)} custom-call(s32[512]{0:T(512)S(1)} %reshape.27.modes, bf16[16,1440,128]{2,1,0:T(8,128)(2,1)S(1)} %copy-done.1, bf16[2,512,720]{2,1,0:T(8,128)(2,1)S(1)} %copy-done.2), custom_call_target="tpu_custom_call" | custom-call | tf_op jit(solution)/shard_map/fourier/pallas_call | solution.py:62
  22.4 0.0 copy-start
  22.4 2.0 %copy-done = bf16[128,4,2,16,128]{4,3,2,1,0:T(8,128)(2,1)} copy-done((bf16[128,4,2,16,128]{4,3,2,1,0:T(8,128)(2,1)}, bf16[128,4,2,16,128]{4,3,2,1,0:T(8,128)(2,1)S(1)}, u32[]{:S(2)}) %copy-start) | copy-done | bytes 4194328
  24.4 0.0 copy-start.4
  24.4 12.0 %all-to-all-start = ((bf16[128,4,2,16,128]{4,3,2,1,0:T(8,128)(2,1)}), bf16[128,4,2,16,128]{4,3,2,1,0:T(8,128)(2,1)}, u32[]{:S(2)}, u32[]{:S(2)}) async-start(bf16[128,4,2,16,128]{4,3,2,1,0:T(8,128)(2,1)} %copy-done), calls=%async_computation | async-start | bytes 8388608 | tf_op jit(solution)/shard_map/all_to_all | solution.py:251
  36.4 0.0 all-gather.3.cloned.1.call-start
  36.4 0.7 all-gather.3.cloned.1.call-update
  37.1 0.9 dynamic-slice_reduce_fusion
  38.0 0.1 reshape.28
  38.1 0.1 broadcast_add_fusion
  38.2 0.1 stack.2.chosen
  38.3 0.0 copy-done.4
  38.3 56.5 %all-gather = bf16[2048,128]{1,0:T(8,128)(2,1)S(1)} all-gather(bf16[512,128]{1,0:T(8,128)(2,1)S(1)} %copy-done.4), channel_id=2, replica_groups=mesh['lat'=32,'chan'=4] {'chan'}, dimensions={0}, use_global_device_ids=true | all-gather | bytes 655360 | tf_op jit(solution)/shard_map/all_gather | solution.py:242
  94.8 3.7 %all-gather.3.cloned.1.call-done = bf16[2,512,512]{2,1,0:T(8,128)(2,1)} async-done(((bf16[2,128,512]{2,1,0:T(8,128)(2,1)}), bf16[2,512,512]{2,1,0:T(8,128)(2,1)}) %all-gather.3.cloned.1.call-update) | async-done | bytes 1048592 | tf_op jit(solution)/shard_map/all_gather | solution.py:243
  98.4 1.1 fusion.1
  99.5 1.3 slice_bitcast_fusion
  100.8 0.3 maximum_maximum_fusion.mix
  101.0 0.0 all-to-all-done
  101.1 10.6 %spectral.1 = bf16[32,4,4,2,16,128]{5,4,3,2,1,0:T(8,128)(2,1)S(1)} custom-call(s32[2,6]{1,0:T(2,128)S(1)} %stack.2.chosen, bf16[32,4,4,2,16,128]{5,4,3,2,1,0:T(8,128)(2,1)} %bitcast.pieces, bf16[16,512,512]{2,1,0:T(8,128)(2,1)} %basis_high.1, bf16[16,512,512]{2,1,0:T(8,128)(2,1)} %basis_high.1, bf16[4,512,128]{2,1,0:T(8,128)(2,1)S(1)} %bitcast.10, ...), custom_call_target="tpu_custom_call" | custom-call | tf_op jit(solution)/shard_map/spectral/pallas_call | solution.py:190
  111.7 0.0 copy-start.3
  111.7 60.2 %all_to_all.10.pieces = bf16[128,4,2,16,128]{4,3,2,1,0:T(8,128)(2,1)S(1)} all-to-all(bf16[128,4,2,16,128]{4,3,2,1,0:T(8,128)(2,1)S(1)} %bitcast.9), channel_id=1, replica_groups=mesh['lat'=32,'chan'=4] {'lat','chan'}, dimensions={0} | all-to-all | bytes 8388608 | tf_op jit(solution)/shard_map/all_to_all | solution.py:255
  171.9 0.0 copy-done.3
  171.9 11.3 %inverse_fourier.1 = bf16[16,1440,128]{2,1,0:T(8,128)(2,1)} custom-call(s32[512]{0:T(512)S(1)} %reshape.27.modes, bf16[128,4,2,16,128]{4,3,2,1,0:T(8,128)(2,1)S(1)} %all_to_all.10.pieces, bf16[2,720,512]{2,1,0:T(8,128)(2,1)S(1)} %copy-done.3), custom_call_target="tpu_custom_call" | custom-call | tf_op jit(solution)/shard_map/inverse_fourier/pallas_call | solution.py:121
Async XLA Ops:
  7.4 2.7 %copy-start.1 = (bf16[16,1440,128]{2,1,0:T(8,128)(2,1)S(1)}, bf16[16,1440,128]{2,1,0:T(8,128)(2,1)}, u32[]{:S(2)}) copy-start(bf16[16,1440,128]{2,1,0:T(8,128)(2,1)} %field.1) | copy-start | bytes 17694724
  10.1 1.4 copy-start.2
  22.4 2.0 %copy-start = (bf16[128,4,2,16,128]{4,3,2,1,0:T(8,128)(2,1)}, bf16[128,4,2,16,128]{4,3,2,1,0:T(8,128)(2,1)S(1)}, u32[]{:S(2)}) copy-start(bf16[128,4,2,16,128]{4,3,2,1,0:T(8,128)(2,1)S(1)} %fourier.1) | copy-start | bytes 12582916
  24.4 13.9 %copy-start.4 = (bf16[512,128]{1,0:T(8,128)(2,1)S(1)}, bf16[512,128]{1,0:T(8,128)(2,1)}, u32[]{:S(2)}) copy-start(bf16[512,128]{1,0:T(8,128)(2,1)} %param.10) | copy-start | bytes 393220
  24.4 76.6 %all-to-all-start = ((bf16[128,4,2,16,128]{4,3,2,1,0:T(8,128)(2,1)}), bf16[128,4,2,16,128]{4,3,2,1,0:T(8,128)(2,1)}, u32[]{:S(2)}, u32[]{:S(2)}) async-start(bf16[128,4,2,16,128]{4,3,2,1,0:T(8,128)(2,1)} %copy-done), calls=%async_computation | async-start | bytes 8388608 | tf_op jit(solution)/shard_map/all_to_all | solution.py:251
  36.4 62.1 %all-gather.3.cloned.1.call-start = ((), (), s32[]{:S(2)}) async-start(), calls=%async_computation.2 | async-start | bytes 1310720 | tf_op jit(solution)/shard_map/all_gather | solution.py:243
  111.7 60.2 %copy-start.3 = (bf16[2,720,512]{2,1,0:T(8,128)(2,1)S(1)}, bf16[2,720,512]{2,1,0:T(8,128)(2,1)}, u32[]{:S(2)}) copy-start(bf16[2,720,512]{2,1,0:T(8,128)(2,1)} %constant.42.clone.table) | copy-start | bytes 4423684
Sparse Core Ops, SparseCore 0:
  38.9 59.5 all-gather.2

commit v2 on v1

v2 whole, which is shorter than its diff:
```python
import functools
import math

import jax
import jax.numpy as jnp
import ml_dtypes
import numpy as np
from jax import lax
from jax.experimental import pallas as pl
from jax.experimental.pallas import tpu as pltpu
from jax.sharding import PartitionSpec as P

BF16 = jnp.bfloat16
F32 = jnp.float32
LATS = 4
SPACING = 24


def folded_tables(lon_count, wave_count):
    half = lon_count // 2
    waves = np.arange(wave_count).reshape(-1, 2).T
    phases = (waves[:, :, None] * np.arange(half)[None, None, :]) % lon_count
    angles = phases * (2.0 * math.pi / lon_count)
    factor = 1.0 / math.sqrt(lon_count)
    table = np.stack([np.cos(angles) * factor, -np.sin(angles) * factor], axis=2)
    table = table.reshape(2, wave_count, half).astype(np.float32).astype(ml_dtypes.bfloat16)
    return table, np.ascontiguousarray(table.transpose(0, 2, 1))


def for_each_tile(modes, devices, slots, move):
    per_row = modes.shape[0] // slots
    last = modes.shape[0] * modes.shape[1] - 1

    def row_step(row, carry):
        for pair in range(modes.shape[0] // 2):
            mode = modes[2 * pair, row]
            odd = mode & 1
            even_row = jnp.where(odd == 1, last - mode, mode) >> 1
            device = row * per_row + 2 * pair // slots
            first = 2 * pair % slots
            move(device, first + odd, 0, even_row)
            move(device, first + 1 - odd, 1, (last >> 1) - even_row)
        return carry

    lax.fori_loop(0, devices // per_row, row_step, 0)


def fourier_kernel(modes, field, table, out, even, odd):
    step = pl.program_id(0)
    lats, lon_count, width = field.shape
    half = lon_count // 2
    waves = table.shape[1]
    devices, slots, _, band, _ = out.shape
    wide = (even, odd)
    low = jnp.concatenate([field[a, :half, :] for a in range(lats)], axis=1)
    high = jnp.concatenate([field[a, half:, :] for a in range(lats)], axis=1)
    for parity in range(2):
        folded = low + high if parity == 0 else low - high
        result = jnp.dot(table[parity], folded, preferred_element_type=F32)
        for a in range(lats):
            rows = pl.ds(step * lats + a, waves, stride=SPACING)
            wide[parity][rows, :] = result[:, a * width : (a + 1) * width]

    def pack(device, slot, parity, row):
        for p in range(2):
            start = pl.multiple_of((2 * row + p) * SPACING, 8)
            out[device, slot, p] = wide[parity][pl.ds(start, band), :].astype(BF16)

    @pl.when(step == pl.num_programs(0) - 1)
    def _():
        for_each_tile(modes, devices, slots, pack)


def fourier(modes, field, table, devices, slots):
    band, lon_count, width = field.shape
    waves = table.shape[1]
    return pl.pallas_call(
        fourier_kernel,
        grid_spec=pltpu.PrefetchScalarGridSpec(
            num_scalar_prefetch=1,
            grid=(band // LATS,),
            in_specs=[
                pl.BlockSpec((LATS, lon_count, width), lambda i, m: (i, 0, 0)),
                pl.BlockSpec(table.shape, lambda i, m: (0, 0, 0)),
            ],
            out_specs=pl.BlockSpec(memory_space=pltpu.VMEM),
            scratch_shapes=[pltpu.VMEM((waves * SPACING, width), F32)] * 2,
        ),
        out_shape=jax.ShapeDtypeStruct((devices, slots, 2, band, width), BF16),
        compiler_params=pltpu.CompilerParams(vmem_limit_bytes=56 * 2**20),
        cost_estimate=pl.CostEstimate(
            flops=4 * band * lon_count * waves * width,
            bytes_accessed=2 * (band * lon_count * width + 4 * waves * band * width),
            transcendentals=0,
        ),
        name="fourier",
    )(modes, field, table)


def inverse_kernel(modes, pieces, table, out, even, odd):
    step = pl.program_id(0)
    lats, lon_count, width = out.shape
    half = lon_count // 2
    waves = table.shape[2]
    devices, slots, _, band, _ = pieces.shape
    wide = (even, odd)

    def unpack(device, slot, parity, row):
        for p in range(2):
            start = pl.multiple_of((2 * row + p) * SPACING, 8)
            wide[parity][pl.ds(start, band), :] = pieces[device, slot, p].astype(F32)

    @pl.when(step == 0)
    def _():
        for_each_tile(modes, devices, slots, unpack)

    sums = []
    for parity in range(2):
        columns = [
            wide[parity][pl.ds(step * lats + a, waves, stride=SPACING), :].astype(BF16)
            for a in range(lats)
        ]
        sums.append(
            jnp.dot(table[parity], jnp.concatenate(columns, axis=1), preferred_element_type=F32)
        )
    low = (sums[0] + sums[1]).astype(BF16)
    high = (sums[0] - sums[1]).astype(BF16)
    for a in range(lats):
        out[a, :half, :] = low[:, a * width : (a + 1) * width]
        out[a, half:, :] = high[:, a * width : (a + 1) * width]


def inverse(modes, pieces, table):
    devices, slots, _, band, width = pieces.shape
    _, half, waves = table.shape
    return pl.pallas_call(
        inverse_kernel,
        grid_spec=pltpu.PrefetchScalarGridSpec(
            num_scalar_prefetch=1,
            grid=(band // LATS,),
            in_specs=[
                pl.BlockSpec(memory_space=pltpu.VMEM),
                pl.BlockSpec(table.shape, lambda i, m: (0, 0, 0)),
            ],
            out_specs=pl.BlockSpec((LATS, 2 * half, width), lambda i, m: (i, 0, 0)),
            scratch_shapes=[pltpu.VMEM((waves * SPACING, width), F32)] * 2,
        ),
        out_shape=jax.ShapeDtypeStruct((band, 2 * half, width), BF16),
        compiler_params=pltpu.CompilerParams(vmem_limit_bytes=48 * 2**20),
        name="inverse_fourier",
    )(modes, pieces, table)


def spectral_kernel(
    modes, place, pieces, basis_low, basis_high, parts, out, mix, column, hidden, mixed
):
    pair = pl.program_id(0)
    lat_parts, chan_parts, slots, _, band, width = pieces.shape
    lat_count = lat_parts * band
    channels = chan_parts * width
    row, chan = place[0], place[1]
    from_chan = [(chan + chan_parts - hops) % chan_parts for hops in range(chan_parts)]

    @pl.when(pair == 0)
    def _():
        for hops in range(chan_parts):
            real, imag = parts[hops, :width, :], parts[hops, width : 2 * width, :]
            here, below = hops * width, channels + hops * width
            mix[here : here + width, :channels] = real
            mix[here : here + width, channels:] = imag
            mix[below : below + width, :channels] = -imag
            mix[below : below + width, channels:] = real

    first_mode = modes[chan * slots + 2 * pair, row]
    second_mode = modes[chan * slots + 2 * pair + 1, row]
    swapped = (first_mode > second_mode).astype(jnp.int32)
    for which, basis in enumerate((basis_low, basis_high)):
        slot = 2 * pair + (swapped if which == 0 else 1 - swapped)
        wave = jnp.minimum(first_mode, second_mode) if which == 0 else jnp.maximum(
            first_mode, second_mode
        )
        count = basis.shape[1]
        first = lat_count - count
        for p in range(2):
            for hops in range(chan_parts):
                start = p * channels + hops * width
                column[:, start : start + width] = pieces[:, from_chan[hops], slot, p].reshape(
                    lat_count, width
                )
        degrees = first + lax.broadcasted_iota(jnp.int32, (count, lat_count), 0)
        kept = jnp.where(degrees >= wave, basis[0], jnp.zeros((), BF16))
        rows = 256
        for begin in range(0, count, rows):
            part = jnp.dot(kept[begin : begin + rows], column[...], preferred_element_type=F32)
            for hops in range(chan_parts):
                for sub in range(0, rows, width):
                    degree = first + begin + sub
                    lane = degree // width * width
                    factor = parts[hops, 2 * width :, lane : lane + width].astype(F32)
                    for p in range(2):
                        start = p * channels + hops * width
                        hidden[begin + sub : begin + sub + width, start : start + width] = (
                            part[sub : sub + width, start : start + width] * factor
                        ).astype(BF16)
        for begin in range(0, count, rows):
            mixed[begin : begin + rows, :] = jnp.dot(
                hidden[begin : begin + rows, :], mix[...], preferred_element_type=F32
            ).astype(BF16)
        for p in range(2):
            for j in range(0, chan_parts, 2):
                start = p * channels + j * width
                back = lax.dot_general(
                    kept,
                    mixed[:count, start : start + 2 * width],
                    (((0,), (0,)), ((), ())),
                    preferred_element_type=F32,
                ).astype(BF16)
                for k in range(2):
                    out[:, j + k, slot, p] = back[:, k * width : (k + 1) * width].reshape(
                        lat_parts, band, width
                    )


def spectral(modes, place, pieces, basis, parts):
    lat_parts, chan_parts, slots, _, band, width = pieces.shape
    degrees, lat_count = basis.shape[1:]
    channels2 = 2 * chan_parts * width

    def basis_slot(which, pair, modes, place):
        begin = place[1] * slots + 2 * pair
        swapped = (modes[begin, place[0]] > modes[begin + 1, place[0]]).astype(jnp.int32)
        return begin + (swapped if which == 0 else 1 - swapped)

    return pl.pallas_call(
        spectral_kernel,
        grid_spec=pltpu.PrefetchScalarGridSpec(
            num_scalar_prefetch=2,
            grid=(slots // 2,),
            in_specs=[
                pl.BlockSpec(memory_space=pltpu.VMEM),
                pl.BlockSpec((1, degrees, lat_count), lambda i, m, c: (basis_slot(0, i, m, c), 0, 0)),
                pl.BlockSpec(
                    (1, degrees // 2, lat_count), lambda i, m, c: (basis_slot(1, i, m, c), 1, 0)
                ),
                pl.BlockSpec(memory_space=pltpu.VMEM),
            ],
            out_specs=pl.BlockSpec(memory_space=pltpu.VMEM),
            scratch_shapes=[
                pltpu.VMEM((channels2, channels2), BF16),
                pltpu.VMEM((lat_count, channels2), BF16),
                pltpu.VMEM((degrees, channels2), BF16),
                pltpu.VMEM((degrees, channels2), BF16),
            ],
        ),
        out_shape=jax.ShapeDtypeStruct(pieces.shape, BF16),
        compiler_params=pltpu.CompilerParams(vmem_limit_bytes=40 * 2**20),
        name="spectral",
    )(modes, place, pieces, basis, basis, parts)


def local(lat_parts, chan_parts, grid_field, mode_lists, lat_basis, degree_gain, channel_mixer):
    devices = lat_parts * chan_parts
    slots = lat_basis.shape[0] // chan_parts
    width = grid_field.shape[2]
    forward_table, back_table = folded_tables(grid_field.shape[1], mode_lists.size)
    modes = mode_lists.T

    mixer_rows = channel_mixer.reshape(2 * width, -1)
    gain_rows = degree_gain.reshape(-1, width, width)
    payload = jnp.concatenate(
        [mixer_rows, jnp.concatenate(list(gain_rows), axis=1)], axis=0
    )
    parts = [payload] + [
        lax.ppermute(payload, "chan", [(i, (i + hops) % chan_parts) for i in range(chan_parts)])
        for hops in range(1, chan_parts)
    ]
    place = jnp.stack([lax.axis_index("lat"), lax.axis_index("chan")]).astype(jnp.int32)

    sent = fourier(modes, grid_field, jnp.asarray(forward_table), devices, slots)
    sent, parts = lax.optimization_barrier((sent, parts))
    got = lax.all_to_all(sent, ("lat", "chan"), 0, 0, tiled=True)
    got = got.reshape((lat_parts, chan_parts) + got.shape[1:])
    back = spectral(modes, place, got, lat_basis, jnp.stack(parts))
    back = back.reshape((devices,) + back.shape[2:])
    returned = lax.all_to_all(back, ("lat", "chan"), 0, 0, tiled=True)
    return inverse(modes, returned, jnp.asarray(back_table))


def solution(mesh):
    return jax.shard_map(
        functools.partial(local, mesh.shape["lat"], mesh.shape["chan"]),
        mesh=mesh,
        in_specs=(
            P("lat", None, "chan"),
            P(),
            P("lat", None, None),
            P(None, "chan"),
            P(None, "chan", None),
        ),
        out_specs=P("lat", None, "chan"),
        check_vma=False,
    )
```

time: 190 us -> 164 us (0.86)
  blocking collectives: 117 us -> 56.7 us
  waiting for transfers between devices: 4.36 us -> 60.9 us
  between operations: 13.5 us -> 0.05 us
  local copies, waits for them, and re-layouts: 9.29 us -> 0.83 us
  Pallas kernels: 32.9 us -> 30.1 us
    all_gather x1 -> x0, blocking collectives: 56.5 us -> none  [local(): all_gain = lax.all_gather(degree_gain, 'chan', axis=0)]
    all_to_all x1, waiting for transfers between devices: 0.01 us -> 52.6 us  [local(): got = lax.all_to_all(sent, ('lat', 'chan'), 0, 0, tiled=True)]
    ppermute x0 -> x3, waiting for transfers between devices: none -> 8.29 us  [local(): lax.ppermute(payload, 'chan', [(i, (i + hops) % chan_parts) for i in rang...]
    unnamed x11 -> x4, local copies, waits for them, and re-layouts: 6.87 us -> 0.01 us
    ppermute x0 -> x3, starting transfers between devices: none -> 5.36 us  [local(): lax.ppermute(payload, 'chan', [(i, (i + hops) % chan_parts) for i in rang...]
    all_to_all x1, starting transfers between devices: 12 us -> 8.15 us  [local(): got = lax.all_to_all(sent, ('lat', 'chan'), 0, 0, tiled=True)]
    all_gather x1 -> x0, waiting for transfers between devices: 3.68 us -> none  [local(): all_mixer = lax.all_gather(channel_mixer, 'chan', axis=1, tiled=True)]
    all_to_all x1, blocking collectives: 60.2 us -> 56.7 us  [local(): returned = lax.all_to_all(back, ('lat', 'chan'), 0, 0, tiled=True)]
  transfers between devices with their start and end apart: 2 -> 4, of which waited for: 1 -> 3; matrix products, arithmetic and copies ran while one was open for 2% -> 0% of each run, Pallas kernels for 0% -> 7%
where the time goes in v2:
time: 164 us; the launch traced here: 163 us
  waiting for transfers between devices  60.9 us (37%)
  blocking collectives  56.7 us (35%)
  Pallas kernels  30.1 us (18%)
  starting transfers between devices  13.5 us (8%)
    all_to_all x1, blocking collectives, local(): returned = lax.all_to_all(back, ('lat', 'chan'), 0, 0, tiled=True)  56.7 us
    all_to_all x1, waiting for transfers between devices, local(): got = lax.all_to_all(sent, ('lat', 'chan'), 0, 0, tiled=True)  52.6 us
    pallas_call x1, Pallas kernels, fourier(): pl.pallas_call(fourier_kernel, grid_spec=pltpu.PrefetchScalarGridSpec(num...  11.3 us
    pallas_call x1, Pallas kernels, spectral(): pl.pallas_call(spectral_kernel, grid_spec=pltpu.PrefetchScalarGridSpec(nu...  10.8 us
    ppermute x3, waiting for transfers between devices, local(): lax.ppermute(payload, 'chan', [(i, (i + hops) % chan_parts) for i in rang...  8.29 us
    all_to_all x1, starting transfers between devices, local(): got = lax.all_to_all(sent, ('lat', 'chan'), 0, 0, tiled=True)  8.15 us
    pallas_call x1, Pallas kernels, inverse(): pl.pallas_call(inverse_kernel, grid_spec=pltpu.PrefetchScalarGridSpec(num...  7.93 us
    ppermute x3, starting transfers between devices, local(): lax.ppermute(payload, 'chan', [(i, (i + hops) % chan_parts) for i in rang...  5.36 us
  transfers between devices with their start and end apart: 4, of which 3 were waited for; matrix products, arithmetic and copies ran while one was open for 0% of the time, Pallas kernels for 7%

profile of v2, /device:TPU:1, one launch (start us, length us, event | category | flops | bytes accessed | tf_op | source)
XLA Modules:
  0.0 163.3 jit_solution(1913912742557500851)
XLA Ops:
  0.0 0.8 fusion
  0.8 1.0 maximum_maximum_fusion
  1.8 4.7 %collective-permute-start.2 = (bf16[384,512]{1,0:T(8,128)(2,1)S(1)}, bf16[384,512]{1,0:T(8,128)(2,1)S(1)}, u32[]{:S(2)}, u32[]{:S(2)}) collective-permute-start(bf16[384,512]{1,0:T(8,128)(2,1)S(1)} %maximum_maximum_fusion), channel_id=1, source_target_pairs={{0,3},{1,0},{2,1},{3,2},{4,7},{5,4},{6,5},{7,6},{8,11},{9,8},{10,9... | collective-permute-start | bytes 1179656 | tf_op jit(solution)/shard_map/ppermute | solution.py:274
  6.5 0.0 collective-permute-start.1
  6.5 0.7 collective-permute-start
  7.2 11.3 %fourier.1 = bf16[128,4,2,16,128]{4,3,2,1,0:T(8,128)(2,1)} custom-call(s32[16,32]{1,0:T(8,128)} %bitcast.11, bf16[16,1440,128]{2,1,0:T(8,128)(2,1)} %field.1, bf16[2,512,720]{2,1,0:T(8,128)(2,1)} %constant.13.clone.table), custom_call_target="tpu_custom_call" | custom-call | flops 6039797760 | bytes 14286848 | tf_op jit(solution)/shard_map/fourier/pallas_call | solution.py:77
  18.5 4.0 %collective-permute-done.2 = bf16[384,512]{1,0:T(8,128)(2,1)S(1)} collective-permute-done((bf16[384,512]{1,0:T(8,128)(2,1)S(1)}, bf16[384,512]{1,0:T(8,128)(2,1)S(1)}, u32[]{:S(2)}, u32[]{:S(2)}) %collective-permute-start.2) | collective-permute-done | bytes 393248 | tf_op jit(solution)/shard_map/ppermute | solution.py:274
  22.5 0.0 collective-permute-done.1
  22.5 4.3 %collective-permute-done = bf16[384,512]{1,0:T(8,128)(2,1)S(1)} collective-permute-done((bf16[384,512]{1,0:T(8,128)(2,1)S(1)}, bf16[384,512]{1,0:T(8,128)(2,1)S(1)}, u32[]{:S(2)}, u32[]{:S(2)}) %collective-permute-start) | collective-permute-done | bytes 393248 | tf_op jit(solution)/shard_map/ppermute | solution.py:274
  26.8 8.2 %all-to-all-start = ((bf16[128,4,2,16,128]{4,3,2,1,0:T(8,128)(2,1)}), bf16[128,4,2,16,128]{4,3,2,1,0:T(8,128)(2,1)}, u32[]{:S(2)}, u32[]{:S(2)}) async-start(bf16[128,4,2,16,128]{4,3,2,1,0:T(8,128)(2,1)} %fourier.1), calls=%async_computation | async-start | bytes 8388608 | tf_op jit(solution)/shard_map/all_to_all | solution.py:281
  35.0 0.1 pad_add_fusion.place
  35.0 0.0 copy-start.1
  35.0 0.2 pad_maximum_fusion.parts
  35.2 52.6 %all-to-all-done = bf16[128,4,2,16,128]{4,3,2,1,0:T(8,128)(2,1)} async-done(((bf16[128,4,2,16,128]{4,3,2,1,0:T(8,128)(2,1)}), bf16[128,4,2,16,128]{4,3,2,1,0:T(8,128)(2,1)}, u32[]{:S(2)}, u32[]{:S(2)}) %all-to-all-start) | async-done | bytes 4194336 | tf_op jit(solution)/shard_map/all_to_all | solution.py:281
  87.8 0.0 copy-done.1
  87.8 10.8 %spectral.1 = bf16[32,4,4,2,16,128]{5,4,3,2,1,0:T(8,128)(2,1)S(1)} custom-call(s32[16,32]{1,0:T(8,128)S(1)} %bitcast.12, s32[2]{0:T(128)S(1)} %pad_add_fusion.place, bf16[32,4,4,2,16,128]{5,4,3,2,1,0:T(8,128)(2,1)} %bitcast.4.pieces, bf16[16,512,512]{2,1,0:T(8,128)(2,1)} %basis_high.1, bf16[16,512,512]{2,1,0:T(8,128)(2,1)} %basis_high.1, ...), custom_call_target="tpu_custom_call" | custom-call | tf_op jit(solution)/shard_map/spectral/pallas_call | solution.py:234
  98.7 0.0 copy-start
  98.7 56.7 %all_to_all.10.pieces = bf16[128,4,2,16,128]{4,3,2,1,0:T(8,128)(2,1)S(1)} all-to-all(bf16[128,4,2,16,128]{4,3,2,1,0:T(8,128)(2,1)S(1)} %bitcast.10), channel_id=1, replica_groups=mesh['lat'=32,'chan'=4] {'lat','chan'}, dimensions={0} | all-to-all | bytes 8388608 | tf_op jit(solution)/shard_map/all_to_all | solution.py:285
  155.4 0.0 copy-done
  155.4 7.9 %inverse_fourier.1 = bf16[16,1440,128]{2,1,0:T(8,128)(2,1)} custom-call(s32[16,32]{1,0:T(8,128)S(1)} %bitcast.13, bf16[128,4,2,16,128]{4,3,2,1,0:T(8,128)(2,1)S(1)} %all_to_all.10.pieces, bf16[2,720,512]{2,1,0:T(8,128)(2,1)S(1)} %copy-done), custom_call_target="tpu_custom_call" | custom-call | tf_op jit(solution)/shard_map/inverse_fourier/pallas_call | solution.py:136
Async XLA Ops:
  1.8 20.7 %collective-permute-start.2 = (bf16[384,512]{1,0:T(8,128)(2,1)S(1)}, bf16[384,512]{1,0:T(8,128)(2,1)S(1)}, u32[]{:S(2)}, u32[]{:S(2)}) collective-permute-start(bf16[384,512]{1,0:T(8,128)(2,1)S(1)} %maximum_maximum_fusion), channel_id=1, source_target_pairs={{0,3},{1,0},{2,1},{3,2},{4,7},{5,4},{6,5},{7,6},{8,11},{9,8},{10,9... | collective-permute-start | bytes 1179656 | tf_op jit(solution)/shard_map/ppermute | solution.py:274
  6.5 16.1 %collective-permute-start.1 = (bf16[384,512]{1,0:T(8,128)(2,1)S(1)}, bf16[384,512]{1,0:T(8,128)(2,1)S(1)}, u32[]{:S(2)}, u32[]{:S(2)}) collective-permute-start(bf16[384,512]{1,0:T(8,128)(2,1)S(1)} %maximum_maximum_fusion), channel_id=1, source_target_pairs={{0,2},{1,3},{2,0},{3,1},{4,6},{5,7},{6,4},{7,5},{8,10},{9,11},{10,... | collective-permute-start | bytes 1179656 | tf_op jit(solution)/shard_map/ppermute | solution.py:274
  6.5 20.3 %collective-permute-start = (bf16[384,512]{1,0:T(8,128)(2,1)S(1)}, bf16[384,512]{1,0:T(8,128)(2,1)S(1)}, u32[]{:S(2)}, u32[]{:S(2)}) collective-permute-start(bf16[384,512]{1,0:T(8,128)(2,1)S(1)} %maximum_maximum_fusion), channel_id=1, source_target_pairs={{0,1},{1,2},{2,3},{3,0},{4,5},{5,6},{6,7},{7,4},{8,9},{9,10},{10,1... | collective-permute-start | bytes 1179656 | tf_op jit(solution)/shard_map/ppermute | solution.py:274
  26.8 61.0 %all-to-all-start = ((bf16[128,4,2,16,128]{4,3,2,1,0:T(8,128)(2,1)}), bf16[128,4,2,16,128]{4,3,2,1,0:T(8,128)(2,1)}, u32[]{:S(2)}, u32[]{:S(2)}) async-start(bf16[128,4,2,16,128]{4,3,2,1,0:T(8,128)(2,1)} %fourier.1), calls=%async_computation | async-start | bytes 8388608 | tf_op jit(solution)/shard_map/all_to_all | solution.py:281
  35.0 52.8 %copy-start.1 = (s32[32,16]{0,1:T(8,128)S(1)}, s32[32,16]{0,1:T(8,128)}, u32[]{:S(2)}) copy-start(s32[32,16]{0,1:T(8,128)} %param.8) | copy-start | bytes 6148
  98.7 56.7 %copy-start = (bf16[2,720,512]{2,1,0:T(8,128)(2,1)S(1)}, bf16[2,720,512]{2,1,0:T(8,128)(2,1)}, u32[]{:S(2)}) copy-start(bf16[2,720,512]{2,1,0:T(8,128)(2,1)} %constant.14.clone.table) | copy-start | bytes 4423684

commit v3 on v2

v3 whole, which is shorter than its diff:
```python
import functools
import math

import jax
import jax.numpy as jnp
import ml_dtypes
import numpy as np
from jax import lax
from jax.experimental import pallas as pl
from jax.experimental.pallas import tpu as pltpu
from jax.sharding import PartitionSpec as P

BF16 = jnp.bfloat16
F32 = jnp.float32
LATS = 4
SPACING = 24


def folded_tables(lon_count, wave_count):
    half = lon_count // 2
    waves = np.arange(wave_count).reshape(-1, 2).T
    phases = (waves[:, :, None] * np.arange(half)[None, None, :]) % lon_count
    angles = phases * (2.0 * math.pi / lon_count)
    factor = 1.0 / math.sqrt(lon_count)
    table = np.stack([np.cos(angles) * factor, -np.sin(angles) * factor], axis=2)
    table = table.reshape(2, wave_count, half).astype(np.float32).astype(ml_dtypes.bfloat16)
    return table, np.ascontiguousarray(table.transpose(0, 2, 1))


def for_each_tile(modes, devices, slots, parities, move):
    per_row = modes.shape[0] // slots
    last = modes.shape[0] * modes.shape[1] - 1

    def row_step(row, carry):
        for pair in range(modes.shape[0] // 2):
            mode = modes[2 * pair, row]
            even_row = jnp.where(mode & 1 == 1, last - mode, mode) >> 1
            device = row * per_row + 2 * pair // slots
            for parity in parities:
                move(
                    device,
                    2 * pair % slots // 2,
                    parity,
                    even_row if parity == 0 else (last >> 1) - even_row,
                )
        return carry

    lax.fori_loop(0, devices // per_row, row_step, 0)


def fourier_kernel(parity, modes, field, table, *rest):
    out, wide = rest[-2:]
    step = pl.program_id(0)
    lats, lon_count, width = field.shape
    half = lon_count // 2
    waves = table.shape[1]
    devices = out.shape[0]
    pairs, _, band, _ = out.shape[-4:]
    low = jnp.concatenate([field[a, :half, :] for a in range(lats)], axis=1)
    high = jnp.concatenate([field[a, half:, :] for a in range(lats)], axis=1)
    folded = low + high if parity == 0 else low - high
    result = jnp.dot(table[0], folded, preferred_element_type=F32)
    for a in range(lats):
        rows = pl.ds(step * lats + a, waves, stride=SPACING)
        wide[rows, :] = result[:, a * width : (a + 1) * width]

    def pack(device, pair, parity, row):
        for p in range(2):
            start = pl.multiple_of((2 * row + p) * SPACING, 8)
            tile = wide[pl.ds(start, band), :].astype(BF16)
            if parity == 0:
                out[device, pair, p] = tile
            else:
                out[device, 1, pair, p] = tile

    @pl.when(step == pl.num_programs(0) - 1)
    def _():
        for_each_tile(modes, devices, 2 * pairs, (parity,), pack)

    if parity == 1:
        count = devices // (band // lats)
        rows = pl.ds(pl.multiple_of(step * count, count), count)
        out[rows, 0] = rest[0][rows]


def fourier(parity, modes, field, table, devices, slots, sent=None):
    band, lon_count, width = field.shape
    waves = table.shape[1]
    given = [] if sent is None else [sent]
    return pl.pallas_call(
        functools.partial(fourier_kernel, parity),
        grid_spec=pltpu.PrefetchScalarGridSpec(
            num_scalar_prefetch=1,
            grid=(band // LATS,),
            in_specs=[
                pl.BlockSpec((LATS, lon_count, width), lambda i, m: (i, 0, 0)),
                pl.BlockSpec((1,) + table.shape[1:], lambda i, m: (parity, 0, 0)),
            ]
            + [pl.BlockSpec(memory_space=pltpu.VMEM)] * len(given),
            out_specs=pl.BlockSpec(memory_space=pltpu.VMEM),
            scratch_shapes=[pltpu.VMEM((waves * SPACING, width), F32)],
        ),
        out_shape=jax.ShapeDtypeStruct(
            (devices,) + (2,) * len(given) + (slots // 2, 2, band, width), BF16
        ),
        compiler_params=pltpu.CompilerParams(vmem_limit_bytes=46 * 2**20),
        cost_estimate=pl.CostEstimate(
            flops=4 * band * lon_count * waves * width,
            bytes_accessed=2 * (band * lon_count * width + 4 * waves * band * width),
            transcendentals=0,
        ),
        name="fourier_odd" if parity else "fourier_even",
    )(modes, field, table, *given)


def inverse_kernel(modes, pieces, table, out, even, odd):
    step = pl.program_id(0)
    lats, lon_count, width = out.shape
    half = lon_count // 2
    waves = table.shape[2]
    devices, _, pairs, _, band, _ = pieces.shape
    wide = (even, odd)

    def unpack(device, pair, parity, row):
        for p in range(2):
            start = pl.multiple_of((2 * row + p) * SPACING, 8)
            wide[parity][pl.ds(start, band), :] = pieces[device, parity, pair, p].astype(F32)

    @pl.when(step == 0)
    def _():
        for_each_tile(modes, devices, 2 * pairs, (0, 1), unpack)

    sums = []
    for parity in range(2):
        columns = [
            wide[parity][pl.ds(step * lats + a, waves, stride=SPACING), :].astype(BF16)
            for a in range(lats)
        ]
        sums.append(
            jnp.dot(table[parity], jnp.concatenate(columns, axis=1), preferred_element_type=F32)
        )
    low = (sums[0] + sums[1]).astype(BF16)
    high = (sums[0] - sums[1]).astype(BF16)
    for a in range(lats):
        out[a, :half, :] = low[:, a * width : (a + 1) * width]
        out[a, half:, :] = high[:, a * width : (a + 1) * width]


def inverse(modes, pieces, table):
    band, width = pieces.shape[-2:]
    _, half, waves = table.shape
    return pl.pallas_call(
        inverse_kernel,
        grid_spec=pltpu.PrefetchScalarGridSpec(
            num_scalar_prefetch=1,
            grid=(band // LATS,),
            in_specs=[
                pl.BlockSpec(memory_space=pltpu.VMEM),
                pl.BlockSpec(table.shape, lambda i, m: (0, 0, 0)),
            ],
            out_specs=pl.BlockSpec((LATS, 2 * half, width), lambda i, m: (i, 0, 0)),
            scratch_shapes=[pltpu.VMEM((waves * SPACING, width), F32)] * 2,
        ),
        out_shape=jax.ShapeDtypeStruct((band, 2 * half, width), BF16),
        compiler_params=pltpu.CompilerParams(vmem_limit_bytes=48 * 2**20),
        name="inverse_fourier",
    )(modes, pieces, table)


def carry_kernel(place, mixer, gain, out):
    core = place[2]
    rows, width = mixer.shape[1], gain.shape[1]
    out[:rows, :] = mixer[core]
    blocks = out.shape[1] // width
    deep = gain.shape[0] // 2 // blocks
    for block in range(blocks):
        start = pl.multiple_of(core * (gain.shape[0] // 2) + block * deep, deep)
        out[rows:, block * width : (block + 1) * width] = gain[pl.ds(start, deep), :]


def carry(place, mixer, gain):
    rows = mixer.shape[1] + gain.size // 2 // mixer.shape[2]
    return pl.pallas_call(
        carry_kernel,
        in_specs=[pl.BlockSpec(memory_space=pltpu.SMEM)]
        + [pl.BlockSpec(memory_space=pltpu.VMEM)] * 2,
        out_specs=pl.BlockSpec(memory_space=pltpu.VMEM),
        out_shape=jax.ShapeDtypeStruct((rows, mixer.shape[2]), BF16),
        name="carry",
    )(place, mixer, gain)


def spectral_kernel(modes, place, pieces, basis_low, basis_high, mixer, gain, *rest):
    out, mix, gains, column, hidden, mixed = rest[-6:]
    pair = pl.program_id(0)
    lat_parts, chan_parts, _, pairs, _, band, width = pieces.shape
    shares = rest[: chan_parts - 1], rest[chan_parts - 1 : 2 * (chan_parts - 1)]
    lat_count = lat_parts * band
    channels = chan_parts * width
    row, chan, core = place[0], place[1], place[2]
    from_chan = [(chan + chan_parts - hops) % chan_parts for hops in range(chan_parts)]

    def place_mixer(hops, real, imag):
        here, below = hops * width, channels + hops * width
        if real is not None:
            mix[here : here + width, :channels] = real
            mix[below : below + width, channels:] = real
        if imag is not None:
            mix[here : here + width, channels:] = imag
            mix[below : below + width, :channels] = -imag

    def place_gain(hops, which, share):
        deep = share.shape[0] - width
        for block in range(chan_parts):
            start = pl.multiple_of(which * (gain.shape[0] // 2) + block * deep, deep)
            gains[hops, pl.ds(start, deep), :] = share[
                width:, block * width : (block + 1) * width
            ]

    @pl.when(pair == 0)
    def _():
        place_mixer(0, mixer[0], mixer[1])
        gains[0] = gain[...]
        for hops in range(1, chan_parts):
            for swap in range(2):
                share = shares[swap][hops - 1]
                place_gain(hops, core ^ swap, share)

                @pl.when(core ^ swap == 0)
                def _():
                    place_mixer(hops, share[:width, :], None)

                @pl.when(core ^ swap == 1)
                def _():
                    place_mixer(hops, None, share[:width, :])

    begin_mode = chan * 2 * pairs + 2 * pair
    lower = jnp.minimum(modes[begin_mode, row], modes[begin_mode + 1, row])
    higher = jnp.maximum(modes[begin_mode, row], modes[begin_mode + 1, row])
    for wave, basis in ((lower, basis_low), (higher, basis_high)):
        parity = wave & 1
        count = basis.shape[1]
        first = lat_count - count
        for p in range(2):
            for hops in range(chan_parts):
                start = p * channels + hops * width
                column[:, start : start + width] = pieces[
                    :, from_chan[hops], parity, pair, p
                ].reshape(lat_count, width)
        degrees = first + lax.broadcasted_iota(jnp.int32, (count, lat_count), 0)
        kept = jnp.where(degrees >= wave, basis[0], jnp.zeros((), BF16))
        rows = 256
        for begin in range(0, count, rows):
            part = jnp.dot(kept[begin : begin + rows], column[...], preferred_element_type=F32)
            for hops in range(chan_parts):
                factor = gains[hops, first + begin : first + begin + rows, :].astype(F32)
                for p in range(2):
                    start = p * channels + hops * width
                    hidden[begin : begin + rows, start : start + width] = (
                        part[:, start : start + width] * factor
                    ).astype(BF16)
        for begin in range(0, count, rows):
            mixed[begin : begin + rows, :] = jnp.dot(
                hidden[begin : begin + rows, :], mix[...], preferred_element_type=F32
            ).astype(BF16)
        for p in range(2):
            for j in range(0, chan_parts, 2):
                start = p * channels + j * width
                back = lax.dot_general(
                    kept,
                    mixed[:count, start : start + 2 * width],
                    (((0,), (0,)), ((), ())),
                    preferred_element_type=F32,
                ).astype(BF16)
                for k in range(2):
                    out[:, j + k, parity, pair, p] = back[:, k * width : (k + 1) * width].reshape(
                        lat_parts, band, width
                    )


def spectral(modes, place, pieces, basis, mixer, gain, shares):
    _, chan_parts, _, pairs, _, _, width = pieces.shape
    degrees, lat_count = basis.shape[1:]
    channels2 = 2 * chan_parts * width

    def basis_slot(which, pair, modes, place):
        begin = place[1] * 2 * pairs + 2 * pair
        swapped = (modes[begin, place[0]] > modes[begin + 1, place[0]]).astype(jnp.int32)
        return begin + (swapped if which == 0 else 1 - swapped)

    whole = pl.BlockSpec(memory_space=pltpu.VMEM)
    return pl.pallas_call(
        spectral_kernel,
        grid_spec=pltpu.PrefetchScalarGridSpec(
            num_scalar_prefetch=2,
            grid=(pairs,),
            in_specs=[
                whole,
                pl.BlockSpec((1, degrees, lat_count), lambda i, m, c: (basis_slot(0, i, m, c), 0, 0)),
                pl.BlockSpec(
                    (1, degrees // 2, lat_count), lambda i, m, c: (basis_slot(1, i, m, c), 1, 0)
                ),
                whole,
                whole,
            ]
            + [whole] * len(shares),
            out_specs=whole,
            scratch_shapes=[
                pltpu.VMEM((channels2, channels2), BF16),
                pltpu.VMEM((chan_parts,) + gain.shape, BF16),
                pltpu.VMEM((lat_count, channels2), BF16),
                pltpu.VMEM((degrees, channels2), BF16),
                pltpu.VMEM((degrees, channels2), BF16),
            ],
        ),
        out_shape=jax.ShapeDtypeStruct(pieces.shape, BF16),
        compiler_params=pltpu.CompilerParams(vmem_limit_bytes=40 * 2**20),
        name="spectral",
    )(modes, place, pieces, basis, basis, mixer, gain, *shares)


def local(lat_parts, chan_parts, grid_field, mode_lists, lat_basis, degree_gain, channel_mixer):
    devices = lat_parts * chan_parts
    slots = lat_basis.shape[0] // chan_parts
    forward_table, back_table = folded_tables(grid_field.shape[1], mode_lists.size)
    forward_table = jnp.asarray(forward_table)
    modes = mode_lists.T
    lat_index = lax.axis_index("lat")
    place = jnp.stack([lat_index, lax.axis_index("chan"), lat_index % 2]).astype(jnp.int32)

    share = carry(place, channel_mixer, degree_gain)
    shares = [
        lax.ppermute(share, "chan", [(i, (i + hops) % chan_parts) for i in range(chan_parts)])
        for hops in range(1, chan_parts)
    ]
    sent = fourier(0, modes, grid_field, forward_table, devices, slots)
    sent, shares = lax.optimization_barrier((sent, shares))
    swapped = [lax.ppermute(s, "lat", [(i, i ^ 1) for i in range(lat_parts)]) for s in shares]
    sent = fourier(1, modes, grid_field, forward_table, devices, slots, sent)
    sent, swapped, place = lax.optimization_barrier((sent, swapped, place))
    got = lax.all_to_all(sent, ("lat", "chan"), 0, 0, tiled=True)
    got = got.reshape((lat_parts, chan_parts) + got.shape[1:])
    back = spectral(
        modes, place, got, lat_basis, channel_mixer, degree_gain, shares + swapped
    )
    back = back.reshape((devices,) + back.shape[2:])
    returned = lax.all_to_all(back, ("lat", "chan"), 0, 0, tiled=True)
    return inverse(modes, returned, jnp.asarray(back_table))


def solution(mesh):
    return jax.shard_map(
        functools.partial(local, mesh.shape["lat"], mesh.shape["chan"]),
        mesh=mesh,
        in_specs=(
            P("lat", None, "chan"),
            P(),
            P("lat", None, None),
            P(None, "chan"),
            P(None, "chan", None),
        ),
        out_specs=P("lat", None, "chan"),
        check_vma=False,
    )
```

time: 164 us -> 161 us (0.982)
  blocking collectives: 56.7 us -> 117 us
  waiting for transfers between devices: 60.9 us -> 2.89 us
  starting transfers between devices: 13.5 us -> 6.64 us
    all_to_all x0 -> x1, blocking collectives: none -> 60 us  [local(): got = lax.all_to_all(sent, ('lat', 'chan'), 0, 0, tiled=True)]
    all_to_all x1 -> x0, waiting for transfers between devices: 52.6 us -> none  [local(): got = lax.all_to_all(sent, ('lat', 'chan'), 0, 0, tiled=True)]
    all_to_all x1 -> x0, starting transfers between devices: 8.15 us -> none  [local(): got = lax.all_to_all(sent, ('lat', 'chan'), 0, 0, tiled=True)]
    ppermute x3 -> x6, waiting for transfers between devices: 8.29 us -> 2.89 us  [the longest x3 2.89 us: local(): lax.ppermute(share, 'chan', [(i, (i + hops) % chan_parts) for i in range(...]
    pallas_call x1 -> x3, Pallas kernels: 11.3 us -> 14.6 us  [the longest x2 12.9 us: fourier(): pl.pallas_call(functools.partial(fourier_kernel, parity), grid_spec=pltpu...]
    unnamed x4 -> x14, local copies, waits for them, and re-layouts: 0.01 us -> 2.13 us
    ppermute x3 -> x6, starting transfers between devices: 5.36 us -> 6.64 us  [the longest x3 5.29 us: local(): lax.ppermute(share, 'chan', [(i, (i + hops) % chan_parts) for i in range(...]
  transfers between devices with their start and end apart: 4 -> 6, of which waited for: 3 -> 1; matrix products, arithmetic and copies ran while one was open for 0% -> 0% of each run, Pallas kernels for 7% -> 8%
where the time goes in v3:
time: 161 us
  blocking collectives  117 us (73%)
  Pallas kernels  31.6 us (20%)
  starting transfers between devices  6.64 us (4%)
  waiting for transfers between devices  2.89 us (2%)
  local copies, waits for them, and re-layouts  2.13 us (1%)
    all_to_all x1, blocking collectives, local(): got = lax.all_to_all(sent, ('lat', 'chan'), 0, 0, tiled=True)  60 us
    all_to_all x1, blocking collectives, local(): returned = lax.all_to_all(back, ('lat', 'chan'), 0, 0, tiled=True)  56.7 us
    pallas_call x2, Pallas kernels, fourier(): pl.pallas_call(functools.partial(fourier_kernel, parity), grid_spec=pltpu...  12.9 us
    pallas_call x1, Pallas kernels, spectral(): pl.pallas_call(spectral_kernel, grid_spec=pltpu.PrefetchScalarGridSpec(nu...  9.66 us
    pallas_call x1, Pallas kernels, inverse(): pl.pallas_call(inverse_kernel, grid_spec=pltpu.PrefetchScalarGridSpec(num...  7.29 us
    ppermute x3, starting transfers between devices, local(): lax.ppermute(share, 'chan', [(i, (i + hops) % chan_parts) for i in range(...  5.29 us
  transfers between devices with their start and end apart: 6, of which 1 were waited for; matrix products, arithmetic and copies ran while one was open for 0% of the time, Pallas kernels for 8%

profile of v3, /device:TPU:1, one launch (start us, length us, event | category | flops | bytes accessed | tf_op | source)
XLA Modules:
  0.0 160.6 jit_solution(2946666528329813957)
XLA Ops:
  0.0 0.6 pad_add_fusion.place
  0.6 1.7 %carry.1 = bf16[192,512]{1,0:T(8,128)(2,1)} custom-call(s32[3]{0:T(128)} %pad_add_fusion.place, bf16[2,128,512]{2,1,0:T(8,128)(2,1)} %mixer.3, bf16[512,128]{1,0:T(8,128)(2,1)} %gain.3), custom_call_target="tpu_custom_call" | custom-call | tf_op jit(solution)/shard_map/carry/pallas_call | solution.py:183
  2.3 4.6 %collective-permute-start.2 = (bf16[192,512]{1,0:T(8,128)(2,1)}, bf16[192,512]{1,0:T(8,128)(2,1)S(1)}, u32[]{:S(2)}, u32[]{:S(2)}) collective-permute-start(bf16[192,512]{1,0:T(8,128)(2,1)} %carry.1), channel_id=1, source_target_pairs={{0,3},{1,0},{2,1},{3,2},{4,7},{5,4},{6,5},{7,6},{8,11},{9,8},{10,9... | collective-permute-start | bytes 589832 | tf_op jit(solution)/shard_map/ppermute | solution.py:333
  6.9 0.0 collective-permute-start.1
  6.9 0.7 collective-permute-start
  7.6 0.7 copy-done.3
  8.3 1.4 copy-done.6
  9.7 6.4 %fourier_even.1.rest_0_ = bf16[128,2,2,16,128]{4,3,2,1,0:T(8,128)(2,1)S(1)} custom-call(s32[16,32]{1,0:T(8,128)S(1)} %bitcast.8, bf16[16,1440,128]{2,1,0:T(8,128)(2,1)} %field.3, bf16[2,512,720]{2,1,0:T(8,128)(2,1)S(1)} %copy-done.6), custom_call_target="tpu_custom_call" | custom-call | flops 6039797760 | bytes 14286848 | tf_op jit(solution)/shard_map/fourier_even/pallas_call | solution.py:90
  16.1 0.0 collective-permute-done.2.rest_2_
  16.1 0.0 collective-permute-done.1.rest_1_
  16.1 2.9 %collective-permute-done.rest_0_ = bf16[192,512]{1,0:T(8,128)(2,1)S(1)} collective-permute-done((bf16[192,512]{1,0:T(8,128)(2,1)}, bf16[192,512]{1,0:T(8,128)(2,1)S(1)}, u32[]{:S(2)}, u32[]{:S(2)}) %collective-permute-start) | collective-permute-done | bytes 196640 | tf_op jit(solution)/shard_map/ppermute | solution.py:333
  19.0 0.8 collective-permute-start.3
  19.9 0.0 collective-permute-start.4
  19.9 0.5 collective-permute-start.5
  20.4 6.5 %fourier_odd.1 = bf16[128,2,2,2,16,128]{5,4,3,2,1,0:T(8,128)(2,1)S(1)} custom-call(s32[16,32]{1,0:T(8,128)S(1)} %bitcast.9, bf16[16,1440,128]{2,1,0:T(8,128)(2,1)} %field.3, bf16[2,512,720]{2,1,0:T(8,128)(2,1)S(1)} %copy-done.6, bf16[128,2,2,16,128]{4,3,2,1,0:T(8,128)(2,1)S(1)} %fourier_even.1.rest_0_), custom_call_target="tpu_custom_call" | custom-call | flops 6039797760 | bytes 14286848 | tf_op jit(solution)/shard_map/fourier_odd/pallas_call | solution.py:90
  26.9 0.0 copy-start.1
  26.9 0.0 copy-start.2
  26.9 0.0 copy-start.5
  26.9 0.0 collective-permute-done.3.rest_3_
  27.0 0.0 collective-permute-done.4.rest_4_
  27.0 0.0 collective-permute-done.5.rest_5_
  27.0 60.0 %all_to_all.10 = bf16[128,2,2,2,16,128]{5,4,3,2,1,0:T(8,128)(2,1)S(1)} all-to-all(bf16[128,2,2,2,16,128]{5,4,3,2,1,0:T(8,128)(2,1)S(1)} %fourier_odd.1), channel_id=1, replica_groups=mesh['lat'=32,'chan'=4] {'lat','chan'}, dimensions={0} | all-to-all | bytes 8388608 | tf_op jit(solution)/shard_map/all_to_all | solution.py:341
  87.0 0.0 copy-done.1
  87.0 0.0 copy-done.2
  87.0 0.0 copy-done.5
  87.0 9.7 %spectral.1 = bf16[32,4,2,2,2,16,128]{6,5,4,3,2,1,0:T(8,128)(2,1)S(1)} custom-call(s32[16,32]{1,0:T(8,128)S(1)} %bitcast.10, s32[3]{0:T(128)S(1)} %copy-done.5, bf16[32,4,2,2,2,16,128]{6,5,4,3,2,1,0:T(8,128)(2,1)S(1)} %bitcast.6, bf16[16,512,512]{2,1,0:T(8,128)(2,1)} %basis_high.1, bf16[16,512,512]{2,1,0:T(8,128)(2,1)} %basis_high.1, ...), custom_call_target="tpu_custom_call" | custom-call | tf_op jit(solution)/shard_map/spectral/pallas_call | solution.py:292
  96.6 0.0 copy-start
  96.6 0.0 copy-start.4
  96.7 56.7 %all_to_all.11.pieces = bf16[128,2,2,2,16,128]{5,4,3,2,1,0:T(8,128)(2,1)S(1)} all-to-all(bf16[128,2,2,2,16,128]{5,4,3,2,1,0:T(8,128)(2,1)S(1)} %bitcast.7), channel_id=1, replica_groups=mesh['lat'=32,'chan'=4] {'lat','chan'}, dimensions={0} | all-to-all | bytes 8388608 | tf_op jit(solution)/shard_map/all_to_all | solution.py:347
  153.3 0.0 copy-done
  153.3 0.0 copy-done.4
  153.3 7.3 %inverse_fourier.1 = bf16[16,1440,128]{2,1,0:T(8,128)(2,1)} custom-call(s32[16,32]{1,0:T(8,128)S(1)} %bitcast.11, bf16[128,2,2,2,16,128]{5,4,3,2,1,0:T(8,128)(2,1)S(1)} %all_to_all.11.pieces, bf16[2,720,512]{2,1,0:T(8,128)(2,1)S(1)} %copy-done), custom_call_target="tpu_custom_call" | custom-call | tf_op jit(solution)/shard_map/inverse_fourier/pallas_call | solution.py:152
  (2 shorter events, 0.0 us)
Async XLA Ops:
  2.3 13.8 %collective-permute-start.2 = (bf16[192,512]{1,0:T(8,128)(2,1)}, bf16[192,512]{1,0:T(8,128)(2,1)S(1)}, u32[]{:S(2)}, u32[]{:S(2)}) collective-permute-start(bf16[192,512]{1,0:T(8,128)(2,1)} %carry.1), channel_id=1, source_target_pairs={{0,3},{1,0},{2,1},{3,2},{4,7},{5,4},{6,5},{7,6},{8,11},{9,8},{10,9... | collective-permute-start | bytes 589832 | tf_op jit(solution)/shard_map/ppermute | solution.py:333
  6.9 9.2 %collective-permute-start.1 = (bf16[192,512]{1,0:T(8,128)(2,1)}, bf16[192,512]{1,0:T(8,128)(2,1)S(1)}, u32[]{:S(2)}, u32[]{:S(2)}) collective-permute-start(bf16[192,512]{1,0:T(8,128)(2,1)} %carry.1), channel_id=1, source_target_pairs={{0,2},{1,3},{2,0},{3,1},{4,6},{5,7},{6,4},{7,5},{8,10},{9,11},{10,... | collective-permute-start | bytes 589832 | tf_op jit(solution)/shard_map/ppermute | solution.py:333
  6.9 12.1 %collective-permute-start = (bf16[192,512]{1,0:T(8,128)(2,1)}, bf16[192,512]{1,0:T(8,128)(2,1)S(1)}, u32[]{:S(2)}, u32[]{:S(2)}) collective-permute-start(bf16[192,512]{1,0:T(8,128)(2,1)} %carry.1), channel_id=1, source_target_pairs={{0,1},{1,2},{2,3},{3,0},{4,5},{5,6},{6,7},{7,4},{8,9},{9,10},{10,1... | collective-permute-start | bytes 589832 | tf_op jit(solution)/shard_map/ppermute | solution.py:333
  7.6 0.7 copy-start.3
  8.3 1.4 copy-start.6
  19.0 7.9 %collective-permute-start.3 = (bf16[192,512]{1,0:T(8,128)(2,1)S(1)}, bf16[192,512]{1,0:T(8,128)(2,1)S(1)}, u32[]{:S(2)}, u32[]{:S(2)}) collective-permute-start(bf16[192,512]{1,0:T(8,128)(2,1)S(1)} %collective-permute-done.rest_0_), channel_id=1, source_target_pairs={{0,4},{4,0},{8,12},{12,8},{16,20},{20,16},{24,28},{28,24},{32,36},... | collective-permute-start | bytes 589832 | tf_op jit(solution)/shard_map/ppermute | solution.py:338
  19.9 7.1 %collective-permute-start.4 = (bf16[192,512]{1,0:T(8,128)(2,1)S(1)}, bf16[192,512]{1,0:T(8,128)(2,1)S(1)}, u32[]{:S(2)}, u32[]{:S(2)}) collective-permute-start(bf16[192,512]{1,0:T(8,128)(2,1)S(1)} %collective-permute-done.1.rest_1_), channel_id=1, source_target_pairs={{0,4},{4,0},{8,12},{12,8},{16,20},{20,16},{24,28},{28,24},{32,36},... | collective-permute-start | bytes 589832 | tf_op jit(solution)/shard_map/ppermute | solution.py:338
  19.9 7.1 %collective-permute-start.5 = (bf16[192,512]{1,0:T(8,128)(2,1)S(1)}, bf16[192,512]{1,0:T(8,128)(2,1)S(1)}, u32[]{:S(2)}, u32[]{:S(2)}) collective-permute-start(bf16[192,512]{1,0:T(8,128)(2,1)S(1)} %collective-permute-done.2.rest_2_), channel_id=1, source_target_pairs={{0,4},{4,0},{8,12},{12,8},{16,20},{20,16},{24,28},{28,24},{32,36},... | collective-permute-start | bytes 589832 | tf_op jit(solution)/shard_map/ppermute | solution.py:338
  26.9 60.0 %copy-start.1 = (bf16[2,128,512]{2,1,0:T(8,128)(2,1)S(1)}, bf16[2,128,512]{2,1,0:T(8,128)(2,1)}, u32[]{:S(2)}) copy-start(bf16[2,128,512]{2,1,0:T(8,128)(2,1)} %mixer.3) | copy-start | bytes 786436
  26.9 60.0 %copy-start.2 = (bf16[512,128]{1,0:T(8,128)(2,1)S(1)}, bf16[512,128]{1,0:T(8,128)(2,1)}, u32[]{:S(2)}) copy-start(bf16[512,128]{1,0:T(8,128)(2,1)} %gain.3) | copy-start | bytes 393220
  26.9 60.0 %copy-start.5 = (s32[3]{0:T(128)S(1)}, s32[3]{0:T(128)}, u32[]{:S(2)}) copy-start(s32[3]{0:T(128)} %pad_add_fusion.place) | copy-start | bytes 40
  96.6 56.7 %copy-start = (bf16[2,720,512]{2,1,0:T(8,128)(2,1)S(1)}, bf16[2,720,512]{2,1,0:T(8,128)(2,1)}, u32[]{:S(2)}) copy-start(bf16[2,720,512]{2,1,0:T(8,128)(2,1)} %constant.27.clone.table) | copy-start | bytes 4423684
  96.6 56.7 %copy-start.4 = (s32[32,16]{0,1:T(8,128)S(1)}, s32[32,16]{0,1:T(8,128)}, u32[]{:S(2)}) copy-start(s32[32,16]{0,1:T(8,128)} %param.8) | copy-start | bytes 6148

commit v4 on v3

--- a/solution.py
+++ b/solution.py
@@ -27,7 +27,7 @@
     return table, np.ascontiguousarray(table.transpose(0, 2, 1))
 
 
-def for_each_tile(modes, devices, slots, parities, move):
+def for_each_tile(modes, devices, slots, move, after=None):
     per_row = modes.shape[0] // slots
     last = modes.shape[0] * modes.shape[1] - 1
 
@@ -36,81 +36,72 @@
             mode = modes[2 * pair, row]
             even_row = jnp.where(mode & 1 == 1, last - mode, mode) >> 1
             device = row * per_row + 2 * pair // slots
-            for parity in parities:
-                move(
-                    device,
-                    2 * pair % slots // 2,
-                    parity,
-                    even_row if parity == 0 else (last >> 1) - even_row,
-                )
+            place = 2 * pair % slots // 2
+            move(device, place, 0, even_row)
+            move(device, place, 1, (last >> 1) - even_row)
+        if after is not None:
+            after(pl.ds(pl.multiple_of(row * per_row, per_row), per_row))
         return carry
 
     lax.fori_loop(0, devices // per_row, row_step, 0)
 
 
-def fourier_kernel(parity, modes, field, table, *rest):
-    out, wide = rest[-2:]
+def fourier_kernel(modes, field, table, out, even, odd, packed, sem):
     step = pl.program_id(0)
     lats, lon_count, width = field.shape
     half = lon_count // 2
     waves = table.shape[1]
-    devices = out.shape[0]
-    pairs, _, band, _ = out.shape[-4:]
+    devices, _, pairs, _, band, _ = out.shape
+    wide = (even, odd)
     low = jnp.concatenate([field[a, :half, :] for a in range(lats)], axis=1)
     high = jnp.concatenate([field[a, half:, :] for a in range(lats)], axis=1)
-    folded = low + high if parity == 0 else low - high
-    result = jnp.dot(table[0], folded, preferred_element_type=F32)
-    for a in range(lats):
-        rows = pl.ds(step * lats + a, waves, stride=SPACING)
-        wide[rows, :] = result[:, a * width : (a + 1) * width]
+    for parity in range(2):
+        folded = low + high if parity == 0 else low - high
+        result = jnp.dot(table[parity], folded, preferred_element_type=F32)
+        for a in range(lats):
+            rows = pl.ds(step * lats + a, waves, stride=SPACING)
+            wide[parity][rows, :] = result[:, a * width : (a + 1) * width]
 
     def pack(device, pair, parity, row):
         for p in range(2):
             start = pl.multiple_of((2 * row + p) * SPACING, 8)
-            tile = wide[pl.ds(start, band), :].astype(BF16)
-            if parity == 0:
-                out[device, pair, p] = tile
-            else:
-                out[device, 1, pair, p] = tile
+            packed[device, parity, pair, p] = wide[parity][pl.ds(start, band), :].astype(BF16)
+
+    def send(some):
+        pltpu.make_async_copy(packed.at[some], out.at[some], sem).start()
 
     @pl.when(step == pl.num_programs(0) - 1)
     def _():
-        for_each_tile(modes, devices, 2 * pairs, (parity,), pack)
-
-    if parity == 1:
-        count = devices // (band // lats)
-        rows = pl.ds(pl.multiple_of(step * count, count), count)
-        out[rows, 0] = rest[0][rows]
-
-
-def fourier(parity, modes, field, table, devices, slots, sent=None):
+        for_each_tile(modes, devices, 2 * pairs, pack, send)
+        pltpu.make_async_copy(packed, out, sem).wait()
+
+
+def fourier(modes, field, table, devices, slots):
     band, lon_count, width = field.shape
     waves = table.shape[1]
-    given = [] if sent is None else [sent]
+    shape = (devices, 2, slots // 2, 2, band, width)
     return pl.pallas_call(
-        functools.partial(fourier_kernel, parity),
+        fourier_kernel,
         grid_spec=pltpu.PrefetchScalarGridSpec(
             num_scalar_prefetch=1,
             grid=(band // LATS,),
             in_specs=[
                 pl.BlockSpec((LATS, lon_count, width), lambda i, m: (i, 0, 0)),
-                pl.BlockSpec((1,) + table.shape[1:], lambda i, m: (parity, 0, 0)),
-            ]
-            + [pl.BlockSpec(memory_space=pltpu.VMEM)] * len(given),
-            out_specs=pl.BlockSpec(memory_space=pltpu.VMEM),
-            scratch_shapes=[pltpu.VMEM((waves * SPACING, width), F32)],
-        ),
-        out_shape=jax.ShapeDtypeStruct(
-            (devices,) + (2,) * len(given) + (slots // 2, 2, band, width), BF16
-        ),
-        compiler_params=pltpu.CompilerParams(vmem_limit_bytes=46 * 2**20),
+                pl.BlockSpec(table.shape, lambda i, m: (0, 0, 0)),
+            ],
+            out_specs=pl.BlockSpec(memory_space=pl.ANY),
+            scratch_shapes=[pltpu.VMEM((waves * SPACING, width), F32)] * 2
+            + [pltpu.VMEM(shape, BF16), pltpu.SemaphoreType.DMA],
+        ),
+        out_shape=jax.ShapeDtypeStruct(shape, BF16),
+        compiler_params=pltpu.CompilerParams(vmem_limit_bytes=56 * 2**20),
         cost_estimate=pl.CostEstimate(
             flops=4 * band * lon_count * waves * width,
             bytes_accessed=2 * (band * lon_count * width + 4 * waves * band * width),
             transcendentals=0,
         ),
-        name="fourier_odd" if parity else "fourier_even",
-    )(modes, field, table, *given)
+        name="fourier",
+    )(modes, field, table)
 
 
 def inverse_kernel(modes, pieces, table, out, even, odd):
@@ -128,7 +119,7 @@
 
     @pl.when(step == 0)
     def _():
-        for_each_tile(modes, devices, 2 * pairs, (0, 1), unpack)
+        for_each_tile(modes, devices, 2 * pairs, unpack)
 
     sums = []
     for parity in range(2):
@@ -167,8 +158,8 @@
     )(modes, pieces, table)
 
 
-def carry_kernel(place, mixer, gain, out):
-    core = place[2]
+def carry_kernel(mixer, gain, out):
+    core = lax.axis_index("lat") & 1
     rows, width = mixer.shape[1], gain.shape[1]
     out[:rows, :] = mixer[core]
     blocks = out.shape[1] // width
@@ -178,22 +169,22 @@
         out[rows:, block * width : (block + 1) * width] = gain[pl.ds(start, deep), :]
 
 
-def carry(place, mixer, gain):
+def carry(mixer, gain):
     rows = mixer.shape[1] + gain.size // 2 // mixer.shape[2]
     return pl.pallas_call(
         carry_kernel,
-        in_specs=[pl.BlockSpec(memory_space=pltpu.SMEM)]
-        + [pl.BlockSpec(memory_space=pltpu.VMEM)] * 2,
+        in_specs=[pl.BlockSpec(memory_space=pltpu.VMEM)] * 2,
         out_specs=pl.BlockSpec(memory_space=pltpu.VMEM),
         out_shape=jax.ShapeDtypeStruct((rows, mixer.shape[2]), BF16),
         name="carry",
-    )(place, mixer, gain)
+    )(mixer, gain)
 
 
 def spectral_kernel(modes, place, pieces, basis_low, basis_high, mixer, gain, *rest):
     out, mix, gains, column, hidden, mixed = rest[-6:]
     pair = pl.program_id(0)
-    lat_parts, chan_parts, _, pairs, _, band, width = pieces.shape
+    lat_parts, chan_parts, _, _, _, band, width = pieces.shape
+    pairs = pl.num_programs(0)
     shares = rest[: chan_parts - 1], rest[chan_parts - 1 : 2 * (chan_parts - 1)]
     lat_count = lat_parts * band
     channels = chan_parts * width
@@ -245,7 +236,7 @@
             for hops in range(chan_parts):
                 start = p * channels + hops * width
                 column[:, start : start + width] = pieces[
-                    :, from_chan[hops], parity, pair, p
+                    :, from_chan[hops], parity, 0, p
                 ].reshape(lat_count, width)
         degrees = first + lax.broadcasted_iota(jnp.int32, (count, lat_count), 0)
         kept = jnp.where(degrees >= wave, basis[0], jnp.zeros((), BF16))
@@ -273,7 +264,7 @@
                     preferred_element_type=F32,
                 ).astype(BF16)
                 for k in range(2):
-                    out[:, j + k, parity, pair, p] = back[:, k * width : (k + 1) * width].reshape(
+                    out[:, j + k, parity, 0, p] = back[:, k * width : (k + 1) * width].reshape(
                         lat_parts, band, width
                     )
 
@@ -289,13 +280,16 @@
         return begin + (swapped if which == 0 else 1 - swapped)
 
     whole = pl.BlockSpec(memory_space=pltpu.VMEM)
+    one_pair = pl.BlockSpec(
+        pieces.shape[:3] + (1,) + pieces.shape[4:], lambda i, m, c: (0, 0, 0, i, 0, 0, 0)
+    )
     return pl.pallas_call(
         spectral_kernel,
         grid_spec=pltpu.PrefetchScalarGridSpec(
             num_scalar_prefetch=2,
             grid=(pairs,),
             in_specs=[
-                whole,
+                one_pair,
                 pl.BlockSpec((1, degrees, lat_count), lambda i, m, c: (basis_slot(0, i, m, c), 0, 0)),
                 pl.BlockSpec(
                     (1, degrees // 2, lat_count), lambda i, m, c: (basis_slot(1, i, m, c), 1, 0)
@@ -304,7 +298,7 @@
                 whole,
             ]
             + [whole] * len(shares),
-            out_specs=whole,
+            out_specs=one_pair,
             scratch_shapes=[
                 pltpu.VMEM((channels2, channels2), BF16),
                 pltpu.VMEM((chan_parts,) + gain.shape, BF16),
@@ -328,16 +322,14 @@
     lat_index = lax.axis_index("lat")
     place = jnp.stack([lat_index, lax.axis_index("chan"), lat_index % 2]).astype(jnp.int32)
 
-    share = carry(place, channel_mixer, degree_gain)
+    share = carry(channel_mixer, degree_gain)
     shares = [
         lax.ppermute(share, "chan", [(i, (i + hops) % chan_parts) for i in range(chan_parts)])
         for hops in range(1, chan_parts)
     ]
-    sent = fourier(0, modes, grid_field, forward_table, devices, slots)
+    sent = fourier(modes, grid_field, forward_table, devices, slots)
     sent, shares = lax.optimization_barrier((sent, shares))
     swapped = [lax.ppermute(s, "lat", [(i, i ^ 1) for i in range(lat_parts)]) for s in shares]
-    sent = fourier(1, modes, grid_field, forward_table, devices, slots, sent)
-    sent, swapped, place = lax.optimization_barrier((sent, swapped, place))
     got = lax.all_to_all(sent, ("lat", "chan"), 0, 0, tiled=True)
     got = got.reshape((lat_parts, chan_parts) + got.shape[1:])
     back = spectral(

time: 161 us -> 154 us (0.957)
  blocking collectives: 117 us -> 56.6 us
  waiting for transfers between devices: 2.89 us -> 53 us
  starting transfers between devices: 6.64 us -> 15.3 us
  Pallas kernels: 31.6 us -> 29 us
  local copies, waits for them, and re-layouts: 2.13 us -> 0.03 us
    all_to_all x1 -> x0, blocking collectives: 60 us -> none  [local(): got = lax.all_to_all(sent, ('lat', 'chan'), 0, 0, tiled=True)]
    all_to_all x0 -> x1, waiting for transfers between devices: none -> 49.9 us  [local(): got = lax.all_to_all(sent, ('lat', 'chan'), 0, 0, tiled=True)]
    all_to_all x0 -> x1, starting transfers between devices: none -> 8.29 us  [local(): got = lax.all_to_all(sent, ('lat', 'chan'), 0, 0, tiled=True)]
    pallas_call x3 -> x2, Pallas kernels: 14.6 us -> 11.1 us  [the longest x1 9.41 us: fourier(): pl.pallas_call(fourier_kernel, grid_spec=pltpu.PrefetchScalarGridSpec(num...]
    unnamed x14 -> x8, local copies, waits for them, and re-layouts: 2.13 us -> 0.03 us
  transfers between devices with their start and end apart: 6 -> 7, of which waited for: 1 -> 5; matrix products, arithmetic and copies ran while one was open for 0% -> 0% of each run, Pallas kernels for 8% -> 6%
where the time goes in v4:
time: 154 us
  blocking collectives  56.6 us (37%)
  waiting for transfers between devices  53 us (34%)
  Pallas kernels  29 us (19%)
  starting transfers between devices  15.3 us (10%)
    all_to_all x1, blocking collectives, local(): returned = lax.all_to_all(back, ('lat', 'chan'), 0, 0, tiled=True)  56.6 us
    all_to_all x1, waiting for transfers between devices, local(): got = lax.all_to_all(sent, ('lat', 'chan'), 0, 0, tiled=True)  49.9 us
    pallas_call x1, Pallas kernels, spectral(): pl.pallas_call(spectral_kernel, grid_spec=pltpu.PrefetchScalarGridSpec(nu...  10.6 us
    pallas_call x1, Pallas kernels, fourier(): pl.pallas_call(fourier_kernel, grid_spec=pltpu.PrefetchScalarGridSpec(num...  9.41 us
    all_to_all x1, starting transfers between devices, local(): got = lax.all_to_all(sent, ('lat', 'chan'), 0, 0, tiled=True)  8.29 us
    pallas_call x1, Pallas kernels, inverse(): pl.pallas_call(inverse_kernel, grid_spec=pltpu.PrefetchScalarGridSpec(num...  7.29 us
    ppermute x3, starting transfers between devices, local(): lax.ppermute(share, 'chan', [(i, (i + hops) % chan_parts) for i in range(...  5.29 us
  transfers between devices with their start and end apart: 7, of which 5 were waited for; matrix products, arithmetic and copies ran while one was open for 0% of the time, Pallas kernels for 6%

profile of v4, /device:TPU:1, one launch (start us, length us, event | category | flops | bytes accessed | tf_op | source)
XLA Modules:
  0.0 154.1 jit_solution(11602179894328709052)
XLA Ops:
  0.0 1.7 %carry.1 = bf16[192,512]{1,0:T(8,128)(2,1)} custom-call(bf16[2,128,512]{2,1,0:T(8,128)(2,1)} %mixer.3, bf16[512,128]{1,0:T(8,128)(2,1)} %gain.3), custom_call_target="tpu_custom_call" | custom-call | tf_op jit(solution)/shard_map/carry/pallas_call | solution.py:174
  1.7 4.6 %collective-permute-start.2 = (bf16[192,512]{1,0:T(8,128)(2,1)}, bf16[192,512]{1,0:T(8,128)(2,1)S(1)}, u32[]{:S(2)}, u32[]{:S(2)}) collective-permute-start(bf16[192,512]{1,0:T(8,128)(2,1)} %carry.1), channel_id=1, source_target_pairs={{0,3},{1,0},{2,1},{3,2},{4,7},{5,4},{6,5},{7,6},{8,11},{9,8},{10,9... | collective-permute-start | bytes 589832 | tf_op jit(solution)/shard_map/ppermute | solution.py:327
  6.3 0.0 collective-permute-start.1
  6.3 0.7 collective-permute-start
  7.0 9.4 %fourier.1 = bf16[128,2,2,2,16,128]{5,4,3,2,1,0:T(8,128)(2,1)} custom-call(s32[16,32]{1,0:T(8,128)} %bitcast.7, bf16[16,1440,128]{2,1,0:T(8,128)(2,1)} %field.1, bf16[2,512,720]{2,1,0:T(8,128)(2,1)} %constant.26.clone.table), custom_call_target="tpu_custom_call" | custom-call | flops 6039797760 | bytes 14286848 | tf_op jit(solution)/shard_map/fourier/pallas_call | solution.py:83
  16.4 0.0 copy-start.1
  16.4 0.0 copy-start.2
  16.4 0.0 copy-start.3
  16.4 0.0 collective-permute-done.2.rest_2_
  16.4 0.0 collective-permute-done.1.rest_1_
  16.4 1.9 %collective-permute-done.rest_0_ = bf16[192,512]{1,0:T(8,128)(2,1)S(1)} collective-permute-done((bf16[192,512]{1,0:T(8,128)(2,1)}, bf16[192,512]{1,0:T(8,128)(2,1)S(1)}, u32[]{:S(2)}, u32[]{:S(2)}) %collective-permute-start) | collective-permute-done | bytes 196640 | tf_op jit(solution)/shard_map/ppermute | solution.py:327
  18.4 8.3 %all-to-all-start = ((bf16[128,2,2,2,16,128]{5,4,3,2,1,0:T(8,128)(2,1)}), bf16[128,2,2,2,16,128]{5,4,3,2,1,0:T(8,128)(2,1)}, u32[]{:S(2)}, u32[]{:S(2)}) async-start(bf16[128,2,2,2,16,128]{5,4,3,2,1,0:T(8,128)(2,1)} %fourier.1), calls=%async_computation | async-start | bytes 8388608 | tf_op jit(solution)/shard_map/all_to_all | solution.py:333
  26.7 1.2 collective-permute-start.3
  27.9 0.1 collective-permute-start.4
  28.0 0.4 collective-permute-start.5
  28.4 0.1 pad_add_fusion.place
  28.5 0.5 collective-permute-done.3.rest_3_
  29.0 0.4 collective-permute-done.4.rest_4_
  29.3 0.3 collective-permute-done.5.rest_5_
  29.6 49.9 %all-to-all-done = bf16[128,2,2,2,16,128]{5,4,3,2,1,0:T(8,128)(2,1)} async-done(((bf16[128,2,2,2,16,128]{5,4,3,2,1,0:T(8,128)(2,1)}), bf16[128,2,2,2,16,128]{5,4,3,2,1,0:T(8,128)(2,1)}, u32[]{:S(2)}, u32[]{:S(2)}) %all-to-all-start) | async-done | bytes 4194336 | tf_op jit(solution)/shard_map/all_to_all | solution.py:333
  79.5 0.0 copy-done.1
  79.5 0.0 copy-done.2
  79.5 0.0 copy-done.3
  79.5 10.6 %spectral.1 = bf16[32,4,2,2,2,16,128]{6,5,4,3,2,1,0:T(8,128)(2,1)S(1)} custom-call(s32[16,32]{1,0:T(8,128)S(1)} %bitcast.8, s32[3]{0:T(128)S(1)} %pad_add_fusion.place, bf16[32,4,2,2,2,16,128]{6,5,4,3,2,1,0:T(8,128)(2,1)} %bitcast.4.pieces, bf16[16,512,512]{2,1,0:T(8,128)(2,1)} %basis_high.1, bf16[16,512,512]{2,1,0:T(8,128)(2,1)} %basis_high.1, ...), custom_call_target="tpu_custom_call" | custom-call | tf_op jit(solution)/shard_map/spectral/pallas_call | solution.py:286
  90.2 0.0 copy-start
  90.2 56.6 %all_to_all.10.pieces = bf16[128,2,2,2,16,128]{5,4,3,2,1,0:T(8,128)(2,1)S(1)} all-to-all(bf16[128,2,2,2,16,128]{5,4,3,2,1,0:T(8,128)(2,1)S(1)} %bitcast.6), channel_id=1, replica_groups=mesh['lat'=32,'chan'=4] {'lat','chan'}, dimensions={0} | all-to-all | bytes 8388608 | tf_op jit(solution)/shard_map/all_to_all | solution.py:339
  146.8 0.0 copy-done
  146.8 7.3 %inverse_fourier.1 = bf16[16,1440,128]{2,1,0:T(8,128)(2,1)} custom-call(s32[16,32]{1,0:T(8,128)S(1)} %bitcast.9, bf16[128,2,2,2,16,128]{5,4,3,2,1,0:T(8,128)(2,1)S(1)} %all_to_all.10.pieces, bf16[2,720,512]{2,1,0:T(8,128)(2,1)S(1)} %copy-done), custom_call_target="tpu_custom_call" | custom-call | tf_op jit(solution)/shard_map/inverse_fourier/pallas_call | solution.py:143
Async XLA Ops:
  1.7 14.7 %collective-permute-start.2 = (bf16[192,512]{1,0:T(8,128)(2,1)}, bf16[192,512]{1,0:T(8,128)(2,1)S(1)}, u32[]{:S(2)}, u32[]{:S(2)}) collective-permute-start(bf16[192,512]{1,0:T(8,128)(2,1)} %carry.1), channel_id=1, source_target_pairs={{0,3},{1,0},{2,1},{3,2},{4,7},{5,4},{6,5},{7,6},{8,11},{9,8},{10,9... | collective-permute-start | bytes 589832 | tf_op jit(solution)/shard_map/ppermute | solution.py:327
  6.3 10.2 %collective-permute-start.1 = (bf16[192,512]{1,0:T(8,128)(2,1)}, bf16[192,512]{1,0:T(8,128)(2,1)S(1)}, u32[]{:S(2)}, u32[]{:S(2)}) collective-permute-start(bf16[192,512]{1,0:T(8,128)(2,1)} %carry.1), channel_id=1, source_target_pairs={{0,2},{1,3},{2,0},{3,1},{4,6},{5,7},{6,4},{7,5},{8,10},{9,11},{10,... | collective-permute-start | bytes 589832 | tf_op jit(solution)/shard_map/ppermute | solution.py:327
  6.3 12.1 %collective-permute-start = (bf16[192,512]{1,0:T(8,128)(2,1)}, bf16[192,512]{1,0:T(8,128)(2,1)S(1)}, u32[]{:S(2)}, u32[]{:S(2)}) collective-permute-start(bf16[192,512]{1,0:T(8,128)(2,1)} %carry.1), channel_id=1, source_target_pairs={{0,1},{1,2},{2,3},{3,0},{4,5},{5,6},{6,7},{7,4},{8,9},{9,10},{10,1... | collective-permute-start | bytes 589832 | tf_op jit(solution)/shard_map/ppermute | solution.py:327
  16.4 63.1 %copy-start.1 = (bf16[2,128,512]{2,1,0:T(8,128)(2,1)S(1)}, bf16[2,128,512]{2,1,0:T(8,128)(2,1)}, u32[]{:S(2)}) copy-start(bf16[2,128,512]{2,1,0:T(8,128)(2,1)} %mixer.3) | copy-start | bytes 786436
  16.4 63.1 %copy-start.2 = (bf16[512,128]{1,0:T(8,128)(2,1)S(1)}, bf16[512,128]{1,0:T(8,128)(2,1)}, u32[]{:S(2)}) copy-start(bf16[512,128]{1,0:T(8,128)(2,1)} %gain.3) | copy-start | bytes 393220
  16.4 63.1 %copy-start.3 = (s32[32,16]{0,1:T(8,128)S(1)}, s32[32,16]{0,1:T(8,128)}, u32[]{:S(2)}) copy-start(s32[32,16]{0,1:T(8,128)} %param.8) | copy-start | bytes 6148
  18.4 61.1 %all-to-all-start = ((bf16[128,2,2,2,16,128]{5,4,3,2,1,0:T(8,128)(2,1)}), bf16[128,2,2,2,16,128]{5,4,3,2,1,0:T(8,128)(2,1)}, u32[]{:S(2)}, u32[]{:S(2)}) async-start(bf16[128,2,2,2,16,128]{5,4,3,2,1,0:T(8,128)(2,1)} %fourier.1), calls=%async_computation | async-start | bytes 8388608 | tf_op jit(solution)/shard_map/all_to_all | solution.py:333
  26.7 2.3 %collective-permute-start.3 = (bf16[192,512]{1,0:T(8,128)(2,1)S(1)}, bf16[192,512]{1,0:T(8,128)(2,1)S(1)}, u32[]{:S(2)}, u32[]{:S(2)}) collective-permute-start(bf16[192,512]{1,0:T(8,128)(2,1)S(1)} %collective-permute-done.rest_0_), channel_id=1, source_target_pairs={{0,4},{4,0},{8,12},{12,8},{16,20},{20,16},{24,28},{28,24},{32,36},... | collective-permute-start | bytes 589832 | tf_op jit(solution)/shard_map/ppermute | solution.py:332
  27.9 1.4 collective-permute-start.4
  28.0 1.6 %collective-permute-start.5 = (bf16[192,512]{1,0:T(8,128)(2,1)S(1)}, bf16[192,512]{1,0:T(8,128)(2,1)S(1)}, u32[]{:S(2)}, u32[]{:S(2)}) collective-permute-start(bf16[192,512]{1,0:T(8,128)(2,1)S(1)} %collective-permute-done.2.rest_2_), channel_id=1, source_target_pairs={{0,4},{4,0},{8,12},{12,8},{16,20},{20,16},{24,28},{28,24},{32,36},... | collective-permute-start | bytes 589832 | tf_op jit(solution)/shard_map/ppermute | solution.py:332
  90.2 56.7 %copy-start = (bf16[2,720,512]{2,1,0:T(8,128)(2,1)S(1)}, bf16[2,720,512]{2,1,0:T(8,128)(2,1)}, u32[]{:S(2)}) copy-start(bf16[2,720,512]{2,1,0:T(8,128)(2,1)} %constant.27.clone.table) | copy-start | bytes 4423684

commit v5 on v4

--- a/solution.py
+++ b/solution.py
@@ -180,16 +180,13 @@
     )(mixer, gain)
 
 
-def spectral_kernel(modes, place, pieces, basis_low, basis_high, mixer, gain, *rest):
-    out, mix, gains, column, hidden, mixed = rest[-6:]
-    pair = pl.program_id(0)
-    lat_parts, chan_parts, _, _, _, band, width = pieces.shape
-    pairs = pl.num_programs(0)
+def gather_kernel(mixer, gain, *rest):
+    mix, gains = rest[-2:]
+    width = gain.shape[1]
+    chan_parts = gains.shape[0]
+    channels = chan_parts * width
+    core = lax.axis_index("lat") & 1
     shares = rest[: chan_parts - 1], rest[chan_parts - 1 : 2 * (chan_parts - 1)]
-    lat_count = lat_parts * band
-    channels = chan_parts * width
-    row, chan, core = place[0], place[1], place[2]
-    from_chan = [(chan + chan_parts - hops) % chan_parts for hops in range(chan_parts)]
 
     def place_mixer(hops, real, imag):
         here, below = hops * width, channels + hops * width
@@ -200,76 +197,145 @@
             mix[here : here + width, channels:] = imag
             mix[below : below + width, :channels] = -imag
 
-    def place_gain(hops, which, share):
-        deep = share.shape[0] - width
-        for block in range(chan_parts):
-            start = pl.multiple_of(which * (gain.shape[0] // 2) + block * deep, deep)
-            gains[hops, pl.ds(start, deep), :] = share[
-                width:, block * width : (block + 1) * width
-            ]
-
-    @pl.when(pair == 0)
-    def _():
-        place_mixer(0, mixer[0], mixer[1])
-        gains[0] = gain[...]
-        for hops in range(1, chan_parts):
-            for swap in range(2):
-                share = shares[swap][hops - 1]
-                place_gain(hops, core ^ swap, share)
-
-                @pl.when(core ^ swap == 0)
-                def _():
-                    place_mixer(hops, share[:width, :], None)
-
-                @pl.when(core ^ swap == 1)
-                def _():
-                    place_mixer(hops, None, share[:width, :])
+    place_mixer(0, mixer[0], mixer[1])
+    gains[0] = gain[...]
+    for hops in range(1, chan_parts):
+        for swap in range(2):
+            share = shares[swap][hops - 1]
+            deep = share.shape[0] - width
+            for block in range(chan_parts):
+                start = pl.multiple_of((core ^ swap) * (gain.shape[0] // 2) + block * deep, deep)
+                gains[hops, pl.ds(start, deep), :] = share[
+                    width:, block * width : (block + 1) * width
+                ]
+
+            @pl.when(core ^ swap == 0)
+            def _():
+                place_mixer(hops, share[:width, :], None)
+
+            @pl.when(core ^ swap == 1)
+            def _():
+                place_mixer(hops, None, share[:width, :])
+
+
+def gather(mixer, gain, shares, chan_parts):
+    channels2 = 2 * mixer.shape[2]
+    whole = pl.BlockSpec(memory_space=pltpu.VMEM)
+    return pl.pallas_call(
+        gather_kernel,
+        in_specs=[whole] * (2 + len(shares)),
+        out_specs=[whole] * 2,
+        out_shape=[
+            jax.ShapeDtypeStruct((channels2, channels2), BF16),
+            jax.ShapeDtypeStruct((chan_parts,) + gain.shape, BF16),
+        ],
+        compiler_params=pltpu.CompilerParams(vmem_limit_bytes=16 * 2**20),
+        name="gather",
+    )(mixer, gain, *shares)
+
+
+def spectral_kernel(
+    modes, place, pieces, basis_low, basis_high, mix, gains, out, column, hidden, mixed, kept_low, kept_high
+):
+    pair = pl.program_id(0)
+    pairs = pl.num_programs(0)
+    lat_parts, chan_parts, _, _, _, band, width = pieces.shape
+    lat_count = lat_parts * band
+    channels = chan_parts * width
+    degrees = basis_low.shape[1]
+    block = degrees // 4
+    row, chan = place[0], place[1]
+    from_chan = [(chan + chan_parts - hops) % chan_parts for hops in range(chan_parts)]
 
     begin_mode = chan * 2 * pairs + 2 * pair
     lower = jnp.minimum(modes[begin_mode, row], modes[begin_mode + 1, row])
     higher = jnp.maximum(modes[begin_mode, row], modes[begin_mode + 1, row])
-    for wave, basis in ((lower, basis_low), (higher, basis_high)):
-        parity = wave & 1
-        count = basis.shape[1]
-        first = lat_count - count
+
+    def masked(basis, begin, count, wave):
+        kept = begin + lax.broadcasted_iota(jnp.int32, (count, lat_count), 0) >= wave
+        first = begin - (degrees - basis.shape[1])
+        return jnp.where(kept, basis[0, first : first + count, :], jnp.zeros((), BF16))
+
+    kept_low[...] = masked(basis_low, 0, degrees, lower)
+    kept_high[:block, :] = masked(basis_high, degrees - block, block, higher)
+    kept_high[block:, :] = masked(basis_high, degrees - 2 * block, block, higher)
+
+    def load_column(wave):
         for p in range(2):
             for hops in range(chan_parts):
                 start = p * channels + hops * width
                 column[:, start : start + width] = pieces[
-                    :, from_chan[hops], parity, 0, p
+                    :, from_chan[hops], wave & 1, 0, p
                 ].reshape(lat_count, width)
-        degrees = first + lax.broadcasted_iota(jnp.int32, (count, lat_count), 0)
-        kept = jnp.where(degrees >= wave, basis[0], jnp.zeros((), BF16))
-        rows = 256
-        for begin in range(0, count, rows):
-            part = jnp.dot(kept[begin : begin + rows], column[...], preferred_element_type=F32)
+
+    def analyse(kept, begin, count, target, spans):
+        for p in range(2):
+            part = jnp.dot(
+                kept[begin : begin + count, :],
+                column[:, p * channels : (p + 1) * channels],
+                preferred_element_type=F32,
+            )
             for hops in range(chan_parts):
-                factor = gains[hops, first + begin : first + begin + rows, :].astype(F32)
-                for p in range(2):
-                    start = p * channels + hops * width
-                    hidden[begin : begin + rows, start : start + width] = (
-                        part[:, start : start + width] * factor
+                start = p * channels + hops * width
+                for offset, rows, degree in spans:
+                    factor = gains[hops, degree : degree + rows, :].astype(F32)
+                    hidden[target + offset : target + offset + rows, start : start + width] = (
+                        part[offset : offset + rows, hops * width : (hops + 1) * width] * factor
                     ).astype(BF16)
-        for begin in range(0, count, rows):
-            mixed[begin : begin + rows, :] = jnp.dot(
-                hidden[begin : begin + rows, :], mix[...], preferred_element_type=F32
-            ).astype(BF16)
+
+    wide_low = lower < block
+    load_column(lower)
+
+    @pl.when(wide_low)
+    def _():
+        analyse(kept_low, 0, degrees, 0, [(0, degrees, 0)])
+        mixed[degrees + block :, :] = jnp.zeros((block, 2 * channels), BF16)
+
+    @pl.when(jnp.logical_not(wide_low))
+    def _():
+        analyse(kept_low, block, degrees - block, block, [(0, degrees - block, block)])
+        mixed[:block, :] = jnp.zeros((block, 2 * channels), BF16)
+
+    load_column(higher)
+
+    @pl.when(wide_low)
+    def _():
+        analyse(kept_high, 0, block, degrees, [(0, block, degrees - block)])
+
+    @pl.when(jnp.logical_not(wide_low))
+    def _():
+        analyse(
+            kept_high,
+            0,
+            2 * block,
+            degrees,
+            [(0, block, degrees - block), (block, block, degrees - 2 * block)],
+        )
+
+    rows = pl.ds(pl.multiple_of(jnp.where(wide_low, 0, block), block), degrees + block)
+    for p in range(2):
+        columns = slice(p * channels, (p + 1) * channels)
+        mixed[rows, columns] = jnp.dot(
+            hidden[rows, :], mix[:, columns], preferred_element_type=F32
+        ).astype(BF16)
+
+    for wave, kept, begin in ((lower, kept_low, 0), (higher, kept_high, degrees)):
         for p in range(2):
             for j in range(0, chan_parts, 2):
                 start = p * channels + j * width
                 back = lax.dot_general(
-                    kept,
-                    mixed[:count, start : start + 2 * width],
+                    kept[...],
+                    mixed[begin : begin + kept.shape[0], start : start + 2 * width],
                     (((0,), (0,)), ((), ())),
                     preferred_element_type=F32,
                 ).astype(BF16)
                 for k in range(2):
-                    out[:, j + k, parity, 0, p] = back[:, k * width : (k + 1) * width].reshape(
+                    out[:, j + k, wave & 1, pair, p] = back[:, k * width : (k + 1) * width].reshape(
                         lat_parts, band, width
                     )
 
 
-def spectral(modes, place, pieces, basis, mixer, gain, shares):
+def spectral(modes, place, pieces, basis, mix, gains):
     _, chan_parts, _, pairs, _, _, width = pieces.shape
     degrees, lat_count = basis.shape[1:]
     channels2 = 2 * chan_parts * width
@@ -296,21 +362,20 @@
                 ),
                 whole,
                 whole,
-            ]
-            + [whole] * len(shares),
-            out_specs=one_pair,
+            ],
+            out_specs=whole,
             scratch_shapes=[
-                pltpu.VMEM((channels2, channels2), BF16),
-                pltpu.VMEM((chan_parts,) + gain.shape, BF16),
                 pltpu.VMEM((lat_count, channels2), BF16),
-                pltpu.VMEM((degrees, channels2), BF16),
-                pltpu.VMEM((degrees, channels2), BF16),
+                pltpu.VMEM((degrees + degrees // 2, channels2), BF16),
+                pltpu.VMEM((degrees + degrees // 2, channels2), BF16),
+                pltpu.VMEM((degrees, lat_count), BF16),
+                pltpu.VMEM((degrees // 2, lat_count), BF16),
             ],
         ),
         out_shape=jax.ShapeDtypeStruct(pieces.shape, BF16),
         compiler_params=pltpu.CompilerParams(vmem_limit_bytes=40 * 2**20),
         name="spectral",
-    )(modes, place, pieces, basis, basis, mixer, gain, *shares)
+    )(modes, place, pieces, basis, basis, mix, gains)
 
 
 def local(lat_parts, chan_parts, grid_field, mode_lists, lat_basis, degree_gain, channel_mixer):
@@ -320,7 +385,7 @@
     forward_table = jnp.asarray(forward_table)
     modes = mode_lists.T
     lat_index = lax.axis_index("lat")
-    place = jnp.stack([lat_index, lax.axis_index("chan"), lat_index % 2]).astype(jnp.int32)
+    place = jnp.stack([lat_index, lax.axis_index("chan")]).astype(jnp.int32)
 
     share = carry(channel_mixer, degree_gain)
     shares = [
@@ -332,9 +397,8 @@
     swapped = [lax.ppermute(s, "lat", [(i, i ^ 1) for i in range(lat_parts)]) for s in shares]
     got = lax.all_to_all(sent, ("lat", "chan"), 0, 0, tiled=True)
     got = got.reshape((lat_parts, chan_parts) + got.shape[1:])
-    back = spectral(
-        modes, place, got, lat_basis, channel_mixer, degree_gain, shares + swapped
-    )
+    mix, gains = gather(channel_mixer, degree_gain, shares + swapped, chan_parts)
+    back = spectral(modes, place, got, lat_basis, mix, gains)
     back = back.reshape((devices,) + back.shape[2:])
     returned = lax.all_to_all(back, ("lat", "chan"), 0, 0, tiled=True)
     return inverse(modes, returned, jnp.asarray(back_table))

time: 154 us -> 155 us (level)
  waiting for transfers between devices: 53 us -> 47 us
  local copies, waits for them, and re-layouts: 0.03 us -> 5.8 us
    unnamed x8 -> x24, local copies, waits for them, and re-layouts: 0.03 us -> 5.8 us
    all_to_all x1, waiting for transfers between devices: 49.9 us -> 44.5 us  [local(): got = lax.all_to_all(sent, ('lat', 'chan'), 0, 0, tiled=True)]
  transfers between devices with their start and end apart: 7 -> 7, of which waited for: 5 -> 3; matrix products, arithmetic and copies ran while one was open for 0% -> 0% of each run, Pallas kernels for 6% -> 6%
where the time goes in v5:
time: 155 us; the launch traced here: 154 us
  blocking collectives  56.7 us (37%)
  waiting for transfers between devices  47 us (30%)
  Pallas kernels  29.4 us (19%)
  starting transfers between devices  15.3 us (10%)
  local copies, waits for them, and re-layouts  5.8 us (4%)
    all_to_all x1, blocking collectives, local(): returned = lax.all_to_all(back, ('lat', 'chan'), 0, 0, tiled=True)  56.7 us
    all_to_all x1, waiting for transfers between devices, local(): got = lax.all_to_all(sent, ('lat', 'chan'), 0, 0, tiled=True)  44.5 us
    pallas_call x1, Pallas kernels, spectral(): pl.pallas_call(spectral_kernel, grid_spec=pltpu.PrefetchScalarGridSpec(nu...  10.8 us
    pallas_call x1, Pallas kernels, fourier(): pl.pallas_call(fourier_kernel, grid_spec=pltpu.PrefetchScalarGridSpec(num...  9.41 us
    all_to_all x1, starting transfers between devices, local(): got = lax.all_to_all(sent, ('lat', 'chan'), 0, 0, tiled=True)  8.29 us
    pallas_call x1, Pallas kernels, inverse(): pl.pallas_call(inverse_kernel, grid_spec=pltpu.PrefetchScalarGridSpec(num...  7.29 us
    unnamed x24, local copies, waits for them, and re-layouts  5.8 us
    ppermute x3, starting transfers between devices, local(): lax.ppermute(share, 'chan', [(i, (i + hops) % chan_parts) for i in range(...  5.29 us
  transfers between devices with their start and end apart: 7, of which 3 were waited for; matrix products, arithmetic and copies ran while one was open for 0% of the time, Pallas kernels for 6%

profile of v5, /device:TPU:1, one launch (start us, length us, event | category | flops | bytes accessed | tf_op | source)
XLA Modules:
  0.0 154.3 jit_solution(765993916242284870)
XLA Ops:
  0.0 1.7 %carry.1 = bf16[192,512]{1,0:T(8,128)(2,1)} custom-call(bf16[2,128,512]{2,1,0:T(8,128)(2,1)} %mixer.3, bf16[512,128]{1,0:T(8,128)(2,1)} %gain.3), custom_call_target="tpu_custom_call" | custom-call | tf_op jit(solution)/shard_map/carry/pallas_call | solution.py:174
  1.7 4.6 %collective-permute-start.2 = (bf16[192,512]{1,0:T(8,128)(2,1)}, bf16[192,512]{1,0:T(8,128)(2,1)S(1)}, u32[]{:S(2)}, u32[]{:S(2)}) collective-permute-start(bf16[192,512]{1,0:T(8,128)(2,1)} %carry.1), channel_id=1, source_target_pairs={{0,3},{1,0},{2,1},{3,2},{4,7},{5,4},{6,5},{7,6},{8,11},{9,8},{10,9... | collective-permute-start | bytes 589832 | tf_op jit(solution)/shard_map/ppermute | solution.py:392
  6.3 0.0 collective-permute-start.1
  6.3 0.7 collective-permute-start
  7.0 9.4 %fourier.1 = bf16[128,2,2,2,16,128]{5,4,3,2,1,0:T(8,128)(2,1)} custom-call(s32[16,32]{1,0:T(8,128)} %bitcast.6, bf16[16,1440,128]{2,1,0:T(8,128)(2,1)} %field.1, bf16[2,512,720]{2,1,0:T(8,128)(2,1)} %constant.13.clone.table), custom_call_target="tpu_custom_call" | custom-call | flops 6039797760 | bytes 14286848 | tf_op jit(solution)/shard_map/fourier/pallas_call | solution.py:83
  16.4 0.0 copy-start.1
  16.4 0.0 copy-start.2
  16.4 0.0 copy-start.11
  16.4 0.0 collective-permute-done.2.rest_2_
  16.4 0.0 collective-permute-done.1.rest_1_
  16.4 1.9 %collective-permute-done.rest_0_ = bf16[192,512]{1,0:T(8,128)(2,1)S(1)} collective-permute-done((bf16[192,512]{1,0:T(8,128)(2,1)}, bf16[192,512]{1,0:T(8,128)(2,1)S(1)}, u32[]{:S(2)}, u32[]{:S(2)}) %collective-permute-start) | collective-permute-done | bytes 196640 | tf_op jit(solution)/shard_map/ppermute | solution.py:392
  18.4 8.3 %all-to-all-start = ((bf16[128,2,2,2,16,128]{5,4,3,2,1,0:T(8,128)(2,1)}), bf16[128,2,2,2,16,128]{5,4,3,2,1,0:T(8,128)(2,1)}, u32[]{:S(2)}, u32[]{:S(2)}) async-start(bf16[128,2,2,2,16,128]{5,4,3,2,1,0:T(8,128)(2,1)} %fourier.1), calls=%async_computation | async-start | bytes 8388608 | tf_op jit(solution)/shard_map/all_to_all | solution.py:398
  26.7 1.2 collective-permute-start.3
  27.9 0.1 collective-permute-start.4
  28.0 0.4 collective-permute-start.5
  28.4 0.1 pad_add_fusion.place
  28.5 0.5 collective-permute-done.3.rest_3_
  29.0 0.7 copy-done.5
  29.7 0.0 collective-permute-done.4.rest_4_
  29.7 0.7 copy-done.7
  30.4 0.0 collective-permute-done.5.rest_5_
  30.4 0.7 copy-done.9
  31.1 0.9 copy-done.4
  32.0 0.9 copy-done.6
  32.9 0.9 copy-done.8
  33.8 0.9 copy-done.10
  34.8 0.2 gather.1
  35.0 44.5 %all-to-all-done = bf16[128,2,2,2,16,128]{5,4,3,2,1,0:T(8,128)(2,1)} async-done(((bf16[128,2,2,2,16,128]{5,4,3,2,1,0:T(8,128)(2,1)}), bf16[128,2,2,2,16,128]{5,4,3,2,1,0:T(8,128)(2,1)}, u32[]{:S(2)}, u32[]{:S(2)}) %all-to-all-start) | async-done | bytes 4194336 | tf_op jit(solution)/shard_map/all_to_all | solution.py:398
  79.5 10.8 %spectral.1 = bf16[32,4,2,2,2,16,128]{6,5,4,3,2,1,0:T(8,128)(2,1)S(1)} custom-call(s32[16,32]{1,0:T(8,128)S(1)} %bitcast.7, s32[2]{0:T(128)S(1)} %pad_add_fusion.place, bf16[32,4,2,2,2,16,128]{6,5,4,3,2,1,0:T(8,128)(2,1)} %bitcast.3.pieces, bf16[16,512,512]{2,1,0:T(8,128)(2,1)} %basis_high.1, bf16[16,512,512]{2,1,0:T(8,128)(2,1)} %basis_high.1, ...), custom_call_target="tpu_custom_call" | custom-call | tf_op jit(solution)/shard_map/spectral/pallas_call | solution.py:352
  90.3 0.0 copy-start
  90.3 56.7 %all_to_all.10.pieces = bf16[128,2,2,2,16,128]{5,4,3,2,1,0:T(8,128)(2,1)S(1)} all-to-all(bf16[128,2,2,2,16,128]{5,4,3,2,1,0:T(8,128)(2,1)S(1)} %bitcast.5), channel_id=1, replica_groups=mesh['lat'=32,'chan'=4] {'lat','chan'}, dimensions={0} | all-to-all | bytes 8388608 | tf_op jit(solution)/shard_map/all_to_all | solution.py:403
  147.0 7.3 %inverse_fourier.1 = bf16[16,1440,128]{2,1,0:T(8,128)(2,1)} custom-call(s32[16,32]{1,0:T(8,128)S(1)} %bitcast.8, bf16[128,2,2,2,16,128]{5,4,3,2,1,0:T(8,128)(2,1)S(1)} %all_to_all.10.pieces, bf16[2,720,512]{2,1,0:T(8,128)(2,1)S(1)} %copy-done), custom_call_target="tpu_custom_call" | custom-call | tf_op jit(solution)/shard_map/inverse_fourier/pallas_call | solution.py:143
  (13 shorter events, 0.0 us)
Async XLA Ops:
  1.7 14.7 %collective-permute-start.2 = (bf16[192,512]{1,0:T(8,128)(2,1)}, bf16[192,512]{1,0:T(8,128)(2,1)S(1)}, u32[]{:S(2)}, u32[]{:S(2)}) collective-permute-start(bf16[192,512]{1,0:T(8,128)(2,1)} %carry.1), channel_id=1, source_target_pairs={{0,3},{1,0},{2,1},{3,2},{4,7},{5,4},{6,5},{7,6},{8,11},{9,8},{10,9... | collective-permute-start | bytes 589832 | tf_op jit(solution)/shard_map/ppermute | solution.py:392
  6.3 10.2 %collective-permute-start.1 = (bf16[192,512]{1,0:T(8,128)(2,1)}, bf16[192,512]{1,0:T(8,128)(2,1)S(1)}, u32[]{:S(2)}, u32[]{:S(2)}) collective-permute-start(bf16[192,512]{1,0:T(8,128)(2,1)} %carry.1), channel_id=1, source_target_pairs={{0,2},{1,3},{2,0},{3,1},{4,6},{5,7},{6,4},{7,5},{8,10},{9,11},{10,... | collective-permute-start | bytes 589832 | tf_op jit(solution)/shard_map/ppermute | solution.py:392
  6.3 12.1 %collective-permute-start = (bf16[192,512]{1,0:T(8,128)(2,1)}, bf16[192,512]{1,0:T(8,128)(2,1)S(1)}, u32[]{:S(2)}, u32[]{:S(2)}) collective-permute-start(bf16[192,512]{1,0:T(8,128)(2,1)} %carry.1), channel_id=1, source_target_pairs={{0,1},{1,2},{2,3},{3,0},{4,5},{5,6},{6,7},{7,4},{8,9},{9,10},{10,1... | collective-permute-start | bytes 589832 | tf_op jit(solution)/shard_map/ppermute | solution.py:392
  16.4 14.7 %copy-start.1 = (bf16[2,128,512]{2,1,0:T(8,128)(2,1)S(1)}, bf16[2,128,512]{2,1,0:T(8,128)(2,1)}, u32[]{:S(2)}) copy-start(bf16[2,128,512]{2,1,0:T(8,128)(2,1)} %mixer.3) | copy-start | bytes 786436
  16.4 14.7 %copy-start.2 = (bf16[512,128]{1,0:T(8,128)(2,1)S(1)}, bf16[512,128]{1,0:T(8,128)(2,1)}, u32[]{:S(2)}) copy-start(bf16[512,128]{1,0:T(8,128)(2,1)} %gain.3) | copy-start | bytes 393220
  16.4 63.1 %copy-start.11 = (s32[32,16]{0,1:T(8,128)S(1)}, s32[32,16]{0,1:T(8,128)}, u32[]{:S(2)}) copy-start(s32[32,16]{0,1:T(8,128)} %param.8) | copy-start | bytes 6148
  18.4 8.3 %copy-start.3 = (bf16[192,512]{1,0:T(8,128)(2,1)}, bf16[192,512]{1,0:T(8,128)(2,1)S(1)}, u32[]{:S(2)}) copy-start(bf16[192,512]{1,0:T(8,128)(2,1)S(1)} %collective-permute-done.rest_0_) | copy-start | bytes 589828
  18.4 61.2 %all-to-all-start = ((bf16[128,2,2,2,16,128]{5,4,3,2,1,0:T(8,128)(2,1)}), bf16[128,2,2,2,16,128]{5,4,3,2,1,0:T(8,128)(2,1)}, u32[]{:S(2)}, u32[]{:S(2)}) async-start(bf16[128,2,2,2,16,128]{5,4,3,2,1,0:T(8,128)(2,1)} %fourier.1), calls=%async_computation | async-start | bytes 8388608 | tf_op jit(solution)/shard_map/all_to_all | solution.py:398
  26.7 2.3 %collective-permute-start.3 = (bf16[192,512]{1,0:T(8,128)(2,1)S(1)}, bf16[192,512]{1,0:T(8,128)(2,1)S(1)}, u32[]{:S(2)}, u32[]{:S(2)}) collective-permute-start(bf16[192,512]{1,0:T(8,128)(2,1)S(1)} %collective-permute-done.rest_0_), channel_id=1, source_target_pairs={{0,4},{4,0},{8,12},{12,8},{16,20},{20,16},{24,28},{28,24},{32,36},... | collective-permute-start | bytes 589832 | tf_op jit(solution)/shard_map/ppermute | solution.py:397
  27.9 1.8 %collective-permute-start.4 = (bf16[192,512]{1,0:T(8,128)(2,1)S(1)}, bf16[192,512]{1,0:T(8,128)(2,1)S(1)}, u32[]{:S(2)}, u32[]{:S(2)}) collective-permute-start(bf16[192,512]{1,0:T(8,128)(2,1)S(1)} %collective-permute-done.1.rest_1_), channel_id=1, source_target_pairs={{0,4},{4,0},{8,12},{12,8},{16,20},{20,16},{24,28},{28,24},{32,36},... | collective-permute-start | bytes 589832 | tf_op jit(solution)/shard_map/ppermute | solution.py:397
  28.0 2.4 %collective-permute-start.5 = (bf16[192,512]{1,0:T(8,128)(2,1)S(1)}, bf16[192,512]{1,0:T(8,128)(2,1)S(1)}, u32[]{:S(2)}, u32[]{:S(2)}) collective-permute-start(bf16[192,512]{1,0:T(8,128)(2,1)S(1)} %collective-permute-done.2.rest_2_), channel_id=1, source_target_pairs={{0,4},{4,0},{8,12},{12,8},{16,20},{20,16},{24,28},{28,24},{32,36},... | collective-permute-start | bytes 589832 | tf_op jit(solution)/shard_map/ppermute | solution.py:397
  29.0 0.7 copy-start.5
  29.7 0.7 copy-start.7
  30.4 0.7 copy-start.9
  31.1 0.9 copy-start.4
  32.0 0.9 copy-start.6
  32.9 0.9 copy-start.8
  33.8 0.9 copy-start.10
  90.3 56.7 %copy-start = (bf16[2,720,512]{2,1,0:T(8,128)(2,1)S(1)}, bf16[2,720,512]{2,1,0:T(8,128)(2,1)}, u32[]{:S(2)}) copy-start(bf16[2,720,512]{2,1,0:T(8,128)(2,1)} %constant.14.clone.table) | copy-start | bytes 4423684

commit v6 on v5

--- a/solution.py
+++ b/solution.py
@@ -393,7 +393,6 @@
         for hops in range(1, chan_parts)
     ]
     sent = fourier(modes, grid_field, forward_table, devices, slots)
-    sent, shares = lax.optimization_barrier((sent, shares))
     swapped = [lax.ppermute(s, "lat", [(i, i ^ 1) for i in range(lat_parts)]) for s in shares]
     got = lax.all_to_all(sent, ("lat", "chan"), 0, 0, tiled=True)
     got = got.reshape((lat_parts, chan_parts) + got.shape[1:])

time: 155 us -> 165 us (1.065)
  starting transfers between devices: 15.3 us -> 19.7 us
  blocking collectives: 56.7 us -> 59.8 us
  waiting for transfers between devices: 47 us -> 48.7 us
    ppermute x3, waiting for transfers between devices: 1.94 us -> 48.7 us  [local(): lax.ppermute(share, 'chan', [(i, (i + hops) % chan_parts) for i in range(...]
    all_to_all x1, waiting for transfers between devices: 44.5 us -> 0.01 us  [local(): got = lax.all_to_all(sent, ('lat', 'chan'), 0, 0, tiled=True)]
    all_to_all x1, starting transfers between devices: 8.29 us -> 12 us  [local(): got = lax.all_to_all(sent, ('lat', 'chan'), 0, 0, tiled=True)]
    all_to_all x1, blocking collectives: 56.7 us -> 59.8 us  [local(): returned = lax.all_to_all(back, ('lat', 'chan'), 0, 0, tiled=True)]
  transfers between devices with their start and end apart: 7 -> 7, of which waited for: 3 -> 2; matrix products, arithmetic and copies ran while one was open for 0% -> 0% of each run, Pallas kernels for 6% -> 1%
where the time goes in v6:
time: 165 us; the launch traced here: 164 us
  blocking collectives  59.8 us (36%)
  waiting for transfers between devices  48.7 us (30%)
  Pallas kernels  29.4 us (18%)
  starting transfers between devices  19.7 us (12%)
  local copies, waits for them, and re-layouts  6.47 us (4%)
    all_to_all x1, blocking collectives, local(): returned = lax.all_to_all(back, ('lat', 'chan'), 0, 0, tiled=True)  59.8 us
    ppermute x3, waiting for transfers between devices, local(): lax.ppermute(share, 'chan', [(i, (i + hops) % chan_parts) for i in range(...  48.7 us
    all_to_all x1, starting transfers between devices, local(): got = lax.all_to_all(sent, ('lat', 'chan'), 0, 0, tiled=True)  12 us
    pallas_call x1, Pallas kernels, spectral(): pl.pallas_call(spectral_kernel, grid_spec=pltpu.PrefetchScalarGridSpec(nu...  10.8 us
    pallas_call x1, Pallas kernels, fourier(): pl.pallas_call(fourier_kernel, grid_spec=pltpu.PrefetchScalarGridSpec(num...  9.41 us
    pallas_call x1, Pallas kernels, inverse(): pl.pallas_call(inverse_kernel, grid_spec=pltpu.PrefetchScalarGridSpec(num...  7.29 us
    unnamed x24, local copies, waits for them, and re-layouts  6.47 us
    ppermute x3, starting transfers between devices, local(): lax.ppermute(share, 'chan', [(i, (i + hops) % chan_parts) for i in range(...  5.35 us
  transfers between devices with their start and end apart: 7, of which 2 were waited for; matrix products, arithmetic and copies ran while one was open for 0% of the time, Pallas kernels for 1%

profile of v6, /device:TPU:1, one launch (start us, length us, event | category | flops | bytes accessed | tf_op | source)
XLA Modules:
  0.0 164.3 jit_solution(10980153358692543168)
XLA Ops:
  0.0 9.4 %fourier.1 = bf16[128,2,2,2,16,128]{5,4,3,2,1,0:T(8,128)(2,1)} custom-call(s32[16,32]{1,0:T(8,128)} %bitcast.6, bf16[16,1440,128]{2,1,0:T(8,128)(2,1)} %field.1, bf16[2,512,720]{2,1,0:T(8,128)(2,1)} %constant.13.clone.table), custom_call_target="tpu_custom_call" | custom-call | flops 6039797760 | bytes 14286848 | tf_op jit(solution)/shard_map/fourier/pallas_call | solution.py:83
  9.4 0.0 copy-start.1
  9.4 0.0 copy-start.2
  9.4 0.0 copy-start.11
  9.5 12.0 %all-to-all-start = ((bf16[128,2,2,2,16,128]{5,4,3,2,1,0:T(8,128)(2,1)}), bf16[128,2,2,2,16,128]{5,4,3,2,1,0:T(8,128)(2,1)}, u32[]{:S(2)}, u32[]{:S(2)}) async-start(bf16[128,2,2,2,16,128]{5,4,3,2,1,0:T(8,128)(2,1)} %fourier.1), calls=%async_computation | async-start | bytes 8388608 | tf_op jit(solution)/shard_map/all_to_all | solution.py:397
  21.4 1.7 %carry.1 = bf16[192,512]{1,0:T(8,128)(2,1)} custom-call(bf16[2,128,512]{2,1,0:T(8,128)(2,1)} %mixer.3, bf16[512,128]{1,0:T(8,128)(2,1)} %gain.3), custom_call_target="tpu_custom_call" | custom-call | tf_op jit(solution)/shard_map/carry/pallas_call | solution.py:174
  23.1 1.5 collective-permute-start
  24.6 2.9 %collective-permute-start.1 = (bf16[192,512]{1,0:T(8,128)(2,1)}, bf16[192,512]{1,0:T(8,128)(2,1)S(1)}, u32[]{:S(2)}, u32[]{:S(2)}) collective-permute-start(bf16[192,512]{1,0:T(8,128)(2,1)} %carry.1), channel_id=1, source_target_pairs={{0,2},{1,3},{2,0},{3,1},{4,6},{5,7},{6,4},{7,5},{8,10},{9,11},{10,... | collective-permute-start | bytes 589832 | tf_op jit(solution)/shard_map/ppermute | solution.py:392
  27.5 0.9 collective-permute-start.2
  28.5 44.5 %collective-permute-done.rest_0_ = bf16[192,512]{1,0:T(8,128)(2,1)S(1)} collective-permute-done((bf16[192,512]{1,0:T(8,128)(2,1)}, bf16[192,512]{1,0:T(8,128)(2,1)S(1)}, u32[]{:S(2)}, u32[]{:S(2)}) %collective-permute-start) | collective-permute-done | bytes 196640 | tf_op jit(solution)/shard_map/ppermute | solution.py:392
  73.0 1.2 collective-permute-start.3
  74.1 4.2 %collective-permute-done.1.rest_1_ = bf16[192,512]{1,0:T(8,128)(2,1)S(1)} collective-permute-done((bf16[192,512]{1,0:T(8,128)(2,1)}, bf16[192,512]{1,0:T(8,128)(2,1)S(1)}, u32[]{:S(2)}, u32[]{:S(2)}) %collective-permute-start.1) | collective-permute-done | bytes 196640 | tf_op jit(solution)/shard_map/ppermute | solution.py:392
  78.3 0.7 collective-permute-start.4
  79.0 0.0 collective-permute-done.2.rest_2_
  79.0 0.6 collective-permute-start.5
  79.6 0.7 copy-done.3
  80.2 0.1 pad_add_fusion.place
  80.3 0.0 collective-permute-done.3.rest_3_
  80.3 0.7 copy-done.5
  81.0 0.0 collective-permute-done.4.rest_4_
  81.0 0.7 copy-done.7
  81.7 0.0 collective-permute-done.5.rest_5_
  81.7 0.7 copy-done.9
  82.4 0.9 copy-done.4
  83.3 0.9 copy-done.6
  84.3 0.9 copy-done.8
  85.2 0.9 copy-done.10
  86.1 0.2 gather.1
  86.4 10.8 %spectral.1 = bf16[32,4,2,2,2,16,128]{6,5,4,3,2,1,0:T(8,128)(2,1)S(1)} custom-call(s32[16,32]{1,0:T(8,128)S(1)} %bitcast.7, s32[2]{0:T(128)S(1)} %pad_add_fusion.place, bf16[32,4,2,2,2,16,128]{6,5,4,3,2,1,0:T(8,128)(2,1)} %bitcast.3.pieces, bf16[16,512,512]{2,1,0:T(8,128)(2,1)} %basis_high.1, bf16[16,512,512]{2,1,0:T(8,128)(2,1)} %basis_high.1, ...), custom_call_target="tpu_custom_call" | custom-call | tf_op jit(solution)/shard_map/spectral/pallas_call | solution.py:352
  97.2 0.0 copy-start
  97.2 59.8 %all_to_all.10.pieces = bf16[128,2,2,2,16,128]{5,4,3,2,1,0:T(8,128)(2,1)S(1)} all-to-all(bf16[128,2,2,2,16,128]{5,4,3,2,1,0:T(8,128)(2,1)S(1)} %bitcast.5), channel_id=1, replica_groups=mesh['lat'=32,'chan'=4] {'lat','chan'}, dimensions={0} | all-to-all | bytes 8388608 | tf_op jit(solution)/shard_map/all_to_all | solution.py:402
  157.0 7.3 %inverse_fourier.1 = bf16[16,1440,128]{2,1,0:T(8,128)(2,1)} custom-call(s32[16,32]{1,0:T(8,128)S(1)} %bitcast.8, bf16[128,2,2,2,16,128]{5,4,3,2,1,0:T(8,128)(2,1)S(1)} %all_to_all.10.pieces, bf16[2,720,512]{2,1,0:T(8,128)(2,1)S(1)} %copy-done), custom_call_target="tpu_custom_call" | custom-call | tf_op jit(solution)/shard_map/inverse_fourier/pallas_call | solution.py:143
  (13 shorter events, 0.0 us)
Async XLA Ops:
  9.4 73.0 %copy-start.1 = (bf16[2,128,512]{2,1,0:T(8,128)(2,1)S(1)}, bf16[2,128,512]{2,1,0:T(8,128)(2,1)}, u32[]{:S(2)}) copy-start(bf16[2,128,512]{2,1,0:T(8,128)(2,1)} %mixer.3) | copy-start | bytes 786436
  9.4 73.0 %copy-start.2 = (bf16[512,128]{1,0:T(8,128)(2,1)S(1)}, bf16[512,128]{1,0:T(8,128)(2,1)}, u32[]{:S(2)}) copy-start(bf16[512,128]{1,0:T(8,128)(2,1)} %gain.3) | copy-start | bytes 393220
  9.4 76.9 %copy-start.11 = (s32[32,16]{0,1:T(8,128)S(1)}, s32[32,16]{0,1:T(8,128)}, u32[]{:S(2)}) copy-start(s32[32,16]{0,1:T(8,128)} %param.8) | copy-start | bytes 6148
  9.5 76.9 %all-to-all-start = ((bf16[128,2,2,2,16,128]{5,4,3,2,1,0:T(8,128)(2,1)}), bf16[128,2,2,2,16,128]{5,4,3,2,1,0:T(8,128)(2,1)}, u32[]{:S(2)}, u32[]{:S(2)}) async-start(bf16[128,2,2,2,16,128]{5,4,3,2,1,0:T(8,128)(2,1)} %fourier.1), calls=%async_computation | async-start | bytes 8388608 | tf_op jit(solution)/shard_map/all_to_all | solution.py:397
  23.1 49.8 %collective-permute-start = (bf16[192,512]{1,0:T(8,128)(2,1)}, bf16[192,512]{1,0:T(8,128)(2,1)S(1)}, u32[]{:S(2)}, u32[]{:S(2)}) collective-permute-start(bf16[192,512]{1,0:T(8,128)(2,1)} %carry.1), channel_id=1, source_target_pairs={{0,1},{1,2},{2,3},{3,0},{4,5},{5,6},{6,7},{7,4},{8,9},{9,10},{10,1... | collective-permute-start | bytes 589832 | tf_op jit(solution)/shard_map/ppermute | solution.py:392
  24.6 53.7 %collective-permute-start.1 = (bf16[192,512]{1,0:T(8,128)(2,1)}, bf16[192,512]{1,0:T(8,128)(2,1)S(1)}, u32[]{:S(2)}, u32[]{:S(2)}) collective-permute-start(bf16[192,512]{1,0:T(8,128)(2,1)} %carry.1), channel_id=1, source_target_pairs={{0,2},{1,3},{2,0},{3,1},{4,6},{5,7},{6,4},{7,5},{8,10},{9,11},{10,... | collective-permute-start | bytes 589832 | tf_op jit(solution)/shard_map/ppermute | solution.py:392
  27.5 51.5 %collective-permute-start.2 = (bf16[192,512]{1,0:T(8,128)(2,1)}, bf16[192,512]{1,0:T(8,128)(2,1)S(1)}, u32[]{:S(2)}, u32[]{:S(2)}) collective-permute-start(bf16[192,512]{1,0:T(8,128)(2,1)} %carry.1), channel_id=1, source_target_pairs={{0,3},{1,0},{2,1},{3,2},{4,7},{5,4},{6,5},{7,6},{8,11},{9,8},{10,9... | collective-permute-start | bytes 589832 | tf_op jit(solution)/shard_map/ppermute | solution.py:392
  73.0 7.4 %collective-permute-start.3 = (bf16[192,512]{1,0:T(8,128)(2,1)S(1)}, bf16[192,512]{1,0:T(8,128)(2,1)S(1)}, u32[]{:S(2)}, u32[]{:S(2)}) collective-permute-start(bf16[192,512]{1,0:T(8,128)(2,1)S(1)} %collective-permute-done.rest_0_), channel_id=1, source_target_pairs={{0,4},{4,0},{8,12},{12,8},{16,20},{20,16},{24,28},{28,24},{32,36},... | collective-permute-start | bytes 589832 | tf_op jit(solution)/shard_map/ppermute | solution.py:396
  78.3 2.7 %collective-permute-start.4 = (bf16[192,512]{1,0:T(8,128)(2,1)S(1)}, bf16[192,512]{1,0:T(8,128)(2,1)S(1)}, u32[]{:S(2)}, u32[]{:S(2)}) collective-permute-start(bf16[192,512]{1,0:T(8,128)(2,1)S(1)} %collective-permute-done.1.rest_1_), channel_id=1, source_target_pairs={{0,4},{4,0},{8,12},{12,8},{16,20},{20,16},{24,28},{28,24},{32,36},... | collective-permute-start | bytes 589832 | tf_op jit(solution)/shard_map/ppermute | solution.py:396
  79.0 2.7 %collective-permute-start.5 = (bf16[192,512]{1,0:T(8,128)(2,1)S(1)}, bf16[192,512]{1,0:T(8,128)(2,1)S(1)}, u32[]{:S(2)}, u32[]{:S(2)}) collective-permute-start(bf16[192,512]{1,0:T(8,128)(2,1)S(1)} %collective-permute-done.2.rest_2_), channel_id=1, source_target_pairs={{0,4},{4,0},{8,12},{12,8},{16,20},{20,16},{24,28},{28,24},{32,36},... | collective-permute-start | bytes 589832 | tf_op jit(solution)/shard_map/ppermute | solution.py:396
  79.6 0.7 copy-start.3
  80.3 0.7 copy-start.5
  81.0 0.7 copy-start.7
  81.7 0.7 copy-start.9
  82.4 0.9 copy-start.4
  83.3 0.9 copy-start.6
  84.3 0.9 copy-start.8
  85.2 0.9 copy-start.10
  97.2 59.9 %copy-start = (bf16[2,720,512]{2,1,0:T(8,128)(2,1)S(1)}, bf16[2,720,512]{2,1,0:T(8,128)(2,1)}, u32[]{:S(2)}) copy-start(bf16[2,720,512]{2,1,0:T(8,128)(2,1)} %constant.14.clone.table) | copy-start | bytes 4423684

commit v7 on v5

--- a/solution.py
+++ b/solution.py
@@ -235,7 +235,7 @@
 
 
 def spectral_kernel(
-    modes, place, pieces, basis_low, basis_high, mix, gains, out, column, hidden, mixed, kept_low, kept_high
+    modes, place, pieces, basis_low, basis_high, mix, gains, out, hidden, mixed, kept_low, kept_high
 ):
     pair = pl.program_id(0)
     pairs = pl.num_programs(0)
@@ -260,51 +260,48 @@
     kept_high[:block, :] = masked(basis_high, degrees - block, block, higher)
     kept_high[block:, :] = masked(basis_high, degrees - 2 * block, block, higher)
 
-    def load_column(wave):
+    def analyse(wave, kept, begin, count, target, spans):
         for p in range(2):
-            for hops in range(chan_parts):
-                start = p * channels + hops * width
-                column[:, start : start + width] = pieces[
-                    :, from_chan[hops], wave & 1, 0, p
-                ].reshape(lat_count, width)
-
-    def analyse(kept, begin, count, target, spans):
-        for p in range(2):
-            part = jnp.dot(
-                kept[begin : begin + count, :],
-                column[:, p * channels : (p + 1) * channels],
-                preferred_element_type=F32,
-            )
-            for hops in range(chan_parts):
-                start = p * channels + hops * width
-                for offset, rows, degree in spans:
-                    factor = gains[hops, degree : degree + rows, :].astype(F32)
-                    hidden[target + offset : target + offset + rows, start : start + width] = (
-                        part[offset : offset + rows, hops * width : (hops + 1) * width] * factor
-                    ).astype(BF16)
+            for first_hop in range(0, chan_parts, 2):
+                columns = [
+                    pieces[:, from_chan[first_hop + k], wave & 1, 0, p].reshape(lat_count, width)
+                    for k in range(2)
+                ]
+                part = jnp.dot(
+                    kept[begin : begin + count, :],
+                    jnp.concatenate(columns, axis=1),
+                    preferred_element_type=F32,
+                )
+                for k in range(2):
+                    hops = first_hop + k
+                    start = p * channels + hops * width
+                    for offset, rows, degree in spans:
+                        factor = gains[hops, degree : degree + rows, :].astype(F32)
+                        hidden[target + offset : target + offset + rows, start : start + width] = (
+                            part[offset : offset + rows, k * width : (k + 1) * width] * factor
+                        ).astype(BF16)
 
     wide_low = lower < block
-    load_column(lower)
 
     @pl.when(wide_low)
     def _():
-        analyse(kept_low, 0, degrees, 0, [(0, degrees, 0)])
+        analyse(lower, kept_low, 0, degrees, 0, [(0, degrees, 0)])
         mixed[degrees + block :, :] = jnp.zeros((block, 2 * channels), BF16)
 
     @pl.when(jnp.logical_not(wide_low))
     def _():
-        analyse(kept_low, block, degrees - block, block, [(0, degrees - block, block)])
+        analyse(lower, kept_low, block, degrees - block, block, [(0, degrees - block, block)])
         mixed[:block, :] = jnp.zeros((block, 2 * channels), BF16)
 
-    load_column(higher)
 
     @pl.when(wide_low)
     def _():
-        analyse(kept_high, 0, block, degrees, [(0, block, degrees - block)])
+        analyse(higher, kept_high, 0, block, degrees, [(0, block, degrees - block)])
 
     @pl.when(jnp.logical_not(wide_low))
     def _():
         analyse(
+            higher,
             kept_high,
             0,
             2 * block,
@@ -365,7 +362,6 @@
             ],
             out_specs=whole,
             scratch_shapes=[
-                pltpu.VMEM((lat_count, channels2), BF16),
                 pltpu.VMEM((degrees + degrees // 2, channels2), BF16),
                 pltpu.VMEM((degrees + degrees // 2, channels2), BF16),
                 pltpu.VMEM((degrees, lat_count), BF16),

time: 155 us -> 154 us (level)
  no operation moved by 1% of the time
where the time goes in v7:
time: 154 us; the launch traced here: 153 us
  blocking collectives  56.7 us (37%)
  waiting for transfers between devices  47 us (31%)
  Pallas kernels  28.3 us (18%)
  starting transfers between devices  15.3 us (10%)
  local copies, waits for them, and re-layouts  5.8 us (4%)
    all_to_all x1, blocking collectives, local(): returned = lax.all_to_all(back, ('lat', 'chan'), 0, 0, tiled=True)  56.7 us
    all_to_all x1, waiting for transfers between devices, local(): got = lax.all_to_all(sent, ('lat', 'chan'), 0, 0, tiled=True)  44.5 us
    pallas_call x1, Pallas kernels, spectral(): pl.pallas_call(spectral_kernel, grid_spec=pltpu.PrefetchScalarGridSpec(nu...  9.65 us
    pallas_call x1, Pallas kernels, fourier(): pl.pallas_call(fourier_kernel, grid_spec=pltpu.PrefetchScalarGridSpec(num...  9.41 us
    all_to_all x1, starting transfers between devices, local(): got = lax.all_to_all(sent, ('lat', 'chan'), 0, 0, tiled=True)  8.29 us
    pallas_call x1, Pallas kernels, inverse(): pl.pallas_call(inverse_kernel, grid_spec=pltpu.PrefetchScalarGridSpec(num...  7.29 us
    unnamed x24, local copies, waits for them, and re-layouts  5.8 us
    ppermute x3, starting transfers between devices, local(): lax.ppermute(share, 'chan', [(i, (i + hops) % chan_parts) for i in range(...  5.29 us
  transfers between devices with their start and end apart: 7, of which 3 were waited for; matrix products, arithmetic and copies ran while one was open for 0% of the time, Pallas kernels for 6%

profile of v7, /device:TPU:1, one launch (start us, length us, event | category | flops | bytes accessed | tf_op | source)
XLA Modules:
  0.0 153.1 jit_solution(4061596806124164178)
XLA Ops:
  0.0 1.7 %carry.1 = bf16[192,512]{1,0:T(8,128)(2,1)} custom-call(bf16[2,128,512]{2,1,0:T(8,128)(2,1)} %mixer.3, bf16[512,128]{1,0:T(8,128)(2,1)} %gain.3), custom_call_target="tpu_custom_call" | custom-call | tf_op jit(solution)/shard_map/carry/pallas_call | solution.py:174
  1.7 4.6 %collective-permute-start.2 = (bf16[192,512]{1,0:T(8,128)(2,1)}, bf16[192,512]{1,0:T(8,128)(2,1)S(1)}, u32[]{:S(2)}, u32[]{:S(2)}) collective-permute-start(bf16[192,512]{1,0:T(8,128)(2,1)} %carry.1), channel_id=1, source_target_pairs={{0,3},{1,0},{2,1},{3,2},{4,7},{5,4},{6,5},{7,6},{8,11},{9,8},{10,9... | collective-permute-start | bytes 589832 | tf_op jit(solution)/shard_map/ppermute | solution.py:388
  6.3 0.0 collective-permute-start.1
  6.3 0.7 collective-permute-start
  7.0 9.4 %fourier.1 = bf16[128,2,2,2,16,128]{5,4,3,2,1,0:T(8,128)(2,1)} custom-call(s32[16,32]{1,0:T(8,128)} %bitcast.6, bf16[16,1440,128]{2,1,0:T(8,128)(2,1)} %field.1, bf16[2,512,720]{2,1,0:T(8,128)(2,1)} %constant.13.clone.table), custom_call_target="tpu_custom_call" | custom-call | flops 6039797760 | bytes 14286848 | tf_op jit(solution)/shard_map/fourier/pallas_call | solution.py:83
  16.4 0.0 copy-start.1
  16.4 0.0 copy-start.2
  16.4 0.0 copy-start.11
  16.4 0.0 collective-permute-done.2.rest_2_
  16.4 0.0 collective-permute-done.1.rest_1_
  16.4 1.9 %collective-permute-done.rest_0_ = bf16[192,512]{1,0:T(8,128)(2,1)S(1)} collective-permute-done((bf16[192,512]{1,0:T(8,128)(2,1)}, bf16[192,512]{1,0:T(8,128)(2,1)S(1)}, u32[]{:S(2)}, u32[]{:S(2)}) %collective-permute-start) | collective-permute-done | bytes 196640 | tf_op jit(solution)/shard_map/ppermute | solution.py:388
  18.4 8.3 %all-to-all-start = ((bf16[128,2,2,2,16,128]{5,4,3,2,1,0:T(8,128)(2,1)}), bf16[128,2,2,2,16,128]{5,4,3,2,1,0:T(8,128)(2,1)}, u32[]{:S(2)}, u32[]{:S(2)}) async-start(bf16[128,2,2,2,16,128]{5,4,3,2,1,0:T(8,128)(2,1)} %fourier.1), calls=%async_computation | async-start | bytes 8388608 | tf_op jit(solution)/shard_map/all_to_all | solution.py:394
  26.7 1.2 collective-permute-start.3
  27.9 0.1 collective-permute-start.4
  28.0 0.4 collective-permute-start.5
  28.4 0.1 pad_add_fusion.place
  28.5 0.5 collective-permute-done.3.rest_3_
  29.0 0.7 copy-done.5
  29.7 0.0 collective-permute-done.4.rest_4_
  29.7 0.7 copy-done.7
  30.4 0.0 collective-permute-done.5.rest_5_
  30.4 0.7 copy-done.9
  31.1 0.9 copy-done.4
  32.0 0.9 copy-done.6
  32.9 0.9 copy-done.8
  33.8 0.9 copy-done.10
  34.8 0.2 gather.1
  35.0 44.5 %all-to-all-done = bf16[128,2,2,2,16,128]{5,4,3,2,1,0:T(8,128)(2,1)} async-done(((bf16[128,2,2,2,16,128]{5,4,3,2,1,0:T(8,128)(2,1)}), bf16[128,2,2,2,16,128]{5,4,3,2,1,0:T(8,128)(2,1)}, u32[]{:S(2)}, u32[]{:S(2)}) %all-to-all-start) | async-done | bytes 4194336 | tf_op jit(solution)/shard_map/all_to_all | solution.py:394
  79.5 9.7 %spectral.1 = bf16[32,4,2,2,2,16,128]{6,5,4,3,2,1,0:T(8,128)(2,1)S(1)} custom-call(s32[16,32]{1,0:T(8,128)S(1)} %bitcast.7, s32[2]{0:T(128)S(1)} %pad_add_fusion.place, bf16[32,4,2,2,2,16,128]{6,5,4,3,2,1,0:T(8,128)(2,1)} %bitcast.3.pieces, bf16[16,512,512]{2,1,0:T(8,128)(2,1)} %basis_high.1, bf16[16,512,512]{2,1,0:T(8,128)(2,1)} %basis_high.1, ...), custom_call_target="tpu_custom_call" | custom-call | tf_op jit(solution)/shard_map/spectral/pallas_call | solution.py:349
  89.2 0.0 copy-start
  89.2 56.7 %all_to_all.10.pieces = bf16[128,2,2,2,16,128]{5,4,3,2,1,0:T(8,128)(2,1)S(1)} all-to-all(bf16[128,2,2,2,16,128]{5,4,3,2,1,0:T(8,128)(2,1)S(1)} %bitcast.5), channel_id=1, replica_groups=mesh['lat'=32,'chan'=4] {'lat','chan'}, dimensions={0} | all-to-all | bytes 8388608 | tf_op jit(solution)/shard_map/all_to_all | solution.py:399
  145.9 7.3 %inverse_fourier.1 = bf16[16,1440,128]{2,1,0:T(8,128)(2,1)} custom-call(s32[16,32]{1,0:T(8,128)S(1)} %bitcast.8, bf16[128,2,2,2,16,128]{5,4,3,2,1,0:T(8,128)(2,1)S(1)} %all_to_all.10.pieces, bf16[2,720,512]{2,1,0:T(8,128)(2,1)S(1)} %copy-done), custom_call_target="tpu_custom_call" | custom-call | tf_op jit(solution)/shard_map/inverse_fourier/pallas_call | solution.py:143
  (13 shorter events, 0.0 us)
Async XLA Ops:
  1.7 14.7 %collective-permute-start.2 = (bf16[192,512]{1,0:T(8,128)(2,1)}, bf16[192,512]{1,0:T(8,128)(2,1)S(1)}, u32[]{:S(2)}, u32[]{:S(2)}) collective-permute-start(bf16[192,512]{1,0:T(8,128)(2,1)} %carry.1), channel_id=1, source_target_pairs={{0,3},{1,0},{2,1},{3,2},{4,7},{5,4},{6,5},{7,6},{8,11},{9,8},{10,9... | collective-permute-start | bytes 589832 | tf_op jit(solution)/shard_map/ppermute | solution.py:388
  6.3 10.2 %collective-permute-start.1 = (bf16[192,512]{1,0:T(8,128)(2,1)}, bf16[192,512]{1,0:T(8,128)(2,1)S(1)}, u32[]{:S(2)}, u32[]{:S(2)}) collective-permute-start(bf16[192,512]{1,0:T(8,128)(2,1)} %carry.1), channel_id=1, source_target_pairs={{0,2},{1,3},{2,0},{3,1},{4,6},{5,7},{6,4},{7,5},{8,10},{9,11},{10,... | collective-permute-start | bytes 589832 | tf_op jit(solution)/shard_map/ppermute | solution.py:388
  6.3 12.1 %collective-permute-start = (bf16[192,512]{1,0:T(8,128)(2,1)}, bf16[192,512]{1,0:T(8,128)(2,1)S(1)}, u32[]{:S(2)}, u32[]{:S(2)}) collective-permute-start(bf16[192,512]{1,0:T(8,128)(2,1)} %carry.1), channel_id=1, source_target_pairs={{0,1},{1,2},{2,3},{3,0},{4,5},{5,6},{6,7},{7,4},{8,9},{9,10},{10,1... | collective-permute-start | bytes 589832 | tf_op jit(solution)/shard_map/ppermute | solution.py:388
  16.4 14.7 %copy-start.1 = (bf16[2,128,512]{2,1,0:T(8,128)(2,1)S(1)}, bf16[2,128,512]{2,1,0:T(8,128)(2,1)}, u32[]{:S(2)}) copy-start(bf16[2,128,512]{2,1,0:T(8,128)(2,1)} %mixer.3) | copy-start | bytes 786436
  16.4 14.7 %copy-start.2 = (bf16[512,128]{1,0:T(8,128)(2,1)S(1)}, bf16[512,128]{1,0:T(8,128)(2,1)}, u32[]{:S(2)}) copy-start(bf16[512,128]{1,0:T(8,128)(2,1)} %gain.3) | copy-start | bytes 393220
  16.4 63.1 %copy-start.11 = (s32[32,16]{0,1:T(8,128)S(1)}, s32[32,16]{0,1:T(8,128)}, u32[]{:S(2)}) copy-start(s32[32,16]{0,1:T(8,128)} %param.8) | copy-start | bytes 6148
  18.4 8.3 %copy-start.3 = (bf16[192,512]{1,0:T(8,128)(2,1)}, bf16[192,512]{1,0:T(8,128)(2,1)S(1)}, u32[]{:S(2)}) copy-start(bf16[192,512]{1,0:T(8,128)(2,1)S(1)} %collective-permute-done.rest_0_) | copy-start | bytes 589828
  18.4 61.2 %all-to-all-start = ((bf16[128,2,2,2,16,128]{5,4,3,2,1,0:T(8,128)(2,1)}), bf16[128,2,2,2,16,128]{5,4,3,2,1,0:T(8,128)(2,1)}, u32[]{:S(2)}, u32[]{:S(2)}) async-start(bf16[128,2,2,2,16,128]{5,4,3,2,1,0:T(8,128)(2,1)} %fourier.1), calls=%async_computation | async-start | bytes 8388608 | tf_op jit(solution)/shard_map/all_to_all | solution.py:394
  26.7 2.3 %collective-permute-start.3 = (bf16[192,512]{1,0:T(8,128)(2,1)S(1)}, bf16[192,512]{1,0:T(8,128)(2,1)S(1)}, u32[]{:S(2)}, u32[]{:S(2)}) collective-permute-start(bf16[192,512]{1,0:T(8,128)(2,1)S(1)} %collective-permute-done.rest_0_), channel_id=1, source_target_pairs={{0,4},{4,0},{8,12},{12,8},{16,20},{20,16},{24,28},{28,24},{32,36},... | collective-permute-start | bytes 589832 | tf_op jit(solution)/shard_map/ppermute | solution.py:393
  27.9 1.8 %collective-permute-start.4 = (bf16[192,512]{1,0:T(8,128)(2,1)S(1)}, bf16[192,512]{1,0:T(8,128)(2,1)S(1)}, u32[]{:S(2)}, u32[]{:S(2)}) collective-permute-start(bf16[192,512]{1,0:T(8,128)(2,1)S(1)} %collective-permute-done.1.rest_1_), channel_id=1, source_target_pairs={{0,4},{4,0},{8,12},{12,8},{16,20},{20,16},{24,28},{28,24},{32,36},... | collective-permute-start | bytes 589832 | tf_op jit(solution)/shard_map/ppermute | solution.py:393
  28.0 2.4 %collective-permute-start.5 = (bf16[192,512]{1,0:T(8,128)(2,1)S(1)}, bf16[192,512]{1,0:T(8,128)(2,1)S(1)}, u32[]{:S(2)}, u32[]{:S(2)}) collective-permute-start(bf16[192,512]{1,0:T(8,128)(2,1)S(1)} %collective-permute-done.2.rest_2_), channel_id=1, source_target_pairs={{0,4},{4,0},{8,12},{12,8},{16,20},{20,16},{24,28},{28,24},{32,36},... | collective-permute-start | bytes 589832 | tf_op jit(solution)/shard_map/ppermute | solution.py:393
  29.0 0.7 copy-start.5
  29.7 0.7 copy-start.7
  30.4 0.7 copy-start.9
  31.1 0.9 copy-start.4
  32.0 0.9 copy-start.6
  32.9 0.9 copy-start.8
  33.8 0.9 copy-start.10
  89.2 56.7 %copy-start = (bf16[2,720,512]{2,1,0:T(8,128)(2,1)S(1)}, bf16[2,720,512]{2,1,0:T(8,128)(2,1)}, u32[]{:S(2)}) copy-start(bf16[2,720,512]{2,1,0:T(8,128)(2,1)} %constant.14.clone.table) | copy-start | bytes 4423684

commit v8 on v7

--- a/solution.py
+++ b/solution.py
@@ -12,6 +12,7 @@
 
 BF16 = jnp.bfloat16
 F32 = jnp.float32
+FOURIER_LATS = 8
 LATS = 4
 SPACING = 24
 
@@ -82,17 +83,15 @@
     shape = (devices, 2, slots // 2, 2, band, width)
     return pl.pallas_call(
         fourier_kernel,
-        grid_spec=pltpu.PrefetchScalarGridSpec(
-            num_scalar_prefetch=1,
-            grid=(band // LATS,),
-            in_specs=[
-                pl.BlockSpec((LATS, lon_count, width), lambda i, m: (i, 0, 0)),
-                pl.BlockSpec(table.shape, lambda i, m: (0, 0, 0)),
-            ],
-            out_specs=pl.BlockSpec(memory_space=pl.ANY),
-            scratch_shapes=[pltpu.VMEM((waves * SPACING, width), F32)] * 2
-            + [pltpu.VMEM(shape, BF16), pltpu.SemaphoreType.DMA],
-        ),
+        grid=(band // FOURIER_LATS,),
+        in_specs=[
+            pl.BlockSpec(memory_space=pltpu.SMEM),
+            pl.BlockSpec((FOURIER_LATS, lon_count, width), lambda i: (i, 0, 0)),
+            pl.BlockSpec(table.shape, lambda i: (0, 0, 0)),
+        ],
+        out_specs=pl.BlockSpec(memory_space=pl.ANY),
+        scratch_shapes=[pltpu.VMEM((waves * SPACING, width), F32)] * 2
+        + [pltpu.VMEM(shape, BF16), pltpu.SemaphoreType.DMA],
         out_shape=jax.ShapeDtypeStruct(shape, BF16),
         compiler_params=pltpu.CompilerParams(vmem_limit_bytes=56 * 2**20),
         cost_estimate=pl.CostEstimate(

time: 154 us -> 153 us (level)
  no operation moved by 1% of the time
where the time goes in v8:
time: 153 us
  blocking collectives  56.6 us (37%)
  waiting for transfers between devices  48.1 us (31%)
  Pallas kernels  27.2 us (18%)
  starting transfers between devices  15.2 us (10%)
  local copies, waits for them, and re-layouts  5.8 us (4%)
    all_to_all x1, blocking collectives, local(): returned = lax.all_to_all(back, ('lat', 'chan'), 0, 0, tiled=True)  56.6 us
    all_to_all x1, waiting for transfers between devices, local(): got = lax.all_to_all(sent, ('lat', 'chan'), 0, 0, tiled=True)  44.5 us
    pallas_call x1, Pallas kernels, spectral(): pl.pallas_call(spectral_kernel, grid_spec=pltpu.PrefetchScalarGridSpec(nu...  9.66 us
    pallas_call x1, Pallas kernels, fourier(): pl.pallas_call(fourier_kernel, grid=(band // FOURIER_LATS,), in_specs=[pl...  8.32 us
    all_to_all x1, starting transfers between devices, local(): got = lax.all_to_all(sent, ('lat', 'chan'), 0, 0, tiled=True)  8.15 us
    pallas_call x1, Pallas kernels, inverse(): pl.pallas_call(inverse_kernel, grid_spec=pltpu.PrefetchScalarGridSpec(num...  7.3 us
    unnamed x24, local copies, waits for them, and re-layouts  5.8 us
    ppermute x3, starting transfers between devices, local(): lax.ppermute(share, 'chan', [(i, (i + hops) % chan_parts) for i in range(...  5.29 us
  transfers between devices with their start and end apart: 7, of which 3 were waited for; matrix products, arithmetic and copies ran while one was open for 0% of the time, Pallas kernels for 6%

profile of v8, /device:TPU:1, one launch (start us, length us, event | category | flops | bytes accessed | tf_op | source)
XLA Modules:
  0.0 153.0 jit_solution(8368025934366837203)
XLA Ops:
  0.0 1.7 %carry.1 = bf16[192,512]{1,0:T(8,128)(2,1)} custom-call(bf16[2,128,512]{2,1,0:T(8,128)(2,1)} %mixer.3, bf16[512,128]{1,0:T(8,128)(2,1)} %gain.3), custom_call_target="tpu_custom_call" | custom-call | tf_op jit(solution)/shard_map/carry/pallas_call | solution.py:173
  1.7 4.6 %collective-permute-start.2 = (bf16[192,512]{1,0:T(8,128)(2,1)}, bf16[192,512]{1,0:T(8,128)(2,1)S(1)}, u32[]{:S(2)}, u32[]{:S(2)}) collective-permute-start(bf16[192,512]{1,0:T(8,128)(2,1)} %carry.1), channel_id=1, source_target_pairs={{0,3},{1,0},{2,1},{3,2},{4,7},{5,4},{6,5},{7,6},{8,11},{9,8},{10,9... | collective-permute-start | bytes 589832 | tf_op jit(solution)/shard_map/ppermute | solution.py:387
  6.3 0.0 collective-permute-start.1
  6.3 0.7 collective-permute-start
  7.0 8.3 %fourier.1 = bf16[128,2,2,2,16,128]{5,4,3,2,1,0:T(8,128)(2,1)} custom-call(s32[16,32]{1,0:T(8,128)} %bitcast.6, bf16[16,1440,128]{2,1,0:T(8,128)(2,1)} %field.1, bf16[2,512,720]{2,1,0:T(8,128)(2,1)} %constant.13.clone.table), custom_call_target="tpu_custom_call" | custom-call | flops 6039797760 | bytes 14286848 | tf_op jit(solution)/shard_map/fourier/pallas_call | solution.py:84
  15.3 0.0 copy-start.1
  15.3 0.0 copy-start.2
  15.3 0.0 copy-start.11
  15.3 0.0 collective-permute-done.2.rest_2_
  15.3 0.0 collective-permute-done.1.rest_1_
  15.3 3.0 %collective-permute-done.rest_0_ = bf16[192,512]{1,0:T(8,128)(2,1)S(1)} collective-permute-done((bf16[192,512]{1,0:T(8,128)(2,1)}, bf16[192,512]{1,0:T(8,128)(2,1)S(1)}, u32[]{:S(2)}, u32[]{:S(2)}) %collective-permute-start) | collective-permute-done | bytes 196640 | tf_op jit(solution)/shard_map/ppermute | solution.py:387
  18.4 8.1 %all-to-all-start = ((bf16[128,2,2,2,16,128]{5,4,3,2,1,0:T(8,128)(2,1)}), bf16[128,2,2,2,16,128]{5,4,3,2,1,0:T(8,128)(2,1)}, u32[]{:S(2)}, u32[]{:S(2)}) async-start(bf16[128,2,2,2,16,128]{5,4,3,2,1,0:T(8,128)(2,1)} %fourier.1), calls=%async_computation | async-start | bytes 8388608 | tf_op jit(solution)/shard_map/all_to_all | solution.py:393
  26.5 1.2 collective-permute-start.3
  27.8 0.1 collective-permute-start.4
  27.9 0.4 collective-permute-start.5
  28.3 0.1 pad_add_fusion.place
  28.4 0.5 collective-permute-done.3.rest_3_
  28.8 0.7 copy-done.5
  29.5 0.0 collective-permute-done.4.rest_4_
  29.5 0.7 copy-done.7
  30.2 0.0 collective-permute-done.5.rest_5_
  30.2 0.7 copy-done.9
  30.9 0.9 copy-done.4
  31.8 0.9 copy-done.6
  32.8 0.9 copy-done.8
  33.7 0.9 copy-done.10
  34.6 0.2 gather.1
  34.9 44.5 %all-to-all-done = bf16[128,2,2,2,16,128]{5,4,3,2,1,0:T(8,128)(2,1)} async-done(((bf16[128,2,2,2,16,128]{5,4,3,2,1,0:T(8,128)(2,1)}), bf16[128,2,2,2,16,128]{5,4,3,2,1,0:T(8,128)(2,1)}, u32[]{:S(2)}, u32[]{:S(2)}) %all-to-all-start) | async-done | bytes 4194336 | tf_op jit(solution)/shard_map/all_to_all | solution.py:393
  79.4 9.7 %spectral.1 = bf16[32,4,2,2,2,16,128]{6,5,4,3,2,1,0:T(8,128)(2,1)S(1)} custom-call(s32[16,32]{1,0:T(8,128)S(1)} %bitcast.7, s32[2]{0:T(128)S(1)} %pad_add_fusion.place, bf16[32,4,2,2,2,16,128]{6,5,4,3,2,1,0:T(8,128)(2,1)} %bitcast.3.pieces, bf16[16,512,512]{2,1,0:T(8,128)(2,1)} %basis_high.1, bf16[16,512,512]{2,1,0:T(8,128)(2,1)} %basis_high.1, ...), custom_call_target="tpu_custom_call" | custom-call | tf_op jit(solution)/shard_map/spectral/pallas_call | solution.py:348
  89.1 0.0 copy-start
  89.1 56.6 %all_to_all.10.pieces = bf16[128,2,2,2,16,128]{5,4,3,2,1,0:T(8,128)(2,1)S(1)} all-to-all(bf16[128,2,2,2,16,128]{5,4,3,2,1,0:T(8,128)(2,1)S(1)} %bitcast.5), channel_id=1, replica_groups=mesh['lat'=32,'chan'=4] {'lat','chan'}, dimensions={0} | all-to-all | bytes 8388608 | tf_op jit(solution)/shard_map/all_to_all | solution.py:398
  145.7 7.3 %inverse_fourier.1 = bf16[16,1440,128]{2,1,0:T(8,128)(2,1)} custom-call(s32[16,32]{1,0:T(8,128)S(1)} %bitcast.8, bf16[128,2,2,2,16,128]{5,4,3,2,1,0:T(8,128)(2,1)S(1)} %all_to_all.10.pieces, bf16[2,720,512]{2,1,0:T(8,128)(2,1)S(1)} %copy-done), custom_call_target="tpu_custom_call" | custom-call | tf_op jit(solution)/shard_map/inverse_fourier/pallas_call | solution.py:142
  (13 shorter events, 0.0 us)
Async XLA Ops:
  1.7 13.7 %collective-permute-start.2 = (bf16[192,512]{1,0:T(8,128)(2,1)}, bf16[192,512]{1,0:T(8,128)(2,1)S(1)}, u32[]{:S(2)}, u32[]{:S(2)}) collective-permute-start(bf16[192,512]{1,0:T(8,128)(2,1)} %carry.1), channel_id=1, source_target_pairs={{0,3},{1,0},{2,1},{3,2},{4,7},{5,4},{6,5},{7,6},{8,11},{9,8},{10,9... | collective-permute-start | bytes 589832 | tf_op jit(solution)/shard_map/ppermute | solution.py:387
  6.3 9.1 %collective-permute-start.1 = (bf16[192,512]{1,0:T(8,128)(2,1)}, bf16[192,512]{1,0:T(8,128)(2,1)S(1)}, u32[]{:S(2)}, u32[]{:S(2)}) collective-permute-start(bf16[192,512]{1,0:T(8,128)(2,1)} %carry.1), channel_id=1, source_target_pairs={{0,2},{1,3},{2,0},{3,1},{4,6},{5,7},{6,4},{7,5},{8,10},{9,11},{10,... | collective-permute-start | bytes 589832 | tf_op jit(solution)/shard_map/ppermute | solution.py:387
  6.3 12.1 %collective-permute-start = (bf16[192,512]{1,0:T(8,128)(2,1)}, bf16[192,512]{1,0:T(8,128)(2,1)S(1)}, u32[]{:S(2)}, u32[]{:S(2)}) collective-permute-start(bf16[192,512]{1,0:T(8,128)(2,1)} %carry.1), channel_id=1, source_target_pairs={{0,1},{1,2},{2,3},{3,0},{4,5},{5,6},{6,7},{7,4},{8,9},{9,10},{10,1... | collective-permute-start | bytes 589832 | tf_op jit(solution)/shard_map/ppermute | solution.py:387
  15.3 15.6 %copy-start.1 = (bf16[2,128,512]{2,1,0:T(8,128)(2,1)S(1)}, bf16[2,128,512]{2,1,0:T(8,128)(2,1)}, u32[]{:S(2)}) copy-start(bf16[2,128,512]{2,1,0:T(8,128)(2,1)} %mixer.3) | copy-start | bytes 786436
  15.3 15.6 %copy-start.2 = (bf16[512,128]{1,0:T(8,128)(2,1)S(1)}, bf16[512,128]{1,0:T(8,128)(2,1)}, u32[]{:S(2)}) copy-start(bf16[512,128]{1,0:T(8,128)(2,1)} %gain.3) | copy-start | bytes 393220
  15.3 64.1 %copy-start.11 = (s32[32,16]{0,1:T(8,128)S(1)}, s32[32,16]{0,1:T(8,128)}, u32[]{:S(2)}) copy-start(s32[32,16]{0,1:T(8,128)} %param.8) | copy-start | bytes 6148
  18.4 8.2 %copy-start.3 = (bf16[192,512]{1,0:T(8,128)(2,1)}, bf16[192,512]{1,0:T(8,128)(2,1)S(1)}, u32[]{:S(2)}) copy-start(bf16[192,512]{1,0:T(8,128)(2,1)S(1)} %collective-permute-done.rest_0_) | copy-start | bytes 589828
  18.4 61.0 %all-to-all-start = ((bf16[128,2,2,2,16,128]{5,4,3,2,1,0:T(8,128)(2,1)}), bf16[128,2,2,2,16,128]{5,4,3,2,1,0:T(8,128)(2,1)}, u32[]{:S(2)}, u32[]{:S(2)}) async-start(bf16[128,2,2,2,16,128]{5,4,3,2,1,0:T(8,128)(2,1)} %fourier.1), calls=%async_computation | async-start | bytes 8388608 | tf_op jit(solution)/shard_map/all_to_all | solution.py:393
  26.5 2.3 %collective-permute-start.3 = (bf16[192,512]{1,0:T(8,128)(2,1)S(1)}, bf16[192,512]{1,0:T(8,128)(2,1)S(1)}, u32[]{:S(2)}, u32[]{:S(2)}) collective-permute-start(bf16[192,512]{1,0:T(8,128)(2,1)S(1)} %collective-permute-done.rest_0_), channel_id=1, source_target_pairs={{0,4},{4,0},{8,12},{12,8},{16,20},{20,16},{24,28},{28,24},{32,36},... | collective-permute-start | bytes 589832 | tf_op jit(solution)/shard_map/ppermute | solution.py:392
  27.8 1.8 %collective-permute-start.4 = (bf16[192,512]{1,0:T(8,128)(2,1)S(1)}, bf16[192,512]{1,0:T(8,128)(2,1)S(1)}, u32[]{:S(2)}, u32[]{:S(2)}) collective-permute-start(bf16[192,512]{1,0:T(8,128)(2,1)S(1)} %collective-permute-done.1.rest_1_), channel_id=1, source_target_pairs={{0,4},{4,0},{8,12},{12,8},{16,20},{20,16},{24,28},{28,24},{32,36},... | collective-permute-start | bytes 589832 | tf_op jit(solution)/shard_map/ppermute | solution.py:392
  27.9 2.4 %collective-permute-start.5 = (bf16[192,512]{1,0:T(8,128)(2,1)S(1)}, bf16[192,512]{1,0:T(8,128)(2,1)S(1)}, u32[]{:S(2)}, u32[]{:S(2)}) collective-permute-start(bf16[192,512]{1,0:T(8,128)(2,1)S(1)} %collective-permute-done.2.rest_2_), channel_id=1, source_target_pairs={{0,4},{4,0},{8,12},{12,8},{16,20},{20,16},{24,28},{28,24},{32,36},... | collective-permute-start | bytes 589832 | tf_op jit(solution)/shard_map/ppermute | solution.py:392
  28.8 0.7 copy-start.5
  29.5 0.7 copy-start.7
  30.2 0.7 copy-start.9
  30.9 0.9 copy-start.4
  31.8 0.9 copy-start.6
  32.8 0.9 copy-start.8
  33.7 0.9 copy-start.10
  89.1 56.7 %copy-start = (bf16[2,720,512]{2,1,0:T(8,128)(2,1)S(1)}, bf16[2,720,512]{2,1,0:T(8,128)(2,1)}, u32[]{:S(2)}) copy-start(bf16[2,720,512]{2,1,0:T(8,128)(2,1)} %constant.14.clone.table) | copy-start | bytes 4423684

commit v9 on v8

--- a/solution.py
+++ b/solution.py
@@ -233,15 +233,64 @@
     )(mixer, gain, *shares)
 
 
+def prepare_kernel(modes, place, basis_low, basis_high, kept):
+    row, chan = place[0], place[1]
+    pairs = pl.num_programs(0)
+    degrees, lat_count = basis_low.shape[1:]
+    block = degrees // 4
+    begin_mode = chan * 2 * pairs + 2 * pl.program_id(0)
+    lower = jnp.minimum(modes[begin_mode, row], modes[begin_mode + 1, row])
+    higher = jnp.maximum(modes[begin_mode, row], modes[begin_mode + 1, row])
+
+    def masked(basis, begin, count, wave):
+        keep = begin + lax.broadcasted_iota(jnp.int32, (count, lat_count), 0) >= wave
+        first = begin - (degrees - basis.shape[1])
+        return jnp.where(keep, basis[0, first : first + count, :], jnp.zeros((), BF16))
+
+    kept[0, :degrees, :] = masked(basis_low, 0, degrees, lower)
+    kept[0, degrees : degrees + block, :] = masked(basis_high, degrees - block, block, higher)
+    kept[0, degrees + block :, :] = masked(basis_high, degrees - 2 * block, block, higher)
+
+
+def prepare(modes, place, basis, pairs):
+    degrees, lat_count = basis.shape[1:]
+
+    def basis_slot(which, pair, modes, place):
+        begin = place[1] * 2 * pairs + 2 * pair
+        swapped = (modes[begin, place[0]] > modes[begin + 1, place[0]]).astype(jnp.int32)
+        return begin + (swapped if which == 0 else 1 - swapped)
+
+    low, high = (1, degrees, lat_count), (1, degrees // 2, lat_count)
+    return pl.pallas_call(
+        prepare_kernel,
+        grid_spec=pltpu.PrefetchScalarGridSpec(
+            num_scalar_prefetch=2,
+            grid=(pairs,),
+            in_specs=[
+                pl.BlockSpec(low, lambda i, m, c: (basis_slot(0, i, m, c), 0, 0)),
+                pl.BlockSpec(high, lambda i, m, c: (basis_slot(1, i, m, c), 1, 0)),
+            ],
+            out_specs=pl.BlockSpec(
+                (1, degrees + degrees // 2, lat_count), lambda i, m, c: (i, 0, 0)
+            ),
+        ),
+        out_shape=jax.ShapeDtypeStruct((pairs, degrees + degrees // 2, lat_count), BF16),
+        compiler_params=pltpu.CompilerParams(vmem_limit_bytes=54 * 2**20),
+        name="prepare",
+    )(modes, place, basis, basis)
+
+
 def spectral_kernel(
-    modes, place, pieces, basis_low, basis_high, mix, gains, out, hidden, mixed, kept_low, kept_high
+    modes, place, pieces, kept_block, mix, gains, out, hidden, mixed
 ):
     pair = pl.program_id(0)
     pairs = pl.num_programs(0)
     lat_parts, chan_parts, _, _, _, band, width = pieces.shape
     lat_count = lat_parts * band
     channels = chan_parts * width
-    degrees = basis_low.shape[1]
+    degrees = gains.shape[1]
+    kept_low = kept_block.at[0, pl.ds(0, degrees)]
+    kept_high = kept_block.at[0, pl.ds(degrees, degrees // 2)]
     block = degrees // 4
     row, chan = place[0], place[1]
     from_chan = [(chan + chan_parts - hops) % chan_parts for hops in range(chan_parts)]
@@ -249,15 +298,6 @@
     begin_mode = chan * 2 * pairs + 2 * pair
     lower = jnp.minimum(modes[begin_mode, row], modes[begin_mode + 1, row])
     higher = jnp.maximum(modes[begin_mode, row], modes[begin_mode + 1, row])
-
-    def masked(basis, begin, count, wave):
-        kept = begin + lax.broadcasted_iota(jnp.int32, (count, lat_count), 0) >= wave
-        first = begin - (degrees - basis.shape[1])
-        return jnp.where(kept, basis[0, first : first + count, :], jnp.zeros((), BF16))
-
-    kept_low[...] = masked(basis_low, 0, degrees, lower)
-    kept_high[:block, :] = masked(basis_high, degrees - block, block, higher)
-    kept_high[block:, :] = masked(basis_high, degrees - 2 * block, block, higher)
 
     def analyse(wave, kept, begin, count, target, spans):
         for p in range(2):
@@ -331,46 +371,33 @@
                     )
 
 
-def spectral(modes, place, pieces, basis, mix, gains):
-    _, chan_parts, _, pairs, _, _, width = pieces.shape
-    degrees, lat_count = basis.shape[1:]
-    channels2 = 2 * chan_parts * width
-
-    def basis_slot(which, pair, modes, place):
-        begin = place[1] * 2 * pairs + 2 * pair
-        swapped = (modes[begin, place[0]] > modes[begin + 1, place[0]]).astype(jnp.int32)
-        return begin + (swapped if which == 0 else 1 - swapped)
-
+def spectral(modes, place, pieces, kept, mix, gains):
+    pairs, rows, lat_count = kept.shape
     whole = pl.BlockSpec(memory_space=pltpu.VMEM)
+    scalars = pl.BlockSpec(memory_space=pltpu.SMEM)
     one_pair = pl.BlockSpec(
-        pieces.shape[:3] + (1,) + pieces.shape[4:], lambda i, m, c: (0, 0, 0, i, 0, 0, 0)
+        pieces.shape[:3] + (1,) + pieces.shape[4:], lambda i: (0, 0, 0, i, 0, 0, 0)
     )
     return pl.pallas_call(
         spectral_kernel,
-        grid_spec=pltpu.PrefetchScalarGridSpec(
-            num_scalar_prefetch=2,
-            grid=(pairs,),
-            in_specs=[
-                one_pair,
-                pl.BlockSpec((1, degrees, lat_count), lambda i, m, c: (basis_slot(0, i, m, c), 0, 0)),
-                pl.BlockSpec(
-                    (1, degrees // 2, lat_count), lambda i, m, c: (basis_slot(1, i, m, c), 1, 0)
-                ),
-                whole,
-                whole,
-            ],
-            out_specs=whole,
-            scratch_shapes=[
-                pltpu.VMEM((degrees + degrees // 2, channels2), BF16),
-                pltpu.VMEM((degrees + degrees // 2, channels2), BF16),
-                pltpu.VMEM((degrees, lat_count), BF16),
-                pltpu.VMEM((degrees // 2, lat_count), BF16),
-            ],
-        ),
+        grid=(pairs,),
+        in_specs=[
+            scalars,
+            scalars,
+            one_pair,
+            pl.BlockSpec((1, rows, lat_count), lambda i: (i, 0, 0)),
+            whole,
+            whole,
+        ],
+        out_specs=whole,
+        scratch_shapes=[
+            pltpu.VMEM((rows, mix.shape[0]), BF16),
+            pltpu.VMEM((rows, mix.shape[0]), BF16),
+        ],
         out_shape=jax.ShapeDtypeStruct(pieces.shape, BF16),
         compiler_params=pltpu.CompilerParams(vmem_limit_bytes=40 * 2**20),
         name="spectral",
-    )(modes, place, pieces, basis, basis, mix, gains)
+    )(modes, place, pieces, kept, mix, gains)
 
 
 def local(lat_parts, chan_parts, grid_field, mode_lists, lat_basis, degree_gain, channel_mixer):
@@ -393,7 +420,9 @@
     got = lax.all_to_all(sent, ("lat", "chan"), 0, 0, tiled=True)
     got = got.reshape((lat_parts, chan_parts) + got.shape[1:])
     mix, gains = gather(channel_mixer, degree_gain, shares + swapped, chan_parts)
-    back = spectral(modes, place, got, lat_basis, mix, gains)
+    late_modes, late_place, _ = lax.optimization_barrier((modes, place, swapped))
+    kept = prepare(late_modes, late_place, lat_basis, slots // 2)
+    back = spectral(late_modes, late_place, got, kept, mix, gains)
     back = back.reshape((devices,) + back.shape[2:])
     returned = lax.all_to_all(back, ("lat", "chan"), 0, 0, tiled=True)
     return inverse(modes, returned, jnp.asarray(back_table))

time: 153 us -> 154 us (level)
  Pallas kernels: 27.2 us -> 29.4 us
  local copies, waits for them, and re-layouts: 5.8 us -> 3.73 us
    pallas_call x1 -> x2, Pallas kernels: 9.66 us -> 11.8 us  [the longest x1 8.48 us: spectral(): pl.pallas_call(spectral_kernel, grid=(pairs,), in_specs=[scalars, scalars...]
    unnamed x24 -> x20, local copies, waits for them, and re-layouts: 5.8 us -> 3.73 us
  transfers between devices with their start and end apart: 7 -> 7, of which waited for: 3 -> 3; matrix products, arithmetic and copies ran while one was open for 0% -> 0% of each run, Pallas kernels for 6% -> 8%
where the time goes in v9:
time: 154 us; the launch traced here: 153 us
  blocking collectives  56.7 us (37%)
  waiting for transfers between devices  47.7 us (31%)
  Pallas kernels  29.4 us (19%)
  starting transfers between devices  15.2 us (10%)
  local copies, waits for them, and re-layouts  3.73 us (2%)
    all_to_all x1, blocking collectives, local(): returned = lax.all_to_all(back, ('lat', 'chan'), 0, 0, tiled=True)  56.7 us
    all_to_all x1, waiting for transfers between devices, local(): got = lax.all_to_all(sent, ('lat', 'chan'), 0, 0, tiled=True)  44.3 us
    pallas_call x1, Pallas kernels, spectral(): pl.pallas_call(spectral_kernel, grid=(pairs,), in_specs=[scalars, scalars...  8.48 us
    pallas_call x1, Pallas kernels, fourier(): pl.pallas_call(fourier_kernel, grid=(band // FOURIER_LATS,), in_specs=[pl...  8.32 us
    all_to_all x1, starting transfers between devices, local(): got = lax.all_to_all(sent, ('lat', 'chan'), 0, 0, tiled=True)  8.15 us
    pallas_call x1, Pallas kernels, inverse(): pl.pallas_call(inverse_kernel, grid_spec=pltpu.PrefetchScalarGridSpec(num...  7.29 us
    ppermute x3, starting transfers between devices, local(): lax.ppermute(share, 'chan', [(i, (i + hops) % chan_parts) for i in range(...  5.29 us
    unnamed x20, local copies, waits for them, and re-layouts  3.73 us
  transfers between devices with their start and end apart: 7, of which 3 were waited for; matrix products, arithmetic and copies ran while one was open for 0% of the time, Pallas kernels for 8%

profile of v9, /device:TPU:1, one launch (start us, length us, event | category | flops | bytes accessed | tf_op | source)
XLA Modules:
  0.0 153.3 jit_solution(15583907302107669459)
XLA Ops:
  0.0 1.7 %carry.1 = bf16[192,512]{1,0:T(8,128)(2,1)} custom-call(bf16[2,128,512]{2,1,0:T(8,128)(2,1)} %mixer.3, bf16[512,128]{1,0:T(8,128)(2,1)} %gain.3), custom_call_target="tpu_custom_call" | custom-call | tf_op jit(solution)/shard_map/carry/pallas_call | solution.py:173
  1.7 4.6 %collective-permute-start.2 = (bf16[192,512]{1,0:T(8,128)(2,1)}, bf16[192,512]{1,0:T(8,128)(2,1)S(1)}, u32[]{:S(2)}, u32[]{:S(2)}) collective-permute-start(bf16[192,512]{1,0:T(8,128)(2,1)} %carry.1), channel_id=1, source_target_pairs={{0,3},{1,0},{2,1},{3,2},{4,7},{5,4},{6,5},{7,6},{8,11},{9,8},{10,9... | collective-permute-start | bytes 589832 | tf_op jit(solution)/shard_map/ppermute | solution.py:414
  6.3 0.0 collective-permute-start.1
  6.3 0.7 collective-permute-start
  7.0 8.3 %fourier.1 = bf16[128,2,2,2,16,128]{5,4,3,2,1,0:T(8,128)(2,1)} custom-call(s32[16,32]{1,0:T(8,128)} %bitcast.6, bf16[16,1440,128]{2,1,0:T(8,128)(2,1)} %field.1, bf16[2,512,720]{2,1,0:T(8,128)(2,1)} %constant.13.clone.table), custom_call_target="tpu_custom_call" | custom-call | flops 6039797760 | bytes 14286848 | tf_op jit(solution)/shard_map/fourier/pallas_call | solution.py:84
  15.3 0.0 collective-permute-done.2.rest_2_
  15.3 0.0 collective-permute-done.1.rest_1_
  15.3 3.1 %collective-permute-done.rest_0_ = bf16[192,512]{1,0:T(8,128)(2,1)S(1)} collective-permute-done((bf16[192,512]{1,0:T(8,128)(2,1)}, bf16[192,512]{1,0:T(8,128)(2,1)S(1)}, u32[]{:S(2)}, u32[]{:S(2)}) %collective-permute-start) | collective-permute-done | bytes 196640 | tf_op jit(solution)/shard_map/ppermute | solution.py:414
  18.4 8.1 %all-to-all-start = ((bf16[128,2,2,2,16,128]{5,4,3,2,1,0:T(8,128)(2,1)}), bf16[128,2,2,2,16,128]{5,4,3,2,1,0:T(8,128)(2,1)}, u32[]{:S(2)}, u32[]{:S(2)}) async-start(bf16[128,2,2,2,16,128]{5,4,3,2,1,0:T(8,128)(2,1)} %fourier.1), calls=%async_computation | async-start | bytes 8388608 | tf_op jit(solution)/shard_map/all_to_all | solution.py:420
  26.6 1.2 collective-permute-start.3
  27.8 0.1 collective-permute-start.4
  27.9 0.4 collective-permute-start.5
  28.3 0.6 pad_add_fusion.place
  28.9 0.0 collective-permute-done.3.rest_3_
  28.9 0.3 collective-permute-done.4.rest_4_
  29.2 0.7 copy-done.4
  29.9 0.0 collective-permute-done.5.rest_5_
  29.9 0.7 copy-done.6
  30.6 3.3 %prepare.1.kept_block = bf16[2,768,512]{2,1,0:T(8,128)(2,1)} custom-call(s32[16,32]{1,0:T(8,128)} %bitcast.7, s32[2]{0:T(128)} %pad_add_fusion.place, bf16[16,512,512]{2,1,0:T(8,128)(2,1)} %basis_high.1, bf16[16,512,512]{2,1,0:T(8,128)(2,1)} %basis_high.1), custom_call_target="tpu_custom_call" | custom-call | tf_op jit(solution)/shard_map/prepare/pallas_call | solution.py:264
  33.9 0.0 copy-done.2
  33.9 0.0 copy-done.3
  33.9 0.0 copy-done.5
  34.0 0.0 copy-start.7
  34.0 0.9 copy-done.7
  34.9 0.2 gather.1
  35.1 44.3 %all-to-all-done = bf16[128,2,2,2,16,128]{5,4,3,2,1,0:T(8,128)(2,1)} async-done(((bf16[128,2,2,2,16,128]{5,4,3,2,1,0:T(8,128)(2,1)}), bf16[128,2,2,2,16,128]{5,4,3,2,1,0:T(8,128)(2,1)}, u32[]{:S(2)}, u32[]{:S(2)}) %all-to-all-start) | async-done | bytes 4194336 | tf_op jit(solution)/shard_map/all_to_all | solution.py:420
  79.4 0.0 copy-done.9
  79.4 1.4 copy-done
  80.8 8.5 %spectral.1 = bf16[32,4,2,2,2,16,128]{6,5,4,3,2,1,0:T(8,128)(2,1)S(1)} custom-call(s32[16,32]{1,0:T(8,128)S(1)} %bitcast.8, s32[2]{0:T(128)S(1)} %copy-done.9, bf16[32,4,2,2,2,16,128]{6,5,4,3,2,1,0:T(8,128)(2,1)} %bitcast.3.pieces, bf16[2,768,512]{2,1,0:T(8,128)(2,1)S(1)} %copy-done, bf16[1024,1024]{1,0:T(8,128)(2,1)S(1)} %get-tuple-element.19.mix, ...), custom_call_target="tpu_custom_call" | custom-call | tf_op jit(solution)/shard_map/spectral/pallas_call | solution.py:381
  89.3 0.0 copy-start.1
  89.3 56.7 %all_to_all.10.pieces = bf16[128,2,2,2,16,128]{5,4,3,2,1,0:T(8,128)(2,1)S(1)} all-to-all(bf16[128,2,2,2,16,128]{5,4,3,2,1,0:T(8,128)(2,1)S(1)} %bitcast.5), channel_id=1, replica_groups=mesh['lat'=32,'chan'=4] {'lat','chan'}, dimensions={0} | all-to-all | bytes 8388608 | tf_op jit(solution)/shard_map/all_to_all | solution.py:427
  146.0 7.3 %inverse_fourier.1 = bf16[16,1440,128]{2,1,0:T(8,128)(2,1)} custom-call(s32[16,32]{1,0:T(8,128)S(1)} %bitcast.9, bf16[128,2,2,2,16,128]{5,4,3,2,1,0:T(8,128)(2,1)S(1)} %all_to_all.10.pieces, bf16[2,720,512]{2,1,0:T(8,128)(2,1)S(1)} %copy-done.1), custom_call_target="tpu_custom_call" | custom-call | tf_op jit(solution)/shard_map/inverse_fourier/pallas_call | solution.py:142
  (10 shorter events, 0.0 us)
Async XLA Ops:
  1.7 13.6 %collective-permute-start.2 = (bf16[192,512]{1,0:T(8,128)(2,1)}, bf16[192,512]{1,0:T(8,128)(2,1)S(1)}, u32[]{:S(2)}, u32[]{:S(2)}) collective-permute-start(bf16[192,512]{1,0:T(8,128)(2,1)} %carry.1), channel_id=1, source_target_pairs={{0,3},{1,0},{2,1},{3,2},{4,7},{5,4},{6,5},{7,6},{8,11},{9,8},{10,9... | collective-permute-start | bytes 589832 | tf_op jit(solution)/shard_map/ppermute | solution.py:414
  6.3 9.0 %collective-permute-start.1 = (bf16[192,512]{1,0:T(8,128)(2,1)}, bf16[192,512]{1,0:T(8,128)(2,1)S(1)}, u32[]{:S(2)}, u32[]{:S(2)}) collective-permute-start(bf16[192,512]{1,0:T(8,128)(2,1)} %carry.1), channel_id=1, source_target_pairs={{0,2},{1,3},{2,0},{3,1},{4,6},{5,7},{6,4},{7,5},{8,10},{9,11},{10,... | collective-permute-start | bytes 589832 | tf_op jit(solution)/shard_map/ppermute | solution.py:414
  6.3 12.1 %collective-permute-start = (bf16[192,512]{1,0:T(8,128)(2,1)}, bf16[192,512]{1,0:T(8,128)(2,1)S(1)}, u32[]{:S(2)}, u32[]{:S(2)}) collective-permute-start(bf16[192,512]{1,0:T(8,128)(2,1)} %carry.1), channel_id=1, source_target_pairs={{0,1},{1,2},{2,3},{3,0},{4,5},{5,6},{6,7},{7,4},{8,9},{9,10},{10,1... | collective-permute-start | bytes 589832 | tf_op jit(solution)/shard_map/ppermute | solution.py:414
  18.4 61.0 %all-to-all-start = ((bf16[128,2,2,2,16,128]{5,4,3,2,1,0:T(8,128)(2,1)}), bf16[128,2,2,2,16,128]{5,4,3,2,1,0:T(8,128)(2,1)}, u32[]{:S(2)}, u32[]{:S(2)}) async-start(bf16[128,2,2,2,16,128]{5,4,3,2,1,0:T(8,128)(2,1)} %fourier.1), calls=%async_computation | async-start | bytes 8388608 | tf_op jit(solution)/shard_map/all_to_all | solution.py:420
  26.6 2.3 %collective-permute-start.3 = (bf16[192,512]{1,0:T(8,128)(2,1)S(1)}, bf16[192,512]{1,0:T(8,128)(2,1)S(1)}, u32[]{:S(2)}, u32[]{:S(2)}) collective-permute-start(bf16[192,512]{1,0:T(8,128)(2,1)S(1)} %collective-permute-done.rest_0_), channel_id=1, source_target_pairs={{0,4},{4,0},{8,12},{12,8},{16,20},{20,16},{24,28},{28,24},{32,36},... | collective-permute-start | bytes 589832 | tf_op jit(solution)/shard_map/ppermute | solution.py:419
  27.8 1.4 collective-permute-start.4
  27.9 2.0 %collective-permute-start.5 = (bf16[192,512]{1,0:T(8,128)(2,1)S(1)}, bf16[192,512]{1,0:T(8,128)(2,1)S(1)}, u32[]{:S(2)}, u32[]{:S(2)}) collective-permute-start(bf16[192,512]{1,0:T(8,128)(2,1)S(1)} %collective-permute-done.2.rest_2_), channel_id=1, source_target_pairs={{0,4},{4,0},{8,12},{12,8},{16,20},{20,16},{24,28},{28,24},{32,36},... | collective-permute-start | bytes 589832 | tf_op jit(solution)/shard_map/ppermute | solution.py:419
  28.9 5.1 %copy-start.2 = (bf16[2,128,512]{2,1,0:T(8,128)(2,1)S(1)}, bf16[2,128,512]{2,1,0:T(8,128)(2,1)}, u32[]{:S(2)}) copy-start(bf16[2,128,512]{2,1,0:T(8,128)(2,1)} %mixer.3) | copy-start | bytes 786436
  28.9 5.1 %copy-start.3 = (bf16[512,128]{1,0:T(8,128)(2,1)S(1)}, bf16[512,128]{1,0:T(8,128)(2,1)}, u32[]{:S(2)}) copy-start(bf16[512,128]{1,0:T(8,128)(2,1)} %gain.3) | copy-start | bytes 393220
  28.9 50.5 %copy-start.8 = (s32[32,16]{0,1:T(8,128)S(1)}, s32[32,16]{0,1:T(8,128)}, u32[]{:S(2)}) copy-start(s32[32,16]{0,1:T(8,128)} %param.8) | copy-start | bytes 6148
  28.9 50.5 %copy-start.9 = (s32[2]{0:T(128)S(1)}, s32[2]{0:T(128)}, u32[]{:S(2)}) copy-start(s32[2]{0:T(128)} %pad_add_fusion.place) | copy-start | bytes 28
  29.2 0.7 copy-start.4
  29.9 0.7 copy-start.6
  30.6 3.4 %copy-start.5 = (bf16[192,512]{1,0:T(8,128)(2,1)S(1)}, bf16[192,512]{1,0:T(8,128)(2,1)}, u32[]{:S(2)}) copy-start(bf16[192,512]{1,0:T(8,128)(2,1)} %copy-done.4) | copy-start | bytes 589828
  34.0 0.9 copy-start.7
  79.4 1.4 copy-start
  89.3 56.7 %copy-start.1 = (bf16[2,720,512]{2,1,0:T(8,128)(2,1)S(1)}, bf16[2,720,512]{2,1,0:T(8,128)(2,1)}, u32[]{:S(2)}) copy-start(bf16[2,720,512]{2,1,0:T(8,128)(2,1)} %constant.14.clone.table) | copy-start | bytes 4423684

commit v10 on v9

--- a/solution.py
+++ b/solution.py
@@ -190,11 +190,9 @@
     def place_mixer(hops, real, imag):
         here, below = hops * width, channels + hops * width
         if real is not None:
-            mix[here : here + width, :channels] = real
-            mix[below : below + width, channels:] = real
+            mix[here : here + width, :] = real
         if imag is not None:
-            mix[here : here + width, channels:] = imag
-            mix[below : below + width, :channels] = -imag
+            mix[below : below + width, :] = imag
 
     place_mixer(0, mixer[0], mixer[1])
     gains[0] = gain[...]
@@ -225,7 +223,7 @@
         in_specs=[whole] * (2 + len(shares)),
         out_specs=[whole] * 2,
         out_shape=[
-            jax.ShapeDtypeStruct((channels2, channels2), BF16),
+            jax.ShapeDtypeStruct((channels2, channels2 // 2), BF16),
             jax.ShapeDtypeStruct((chan_parts,) + gain.shape, BF16),
         ],
         compiler_params=pltpu.CompilerParams(vmem_limit_bytes=16 * 2**20),
@@ -275,13 +273,13 @@
             ),
         ),
         out_shape=jax.ShapeDtypeStruct((pairs, degrees + degrees // 2, lat_count), BF16),
-        compiler_params=pltpu.CompilerParams(vmem_limit_bytes=54 * 2**20),
+        compiler_params=pltpu.CompilerParams(vmem_limit_bytes=16 * 2**20),
         name="prepare",
     )(modes, place, basis, basis)
 
 
 def spectral_kernel(
-    modes, place, pieces, kept_block, mix, gains, out, hidden, mixed
+    modes, place, pieces, kept_block, mix, gains, out, for_real, for_imag, mixed
 ):
     pair = pl.program_id(0)
     pairs = pl.num_programs(0)
@@ -313,12 +311,16 @@
                 )
                 for k in range(2):
                     hops = first_hop + k
-                    start = p * channels + hops * width
                     for offset, rows, degree in spans:
                         factor = gains[hops, degree : degree + rows, :].astype(F32)
-                        hidden[target + offset : target + offset + rows, start : start + width] = (
+                        value = (
                             part[offset : offset + rows, k * width : (k + 1) * width] * factor
                         ).astype(BF16)
+                        where = slice(target + offset, target + offset + rows)
+                        first = slice(hops * width, (hops + 1) * width)
+                        second = slice(channels + hops * width, channels + (hops + 1) * width)
+                        for_real[where, first if p == 0 else second] = value if p == 0 else -value
+                        for_imag[where, second if p == 0 else first] = value
 
     wide_low = lower < block
 
@@ -351,8 +353,9 @@
     rows = pl.ds(pl.multiple_of(jnp.where(wide_low, 0, block), block), degrees + block)
     for p in range(2):
         columns = slice(p * channels, (p + 1) * channels)
+        hidden = for_imag if p else for_real
         mixed[rows, columns] = jnp.dot(
-            hidden[rows, :], mix[:, columns], preferred_element_type=F32
+            hidden[rows, :], mix[...], preferred_element_type=F32
         ).astype(BF16)
 
     for wave, kept, begin in ((lower, kept_low, 0), (higher, kept_high, degrees)):
@@ -391,6 +394,7 @@
         ],
         out_specs=whole,
         scratch_shapes=[
+            pltpu.VMEM((rows, mix.shape[0]), BF16),
             pltpu.VMEM((rows, mix.shape[0]), BF16),
             pltpu.VMEM((rows, mix.shape[0]), BF16),
         ],

time: 154 us -> 152 us (0.987)
  local copies, waits for them, and re-layouts: 3.73 us -> 6.67 us
  Pallas kernels: 29.4 us -> 26.6 us
    unnamed x20 -> x26, local copies, waits for them, and re-layouts: 3.73 us -> 6.67 us
    pallas_call x1, Pallas kernels: 3.34 us -> 0.89 us  [prepare(): pl.pallas_call(prepare_kernel, grid_spec=pltpu.PrefetchScalarGridSpec(num...]
  transfers between devices with their start and end apart: 7 -> 7, of which waited for: 3 -> 3; matrix products, arithmetic and copies ran while one was open for 0% -> 0% of each run, Pallas kernels for 8% -> 6%
where the time goes in v10:
time: 152 us
  blocking collectives  56.7 us (37%)
  waiting for transfers between devices  46.3 us (30%)
  Pallas kernels  26.6 us (18%)
  starting transfers between devices  15.2 us (10%)
  local copies, waits for them, and re-layouts  6.67 us (4%)
    all_to_all x1, blocking collectives, local(): returned = lax.all_to_all(back, ('lat', 'chan'), 0, 0, tiled=True)  56.7 us
    all_to_all x1, waiting for transfers between devices, local(): got = lax.all_to_all(sent, ('lat', 'chan'), 0, 0, tiled=True)  42.8 us
    pallas_call x1, Pallas kernels, fourier(): pl.pallas_call(fourier_kernel, grid=(band // FOURIER_LATS,), in_specs=[pl...  8.32 us
    pallas_call x1, Pallas kernels, spectral(): pl.pallas_call(spectral_kernel, grid=(pairs,), in_specs=[scalars, scalars...  8.3 us
    all_to_all x1, starting transfers between devices, local(): got = lax.all_to_all(sent, ('lat', 'chan'), 0, 0, tiled=True)  8.15 us
    pallas_call x1, Pallas kernels, inverse(): pl.pallas_call(inverse_kernel, grid_spec=pltpu.PrefetchScalarGridSpec(num...  7.3 us
    unnamed x26, local copies, waits for them, and re-layouts  6.67 us
    ppermute x3, starting transfers between devices, local(): lax.ppermute(share, 'chan', [(i, (i + hops) % chan_parts) for i in range(...  5.29 us
  transfers between devices with their start and end apart: 7, of which 3 were waited for; matrix products, arithmetic and copies ran while one was open for 0% of the time, Pallas kernels for 6%

profile of v10, /device:TPU:1, one launch (start us, length us, event | category | flops | bytes accessed | tf_op | source)
XLA Modules:
  0.0 151.7 jit_solution(6209965512140807991)
XLA Ops:
  0.0 1.7 %carry.1 = bf16[192,512]{1,0:T(8,128)(2,1)} custom-call(bf16[2,128,512]{2,1,0:T(8,128)(2,1)} %mixer.3, bf16[512,128]{1,0:T(8,128)(2,1)} %gain.3), custom_call_target="tpu_custom_call" | custom-call | tf_op jit(solution)/shard_map/carry/pallas_call | solution.py:173
  1.7 4.6 %collective-permute-start.2 = (bf16[192,512]{1,0:T(8,128)(2,1)}, bf16[192,512]{1,0:T(8,128)(2,1)S(1)}, u32[]{:S(2)}, u32[]{:S(2)}) collective-permute-start(bf16[192,512]{1,0:T(8,128)(2,1)} %carry.1), channel_id=1, source_target_pairs={{0,3},{1,0},{2,1},{3,2},{4,7},{5,4},{6,5},{7,6},{8,11},{9,8},{10,9... | collective-permute-start | bytes 589832 | tf_op jit(solution)/shard_map/ppermute | solution.py:418
  6.3 0.0 collective-permute-start.1
  6.3 0.7 collective-permute-start
  7.0 8.3 %fourier.1 = bf16[128,2,2,2,16,128]{5,4,3,2,1,0:T(8,128)(2,1)} custom-call(s32[16,32]{1,0:T(8,128)} %bitcast.6, bf16[16,1440,128]{2,1,0:T(8,128)(2,1)} %field.1, bf16[2,512,720]{2,1,0:T(8,128)(2,1)} %constant.13.clone.table), custom_call_target="tpu_custom_call" | custom-call | flops 6039797760 | bytes 14286848 | tf_op jit(solution)/shard_map/fourier/pallas_call | solution.py:84
  15.3 0.0 copy-start.12
  15.3 0.0 collective-permute-done.2.rest_2_
  15.3 0.0 collective-permute-done.1.rest_1_
  15.3 3.1 %collective-permute-done.rest_0_ = bf16[192,512]{1,0:T(8,128)(2,1)S(1)} collective-permute-done((bf16[192,512]{1,0:T(8,128)(2,1)}, bf16[192,512]{1,0:T(8,128)(2,1)S(1)}, u32[]{:S(2)}, u32[]{:S(2)}) %collective-permute-start) | collective-permute-done | bytes 196640 | tf_op jit(solution)/shard_map/ppermute | solution.py:418
  18.4 8.1 %all-to-all-start = ((bf16[128,2,2,2,16,128]{5,4,3,2,1,0:T(8,128)(2,1)}), bf16[128,2,2,2,16,128]{5,4,3,2,1,0:T(8,128)(2,1)}, u32[]{:S(2)}, u32[]{:S(2)}) async-start(bf16[128,2,2,2,16,128]{5,4,3,2,1,0:T(8,128)(2,1)} %fourier.1), calls=%async_computation | async-start | bytes 8388608 | tf_op jit(solution)/shard_map/all_to_all | solution.py:424
  26.5 1.2 collective-permute-start.3
  27.8 0.1 collective-permute-start.4
  27.9 0.4 collective-permute-start.5
  28.3 0.1 pad_add_fusion.place
  28.3 0.5 collective-permute-done.3.rest_3_
  28.8 0.7 copy-done.6
  29.5 0.7 copy-done.8
  30.2 0.7 copy-done.10
  30.9 3.4 %copy-done = bf16[16,512,512]{2,1,0:T(8,128)(2,1)S(1)} copy-done((bf16[16,512,512]{2,1,0:T(8,128)(2,1)S(1)}, bf16[16,512,512]{2,1,0:T(8,128)(2,1)}, u32[]{:S(2)}) %copy-start) | copy-done | bytes 8388632
  34.3 0.9 prepare.1.kept_block
  35.2 0.0 copy-done.2
  35.2 0.0 copy-done.3
  35.2 0.1 copy-done.5
  35.3 0.1 copy-done.7
  35.4 0.1 copy-done.9
  35.5 0.9 copy-done.11
  36.4 0.2 gather.1
  36.6 42.8 %all-to-all-done = bf16[128,2,2,2,16,128]{5,4,3,2,1,0:T(8,128)(2,1)} async-done(((bf16[128,2,2,2,16,128]{5,4,3,2,1,0:T(8,128)(2,1)}), bf16[128,2,2,2,16,128]{5,4,3,2,1,0:T(8,128)(2,1)}, u32[]{:S(2)}, u32[]{:S(2)}) %all-to-all-start) | async-done | bytes 4194336 | tf_op jit(solution)/shard_map/all_to_all | solution.py:424
  79.4 8.3 %spectral.1 = bf16[32,4,2,2,2,16,128]{6,5,4,3,2,1,0:T(8,128)(2,1)S(1)} custom-call(s32[16,32]{1,0:T(8,128)S(1)} %bitcast.8, s32[2]{0:T(128)S(1)} %pad_add_fusion.place, bf16[32,4,2,2,2,16,128]{6,5,4,3,2,1,0:T(8,128)(2,1)} %bitcast.3.pieces, bf16[2,768,512]{2,1,0:T(8,128)(2,1)S(1)} %prepare.1.kept_block, bf16[1024,512]{1,0:T(8,128)(2,1)S(1)} %get-tuple-element.19.mix, ...), custom_call_target="tpu_custom_call" | custom-call | tf_op jit(solution)/shard_map/spectral/pallas_call | solution.py:384
  87.7 0.0 copy-start.1
  87.7 56.7 %all_to_all.10.pieces = bf16[128,2,2,2,16,128]{5,4,3,2,1,0:T(8,128)(2,1)S(1)} all-to-all(bf16[128,2,2,2,16,128]{5,4,3,2,1,0:T(8,128)(2,1)S(1)} %bitcast.5), channel_id=1, replica_groups=mesh['lat'=32,'chan'=4] {'lat','chan'}, dimensions={0} | all-to-all | bytes 8388608 | tf_op jit(solution)/shard_map/all_to_all | solution.py:431
  144.4 7.3 %inverse_fourier.1 = bf16[16,1440,128]{2,1,0:T(8,128)(2,1)} custom-call(s32[16,32]{1,0:T(8,128)S(1)} %bitcast.9, bf16[128,2,2,2,16,128]{5,4,3,2,1,0:T(8,128)(2,1)S(1)} %all_to_all.10.pieces, bf16[2,720,512]{2,1,0:T(8,128)(2,1)S(1)} %copy-done.1), custom_call_target="tpu_custom_call" | custom-call | tf_op jit(solution)/shard_map/inverse_fourier/pallas_call | solution.py:142
  (16 shorter events, 0.0 us)
Async XLA Ops:
  1.7 13.6 %collective-permute-start.2 = (bf16[192,512]{1,0:T(8,128)(2,1)}, bf16[192,512]{1,0:T(8,128)(2,1)S(1)}, u32[]{:S(2)}, u32[]{:S(2)}) collective-permute-start(bf16[192,512]{1,0:T(8,128)(2,1)} %carry.1), channel_id=1, source_target_pairs={{0,3},{1,0},{2,1},{3,2},{4,7},{5,4},{6,5},{7,6},{8,11},{9,8},{10,9... | collective-permute-start | bytes 589832 | tf_op jit(solution)/shard_map/ppermute | solution.py:418
  6.3 9.1 %collective-permute-start.1 = (bf16[192,512]{1,0:T(8,128)(2,1)}, bf16[192,512]{1,0:T(8,128)(2,1)S(1)}, u32[]{:S(2)}, u32[]{:S(2)}) collective-permute-start(bf16[192,512]{1,0:T(8,128)(2,1)} %carry.1), channel_id=1, source_target_pairs={{0,2},{1,3},{2,0},{3,1},{4,6},{5,7},{6,4},{7,5},{8,10},{9,11},{10,... | collective-permute-start | bytes 589832 | tf_op jit(solution)/shard_map/ppermute | solution.py:418
  6.3 12.1 %collective-permute-start = (bf16[192,512]{1,0:T(8,128)(2,1)}, bf16[192,512]{1,0:T(8,128)(2,1)S(1)}, u32[]{:S(2)}, u32[]{:S(2)}) collective-permute-start(bf16[192,512]{1,0:T(8,128)(2,1)} %carry.1), channel_id=1, source_target_pairs={{0,1},{1,2},{2,3},{3,0},{4,5},{5,6},{6,7},{7,4},{8,9},{9,10},{10,1... | collective-permute-start | bytes 589832 | tf_op jit(solution)/shard_map/ppermute | solution.py:418
  15.3 15.6 %copy-start.12 = (s32[32,16]{0,1:T(8,128)S(1)}, s32[32,16]{0,1:T(8,128)}, u32[]{:S(2)}) copy-start(s32[32,16]{0,1:T(8,128)} %param.8) | copy-start | bytes 6148
  18.4 8.2 %copy-start.4 = (bf16[192,512]{1,0:T(8,128)(2,1)}, bf16[192,512]{1,0:T(8,128)(2,1)S(1)}, u32[]{:S(2)}) copy-start(bf16[192,512]{1,0:T(8,128)(2,1)S(1)} %collective-permute-done.rest_0_) | copy-start | bytes 589828
  18.4 61.0 %all-to-all-start = ((bf16[128,2,2,2,16,128]{5,4,3,2,1,0:T(8,128)(2,1)}), bf16[128,2,2,2,16,128]{5,4,3,2,1,0:T(8,128)(2,1)}, u32[]{:S(2)}, u32[]{:S(2)}) async-start(bf16[128,2,2,2,16,128]{5,4,3,2,1,0:T(8,128)(2,1)} %fourier.1), calls=%async_computation | async-start | bytes 8388608 | tf_op jit(solution)/shard_map/all_to_all | solution.py:424
  26.5 2.3 %collective-permute-start.3 = (bf16[192,512]{1,0:T(8,128)(2,1)S(1)}, bf16[192,512]{1,0:T(8,128)(2,1)S(1)}, u32[]{:S(2)}, u32[]{:S(2)}) collective-permute-start(bf16[192,512]{1,0:T(8,128)(2,1)S(1)} %collective-permute-done.rest_0_), channel_id=1, source_target_pairs={{0,4},{4,0},{8,12},{12,8},{16,20},{20,16},{24,28},{28,24},{32,36},... | collective-permute-start | bytes 589832 | tf_op jit(solution)/shard_map/ppermute | solution.py:423
  27.8 1.7 %collective-permute-start.4 = (bf16[192,512]{1,0:T(8,128)(2,1)S(1)}, bf16[192,512]{1,0:T(8,128)(2,1)S(1)}, u32[]{:S(2)}, u32[]{:S(2)}) collective-permute-start(bf16[192,512]{1,0:T(8,128)(2,1)S(1)} %collective-permute-done.1.rest_1_), channel_id=1, source_target_pairs={{0,4},{4,0},{8,12},{12,8},{16,20},{20,16},{24,28},{28,24},{32,36},... | collective-permute-start | bytes 589832 | tf_op jit(solution)/shard_map/ppermute | solution.py:423
  27.9 2.3 %collective-permute-start.5 = (bf16[192,512]{1,0:T(8,128)(2,1)S(1)}, bf16[192,512]{1,0:T(8,128)(2,1)S(1)}, u32[]{:S(2)}, u32[]{:S(2)}) collective-permute-start(bf16[192,512]{1,0:T(8,128)(2,1)S(1)} %collective-permute-done.2.rest_2_), channel_id=1, source_target_pairs={{0,4},{4,0},{8,12},{12,8},{16,20},{20,16},{24,28},{28,24},{32,36},... | collective-permute-start | bytes 589832 | tf_op jit(solution)/shard_map/ppermute | solution.py:423
  28.8 0.7 copy-start.6
  29.5 0.7 copy-start.8
  30.2 0.7 copy-start.10
  30.9 3.4 %copy-start = (bf16[16,512,512]{2,1,0:T(8,128)(2,1)S(1)}, bf16[16,512,512]{2,1,0:T(8,128)(2,1)}, u32[]{:S(2)}) copy-start(bf16[16,512,512]{2,1,0:T(8,128)(2,1)} %basis_high.1) | copy-start | bytes 25165828
  34.3 0.9 copy-start.2
  34.3 1.0 copy-start.3
  34.3 1.1 copy-start.5
  34.3 1.2 copy-start.7
  34.3 1.2 copy-start.9
  35.5 0.9 copy-start.11
  87.7 56.7 %copy-start.1 = (bf16[2,720,512]{2,1,0:T(8,128)(2,1)S(1)}, bf16[2,720,512]{2,1,0:T(8,128)(2,1)}, u32[]{:S(2)}) copy-start(bf16[2,720,512]{2,1,0:T(8,128)(2,1)} %constant.14.clone.table) | copy-start | bytes 4423684

commit v11 on v10

--- a/solution.py
+++ b/solution.py
@@ -157,6 +157,10 @@
     )(modes, pieces, table)
 
 
+def hop_order(chan_parts):
+    return sorted(range(1, chan_parts), key=lambda hops: min(hops, chan_parts - hops))
+
+
 def carry_kernel(mixer, gain, out):
     core = lax.axis_index("lat") & 1
     rows, width = mixer.shape[1], gain.shape[1]
@@ -196,9 +200,9 @@
 
     place_mixer(0, mixer[0], mixer[1])
     gains[0] = gain[...]
-    for hops in range(1, chan_parts):
+    for index, hops in enumerate(hop_order(chan_parts)):
         for swap in range(2):
-            share = shares[swap][hops - 1]
+            share = shares[swap][index]
             deep = share.shape[0] - width
             for block in range(chan_parts):
                 start = pl.multiple_of((core ^ swap) * (gain.shape[0] // 2) + block * deep, deep)
@@ -416,7 +420,7 @@
     share = carry(channel_mixer, degree_gain)
     shares = [
         lax.ppermute(share, "chan", [(i, (i + hops) % chan_parts) for i in range(chan_parts)])
-        for hops in range(1, chan_parts)
+        for hops in hop_order(chan_parts)
     ]
     sent = fourier(modes, grid_field, forward_table, devices, slots)
     sent, shares = lax.optimization_barrier((sent, shares))

time: 152 us -> 152 us (level)
  waiting for transfers between devices: 46.3 us -> 43.3 us
  starting transfers between devices: 15.2 us -> 17.9 us
    ppermute x3, waiting for transfers between devices: 3.06 us -> 0.01 us  [local(): lax.ppermute(share, 'chan', [(i, (i + hops) % chan_parts) for i in range(...]
    all_to_all x1, starting transfers between devices: 8.15 us -> 10.2 us  [local(): got = lax.all_to_all(sent, ('lat', 'chan'), 0, 0, tiled=True)]
  transfers between devices with their start and end apart: 7 -> 7, of which waited for: 3 -> 2; matrix products, arithmetic and copies ran while one was open for 0% -> 0% of each run, Pallas kernels for 6% -> 6%
where the time goes in v11:
time: 152 us; the launch traced here: 151 us
  blocking collectives  56.7 us (37%)
  waiting for transfers between devices  43.3 us (28%)
  Pallas kernels  26.7 us (18%)
  starting transfers between devices  17.9 us (12%)
  local copies, waits for them, and re-layouts  6.67 us (4%)
    all_to_all x1, blocking collectives, local(): returned = lax.all_to_all(back, ('lat', 'chan'), 0, 0, tiled=True)  56.7 us
    all_to_all x1, waiting for transfers between devices, local(): got = lax.all_to_all(sent, ('lat', 'chan'), 0, 0, tiled=True)  42.8 us
    all_to_all x1, starting transfers between devices, local(): got = lax.all_to_all(sent, ('lat', 'chan'), 0, 0, tiled=True)  10.2 us
    pallas_call x1, Pallas kernels, fourier(): pl.pallas_call(fourier_kernel, grid=(band // FOURIER_LATS,), in_specs=[pl...  8.33 us
    pallas_call x1, Pallas kernels, spectral(): pl.pallas_call(spectral_kernel, grid=(pairs,), in_specs=[scalars, scalars...  8.31 us
    pallas_call x1, Pallas kernels, inverse(): pl.pallas_call(inverse_kernel, grid_spec=pltpu.PrefetchScalarGridSpec(num...  7.3 us
    unnamed x26, local copies, waits for them, and re-layouts  6.67 us
    ppermute x3, starting transfers between devices, local(): lax.ppermute(share, 'chan', [(i, (i + hops) % chan_parts) for i in range(...  5.89 us
  transfers between devices with their start and end apart: 7, of which 2 were waited for; matrix products, arithmetic and copies ran while one was open for 0% of the time, Pallas kernels for 6%

profile of v11, /device:TPU:1, one launch (start us, length us, event | category | flops | bytes accessed | tf_op | source)
XLA Modules:
  0.0 151.3 jit_solution(13272696024666484872)
XLA Ops:
  0.0 1.7 %carry.1 = bf16[192,512]{1,0:T(8,128)(2,1)} custom-call(bf16[2,128,512]{2,1,0:T(8,128)(2,1)} %mixer.3, bf16[512,128]{1,0:T(8,128)(2,1)} %gain.3), custom_call_target="tpu_custom_call" | custom-call | tf_op jit(solution)/shard_map/carry/pallas_call | solution.py:177
  1.7 4.4 %collective-permute-start.2 = (bf16[192,512]{1,0:T(8,128)(2,1)}, bf16[192,512]{1,0:T(8,128)(2,1)S(1)}, u32[]{:S(2)}, u32[]{:S(2)}) collective-permute-start(bf16[192,512]{1,0:T(8,128)(2,1)} %carry.1), channel_id=1, source_target_pairs={{0,2},{1,3},{2,0},{3,1},{4,6},{5,7},{6,4},{7,5},{8,10},{9,11},{10,... | collective-permute-start | bytes 589832 | tf_op jit(solution)/shard_map/ppermute | solution.py:422
  6.1 0.4 collective-permute-start.1
  6.5 1.0 collective-permute-start
  7.6 8.3 %fourier.1 = bf16[128,2,2,2,16,128]{5,4,3,2,1,0:T(8,128)(2,1)} custom-call(s32[16,32]{1,0:T(8,128)} %bitcast.6, bf16[16,1440,128]{2,1,0:T(8,128)(2,1)} %field.1, bf16[2,512,720]{2,1,0:T(8,128)(2,1)} %constant.13.clone.table), custom_call_target="tpu_custom_call" | custom-call | flops 6039797760 | bytes 14286848 | tf_op jit(solution)/shard_map/fourier/pallas_call | solution.py:84
  15.9 0.0 copy-start.12
  15.9 0.0 collective-permute-done.2.rest_2_
  15.9 0.0 collective-permute-done.1.rest_1_
  15.9 10.2 %all-to-all-start = ((bf16[128,2,2,2,16,128]{5,4,3,2,1,0:T(8,128)(2,1)}), bf16[128,2,2,2,16,128]{5,4,3,2,1,0:T(8,128)(2,1)}, u32[]{:S(2)}, u32[]{:S(2)}) async-start(bf16[128,2,2,2,16,128]{5,4,3,2,1,0:T(8,128)(2,1)} %fourier.1), calls=%async_computation | async-start | bytes 8388608 | tf_op jit(solution)/shard_map/all_to_all | solution.py:428
  26.2 1.2 collective-permute-start.3
  27.4 0.1 collective-permute-start.4
  27.5 0.4 collective-permute-start.5
  27.9 0.1 pad_add_fusion.place
  28.0 0.5 collective-permute-done.3.rest_3_
  28.5 0.7 copy-done.6
  29.2 0.7 copy-done.8
  29.8 0.0 collective-permute-done.5.rest_5_
  29.8 0.7 copy-done.10
  30.5 3.4 %copy-done = bf16[16,512,512]{2,1,0:T(8,128)(2,1)S(1)} copy-done((bf16[16,512,512]{2,1,0:T(8,128)(2,1)S(1)}, bf16[16,512,512]{2,1,0:T(8,128)(2,1)}, u32[]{:S(2)}) %copy-start) | copy-done | bytes 8388632
  33.9 0.9 prepare.1.kept_block
  34.8 0.0 copy-done.2
  34.9 0.0 copy-done.3
  34.9 0.1 copy-done.5
  35.0 0.1 copy-done.7
  35.1 0.1 copy-done.9
  35.1 0.9 copy-done.11
  36.1 0.2 gather.1
  36.2 42.8 %all-to-all-done = bf16[128,2,2,2,16,128]{5,4,3,2,1,0:T(8,128)(2,1)} async-done(((bf16[128,2,2,2,16,128]{5,4,3,2,1,0:T(8,128)(2,1)}), bf16[128,2,2,2,16,128]{5,4,3,2,1,0:T(8,128)(2,1)}, u32[]{:S(2)}, u32[]{:S(2)}) %all-to-all-start) | async-done | bytes 4194336 | tf_op jit(solution)/shard_map/all_to_all | solution.py:428
  79.0 8.3 %spectral.1 = bf16[32,4,2,2,2,16,128]{6,5,4,3,2,1,0:T(8,128)(2,1)S(1)} custom-call(s32[16,32]{1,0:T(8,128)S(1)} %bitcast.8, s32[2]{0:T(128)S(1)} %pad_add_fusion.place, bf16[32,4,2,2,2,16,128]{6,5,4,3,2,1,0:T(8,128)(2,1)} %bitcast.3.pieces, bf16[2,768,512]{2,1,0:T(8,128)(2,1)S(1)} %prepare.1.kept_block, bf16[1024,512]{1,0:T(8,128)(2,1)S(1)} %get-tuple-element.19.mix, ...), custom_call_target="tpu_custom_call" | custom-call | tf_op jit(solution)/shard_map/spectral/pallas_call | solution.py:388
  87.4 0.0 copy-start.1
  87.4 56.7 %all_to_all.10.pieces = bf16[128,2,2,2,16,128]{5,4,3,2,1,0:T(8,128)(2,1)S(1)} all-to-all(bf16[128,2,2,2,16,128]{5,4,3,2,1,0:T(8,128)(2,1)S(1)} %bitcast.5), channel_id=1, replica_groups=mesh['lat'=32,'chan'=4] {'lat','chan'}, dimensions={0} | all-to-all | bytes 8388608 | tf_op jit(solution)/shard_map/all_to_all | solution.py:435
  144.0 7.3 %inverse_fourier.1 = bf16[16,1440,128]{2,1,0:T(8,128)(2,1)} custom-call(s32[16,32]{1,0:T(8,128)S(1)} %bitcast.9, bf16[128,2,2,2,16,128]{5,4,3,2,1,0:T(8,128)(2,1)S(1)} %all_to_all.10.pieces, bf16[2,720,512]{2,1,0:T(8,128)(2,1)S(1)} %copy-done.1), custom_call_target="tpu_custom_call" | custom-call | tf_op jit(solution)/shard_map/inverse_fourier/pallas_call | solution.py:142
  (16 shorter events, 0.0 us)
Async XLA Ops:
  1.7 14.2 %collective-permute-start.2 = (bf16[192,512]{1,0:T(8,128)(2,1)}, bf16[192,512]{1,0:T(8,128)(2,1)S(1)}, u32[]{:S(2)}, u32[]{:S(2)}) collective-permute-start(bf16[192,512]{1,0:T(8,128)(2,1)} %carry.1), channel_id=1, source_target_pairs={{0,2},{1,3},{2,0},{3,1},{4,6},{5,7},{6,4},{7,5},{8,10},{9,11},{10,... | collective-permute-start | bytes 589832 | tf_op jit(solution)/shard_map/ppermute | solution.py:422
  6.1 9.8 %collective-permute-start.1 = (bf16[192,512]{1,0:T(8,128)(2,1)}, bf16[192,512]{1,0:T(8,128)(2,1)S(1)}, u32[]{:S(2)}, u32[]{:S(2)}) collective-permute-start(bf16[192,512]{1,0:T(8,128)(2,1)} %carry.1), channel_id=1, source_target_pairs={{0,3},{1,0},{2,1},{3,2},{4,7},{5,4},{6,5},{7,6},{8,11},{9,8},{10,9... | collective-permute-start | bytes 589832 | tf_op jit(solution)/shard_map/ppermute | solution.py:422
  6.5 9.4 %collective-permute-start = (bf16[192,512]{1,0:T(8,128)(2,1)}, bf16[192,512]{1,0:T(8,128)(2,1)S(1)}, u32[]{:S(2)}, u32[]{:S(2)}) collective-permute-start(bf16[192,512]{1,0:T(8,128)(2,1)} %carry.1), channel_id=1, source_target_pairs={{0,1},{1,2},{2,3},{3,0},{4,5},{5,6},{6,7},{7,4},{8,9},{9,10},{10,1... | collective-permute-start | bytes 589832 | tf_op jit(solution)/shard_map/ppermute | solution.py:422
  15.9 14.6 %copy-start.12 = (s32[32,16]{0,1:T(8,128)S(1)}, s32[32,16]{0,1:T(8,128)}, u32[]{:S(2)}) copy-start(s32[32,16]{0,1:T(8,128)} %param.8) | copy-start | bytes 6148
  15.9 10.3 %copy-start.4 = (bf16[192,512]{1,0:T(8,128)(2,1)}, bf16[192,512]{1,0:T(8,128)(2,1)S(1)}, u32[]{:S(2)}) copy-start(bf16[192,512]{1,0:T(8,128)(2,1)S(1)} %collective-permute-done.rest_0_) | copy-start | bytes 589828
  15.9 63.1 %all-to-all-start = ((bf16[128,2,2,2,16,128]{5,4,3,2,1,0:T(8,128)(2,1)}), bf16[128,2,2,2,16,128]{5,4,3,2,1,0:T(8,128)(2,1)}, u32[]{:S(2)}, u32[]{:S(2)}) async-start(bf16[128,2,2,2,16,128]{5,4,3,2,1,0:T(8,128)(2,1)} %fourier.1), calls=%async_computation | async-start | bytes 8388608 | tf_op jit(solution)/shard_map/all_to_all | solution.py:428
  26.2 2.3 %collective-permute-start.3 = (bf16[192,512]{1,0:T(8,128)(2,1)S(1)}, bf16[192,512]{1,0:T(8,128)(2,1)S(1)}, u32[]{:S(2)}, u32[]{:S(2)}) collective-permute-start(bf16[192,512]{1,0:T(8,128)(2,1)S(1)} %collective-permute-done.rest_0_), channel_id=1, source_target_pairs={{0,4},{4,0},{8,12},{12,8},{16,20},{20,16},{24,28},{28,24},{32,36},... | collective-permute-start | bytes 589832 | tf_op jit(solution)/shard_map/ppermute | solution.py:427
  27.4 1.7 %collective-permute-start.4 = (bf16[192,512]{1,0:T(8,128)(2,1)S(1)}, bf16[192,512]{1,0:T(8,128)(2,1)S(1)}, u32[]{:S(2)}, u32[]{:S(2)}) collective-permute-start(bf16[192,512]{1,0:T(8,128)(2,1)S(1)} %collective-permute-done.1.rest_1_), channel_id=1, source_target_pairs={{0,4},{4,0},{8,12},{12,8},{16,20},{20,16},{24,28},{28,24},{32,36},... | collective-permute-start | bytes 589832 | tf_op jit(solution)/shard_map/ppermute | solution.py:427
  27.5 2.3 %collective-permute-start.5 = (bf16[192,512]{1,0:T(8,128)(2,1)S(1)}, bf16[192,512]{1,0:T(8,128)(2,1)S(1)}, u32[]{:S(2)}, u32[]{:S(2)}) collective-permute-start(bf16[192,512]{1,0:T(8,128)(2,1)S(1)} %collective-permute-done.2.rest_2_), channel_id=1, source_target_pairs={{0,4},{4,0},{8,12},{12,8},{16,20},{20,16},{24,28},{28,24},{32,36},... | collective-permute-start | bytes 589832 | tf_op jit(solution)/shard_map/ppermute | solution.py:427
  28.5 0.7 copy-start.6
  29.2 0.7 copy-start.8
  29.8 0.7 copy-start.10
  30.5 3.4 %copy-start = (bf16[16,512,512]{2,1,0:T(8,128)(2,1)S(1)}, bf16[16,512,512]{2,1,0:T(8,128)(2,1)}, u32[]{:S(2)}) copy-start(bf16[16,512,512]{2,1,0:T(8,128)(2,1)} %basis_high.1) | copy-start | bytes 25165828
  33.9 0.9 copy-start.2
  33.9 1.0 copy-start.3
  33.9 1.1 copy-start.5
  33.9 1.2 copy-start.7
  33.9 1.2 copy-start.9
  35.1 0.9 copy-start.11
  87.4 56.7 %copy-start.1 = (bf16[2,720,512]{2,1,0:T(8,128)(2,1)S(1)}, bf16[2,720,512]{2,1,0:T(8,128)(2,1)}, u32[]{:S(2)}) copy-start(bf16[2,720,512]{2,1,0:T(8,128)(2,1)} %constant.14.clone.table) | copy-start | bytes 4423684
